TPU v7x, 256 devices: a whole 4x4x8 slice. The times are simulated.
256 devices in a mesh: section: 64 (over z_hi, y, x, core), tensor: 4 (over z_lo).
Axes of the slice: x: 4, y: 4, z: 8 (z_hi: 2, z_lo: 4; z = z_hi * 4 + z_lo), core: 2. Of those that a mesh axis runs over, the one named last changes fastest.
Arguments:
- stash: bfloat16 [64, 8, 6144], P('section', None, 'tensor'), may hold values from -6 to 6
- out_grad: bfloat16 [64, 8, 6144], P('section', None, 'tensor'), may hold values from -6 to 6
- router_weight: bfloat16 [4, 6144], P(None, 'tensor'), may hold values from -0.078125 to 0.078125
- gate_weight: bfloat16 [32768, 6144], P('section', 'tensor'), may hold values from -0.078125 to 0.078125
- up_weight: bfloat16 [32768, 6144], P('section', 'tensor'), may hold values from -0.078125 to 0.078125
- down_weight: bfloat16 [32768, 6144], P('section', 'tensor'), may hold values from -0.0625 to 0.0625
- expert_ids: int32 [64, 8, 2], P('section'), may hold values from 0 to 3, all different within a row; in each aligned block of 8 rows (0 to 7, 8 to 15, ..., all dimensions but the last counted through in order) at most 5 rows name the same one
Outputs:
- in_grad: bfloat16 [64, 8, 6144], P('section', None, 'tensor')
- gate_grad: bfloat16 [32768, 6144], P('section', 'tensor')
- up_grad: bfloat16 [32768, 6144], P('section', 'tensor')
- down_grad: bfloat16 [32768, 6144], P('section', 'tensor')
- router_grad: float32 [4, 6144], P(None, 'tensor')
- aux_losses: float32 [64, 2], P('section')
Inputs may be any that keep to these rules, and one draw needn't show every extreme that they name: `expert_ids`: each token names two different experts; among the 8 tokens of one block no expert is named more than 5 times, a bound that some block reaches.
All inputs are finite; a program needn't handle non-finite values.
Results may differ from a plain program's by a relative error of at most 0.0049.
Values may be sent and summed in bfloat16 or wider, within the bound.
No kernel may reach another device: no remote copies, remote signals or barrier semaphores. Data moves between devices by JAX's collectives and lax.ppermute only.
A program may use at most 64 MiB of HBM per device.

v0:
```python
import jax
import jax.numpy as jnp
from jax import lax
from jax.sharding import PartitionSpec as P

CAP = 5


Z_WEIGHT = 0.25
BALANCE_WEIGHT = 1.0


def from_partner(value, axis, stride):
    mask = 2**stride
    pairs = [(source, source ^ mask) for source in range(lax.axis_size(axis))]
    return lax.ppermute(value, axis, pairs)


def block_routes(chosen_blocks, experts, capacity):
    blocks = chosen_blocks.shape[0]
    flat_ids = chosen_blocks.reshape(blocks, -1)
    labels = jnp.arange(experts, dtype=jnp.int32)
    onehot = (flat_ids[:, :, None] == labels[None, None, :]).astype(jnp.int32)
    before = jnp.cumsum(onehot, axis=1) - onehot
    position = jnp.sum(before * onehot, axis=2)
    block_number = jnp.arange(blocks, dtype=jnp.int32)[:, None]
    slot_of = flat_ids * (blocks * capacity) + block_number * capacity + position
    pair_count = flat_ids.shape[0] * flat_ids.shape[1]
    source = jnp.full((experts * blocks * capacity,), pair_count, dtype=jnp.int32)
    source = source.at[slot_of.reshape(-1)].set(jnp.arange(pair_count, dtype=jnp.int32))
    filled = source < pair_count
    clipped = jnp.minimum(source, pair_count - 1)
    counts = jnp.sum(onehot, axis=1)
    return (slot_of, clipped, filled, counts)


def pair_gates(logits, chosen):
    picked = jnp.take_along_axis(logits, chosen, axis=1)
    return jax.nn.sigmoid(picked[:, 0] - picked[:, 1])


def router_terms(logits, chosen, counts, lead_gate, dgate_pairs):
    tokens, experts = logits.shape
    exp_logits = jnp.exp(logits)
    exp_total = jnp.sum(exp_logits, axis=1, keepdims=True)
    log_total = jnp.log(exp_total)
    prob_rows = exp_logits / exp_total
    fraction = counts.astype(jnp.float32) / (2.0 * tokens)
    labels = jnp.arange(experts, dtype=jnp.int32)[None, :]
    toward = (chosen[:, 0:1] == labels).astype(jnp.float32) - (chosen[:, 1:2] == labels).astype(
        jnp.float32
    )
    spread = lead_gate * (1.0 - lead_gate) * (dgate_pairs[:, 0] - dgate_pairs[:, 1])
    balance_pull = BALANCE_WEIGHT * experts * fraction[None, :]
    local_part = 2.0 * Z_WEIGHT * log_total * prob_rows + prob_rows * (
        balance_pull - jnp.sum(prob_rows * balance_pull, axis=1, keepdims=True)
    )
    dlogits = spread[:, None] * toward + local_part
    losses = jnp.stack(
        [
            jnp.mean(log_total[:, 0] * log_total[:, 0]),
            experts * jnp.sum(fraction * jnp.mean(prob_rows, axis=0)),
        ]
    )
    return (dlogits, losses)


def bit_order(bit_count):
    return list(range(bit_count))


def shards(stash, out_grad, router_weight, gate_weight, up_weight, down_weight, expert_ids):
    sections = lax.axis_size("section")
    section_index = lax.axis_index("section")
    experts = router_weight.shape[0]
    token_count = stash.shape[1]
    group_size = sections // experts
    expert = section_index // group_size
    slot_span = sections * CAP
    x_own = stash[0]
    for bit_index in bit_order(sections.bit_length() - 1):
        x_own = from_partner(x_own, "section", bit_index)
    g_own = out_grad[0]
    x_rows, g_rows = (
        lax.all_gather(x_own, "section", axis=0, tiled=True),
        lax.all_gather(g_own, "section", axis=0, tiled=True),
    )
    chosen_all = lax.all_gather(expert_ids[0], "section", axis=0, tiled=True)
    total_tokens = x_rows.shape[0]
    logit_part = jnp.dot(x_rows, router_weight.T, preferred_element_type=jnp.float32)
    logits = lax.psum(logit_part, "tensor")
    lead_gate = pair_gates(logits, chosen_all)
    gate_pairs = jnp.stack([lead_gate, 1.0 - lead_gate], axis=1).reshape(-1)
    chosen_blocks = chosen_all.reshape(sections, token_count, 2)
    slot_of, clipped, filled, counts = block_routes(chosen_blocks, experts, CAP)
    start = expert * slot_span
    source = lax.dynamic_slice_in_dim(clipped, start, slot_span, 0)
    used = lax.dynamic_slice_in_dim(filled, start, slot_span, 0)
    row_index = source // 2
    keep = used[:, None]
    x_slot = jnp.where(keep, jnp.take(x_rows, row_index, axis=0), jnp.zeros((), x_rows.dtype))
    g_slot = jnp.where(keep, jnp.take(g_rows, row_index, axis=0), jnp.zeros((), g_rows.dtype))
    w_slot = jnp.where(used, jnp.take(gate_pairs, source), 0.0)[:, None]
    gate_part = jnp.dot(x_slot, gate_weight.T, preferred_element_type=jnp.float32)
    up_part = jnp.dot(x_slot, up_weight.T, preferred_element_type=jnp.float32)
    back_part = jnp.dot(g_slot, down_weight.T, preferred_element_type=jnp.float32)
    gate_proj, up_proj, back_proj = (
        lax.psum_scatter(gate_part, "tensor", scatter_dimension=1, tiled=True),
        lax.psum_scatter(up_part, "tensor", scatter_dimension=1, tiled=True),
        lax.psum_scatter(back_part, "tensor", scatter_dimension=1, tiled=True),
    )
    gate_sig = jax.nn.sigmoid(gate_proj)
    silu_gate = gate_proj * gate_sig
    dgate_local = jnp.sum(silu_gate * up_proj * back_proj, axis=1)
    scaled = w_slot * back_proj
    d_gate_share = (scaled * up_proj * gate_sig * (1.0 + gate_proj * (1.0 - gate_sig))).astype(
        jnp.bfloat16
    )
    d_up_share = (scaled * silu_gate).astype(jnp.bfloat16)
    weighted_share = (w_slot * silu_gate * up_proj).astype(jnp.bfloat16)
    d_gate_proj, d_up_proj, weighted_act = (
        lax.all_gather(d_gate_share, "tensor", axis=1, tiled=True),
        lax.all_gather(d_up_share, "tensor", axis=1, tiled=True),
        lax.all_gather(weighted_share, "tensor", axis=1, tiled=True),
    )
    dgate_holder = lax.dynamic_update_slice_in_dim(
        jnp.zeros((experts * slot_span,), jnp.float32), dgate_local, start, 0
    )
    dgate_all = lax.psum(dgate_holder, ("section", "tensor"))
    dx_slot = jnp.dot(d_gate_proj, gate_weight, preferred_element_type=jnp.float32) + jnp.dot(
        d_up_proj, up_weight, preferred_element_type=jnp.float32
    )
    dx_tokens = (
        jnp.zeros((total_tokens, dx_slot.shape[1]), jnp.float32)
        .at[row_index]
        .add(jnp.where(keep, dx_slot, 0.0))
    )
    expert_dx = lax.psum_scatter(dx_tokens, "section", scatter_dimension=0, tiled=True)
    grad_gate = jnp.dot(d_gate_proj.T, x_slot, preferred_element_type=jnp.float32).astype(
        jnp.bfloat16
    )
    grad_up = jnp.dot(d_up_proj.T, x_slot, preferred_element_type=jnp.float32).astype(jnp.bfloat16)
    grad_down = jnp.dot(weighted_act.T, g_slot, preferred_element_type=jnp.float32).astype(
        jnp.bfloat16
    )
    own_slots = lax.dynamic_index_in_dim(slot_of, section_index, 0, keepdims=False)
    own_counts = lax.dynamic_index_in_dim(counts, section_index, 0, keepdims=False)
    dgate_pairs = jnp.take(dgate_all, own_slots).reshape(token_count, 2)
    own_offset = section_index * token_count
    own_logits = lax.dynamic_slice_in_dim(logits, own_offset, token_count, 0)
    own_gate = lax.dynamic_slice_in_dim(lead_gate, own_offset, token_count, 0)
    dlogits, losses = router_terms(own_logits, expert_ids[0], own_counts, own_gate, dgate_pairs)
    router_dx = jnp.dot(dlogits, router_weight.astype(jnp.float32), precision=lax.Precision.HIGHEST)
    in_grad = (g_own.astype(jnp.float32) + expert_dx + router_dx).astype(jnp.bfloat16)
    router_part = jnp.dot(dlogits.T, x_own.astype(jnp.float32), precision=lax.Precision.HIGHEST)
    router_grad = lax.psum(router_part, "section")
    return (in_grad[None], grad_gate, grad_up, grad_down, router_grad, losses[None])


def solution(mesh):
    in_specs = (
        P("section", None, "tensor"),
        P("section", None, "tensor"),
        P(None, "tensor"),
        P("section", "tensor"),
        P("section", "tensor"),
        P("section", "tensor"),
        P("section", None, None),
    )
    out_specs = (
        P("section", None, "tensor"),
        P("section", "tensor"),
        P("section", "tensor"),
        P("section", "tensor"),
        P(None, "tensor"),
        P("section", None),
    )
    return jax.shard_map(shards, mesh=mesh, in_specs=in_specs, out_specs=out_specs, check_vma=False)
```

profile of v0, /device:TPU:1, one launch (start us, length us, event | category | flops | bytes accessed | tf_op | source)
XLA Modules:
  0.0 821.5 jit_solution(8031257327262884898)
XLA Ops:
  8.0 3.3 collective-permute-start
  12.4 2.7 collective-permute-done.1
  16.0 3.2 collective-permute-done.2
  19.2 2.7 collective-permute-done.3
  23.1 3.0 collective-permute-done.4
  26.1 5.2 collective-permute-start.5
  31.2 1.4 collective-permute-done.5
  34.1 124.4 %all-gather = s32[1,512,2]{2,0,1:T(1,128)S(1)} all-gather(s32[1,8,2]{2,0,1:T(1,128)S(1)} %copy.48), channel_id=2, replica_groups=mesh['section'=64,'tensor'=4] {'section'}, dimensions={1}, use_global_device_ids=true | all-gather | bytes 4160 | tf_op jit(solution)/shard_map/all_gather | solution.py:88
  162.5 4.3 scatter_custom_fusion
  167.0 5.9 gather_fusion.3
  174.3 1.9 fusion.30
  176.2 8.7 %psum.21 = f32[512,4]{0,1:T(4,128)S(1)} all-reduce(f32[512,4]{0,1:T(4,128)S(1)} %fusion.30), channel_id=1, replica_groups=mesh['section'=64,'tensor'=4] {'tensor'}, use_global_device_ids=true, to_apply=%region_3.4 | all-reduce | flops 2048 | bytes 16384 | tf_op jit(solution)/shard_map/psum | solution.py:91
  184.9 9.1 %gather_fusion.2 = f32[1024]{0:T(1024)S(1)} fusion(f32[512,4]{0,1:T(4,128)S(1)} %psum.21, s32[1024]{0:T(1024)S(1)} %reshape.181), kind=kCustom, calls=%fused_computation.4 | custom fusion | bytes 16384 | tf_op jit(solution)/shard_map/jit(take_along_axis)/gather | solution.py:38
  194.7 1.7 gather_fusion
  196.4 3.4 fusion.24
  200.1 2.7 gather_fusion.4
  202.8 3.3 fusion.26
  206.3 1.6 fusion.25
  207.9 13.1 %reduce-scatter.5.cloned.1.call-done = f32[320,128]{1,0:T(8,128)} async-done(((f32[320,512]{1,0:T(8,128)}), f32[320,128]{1,0:T(8,128)}) %reduce-scatter.5.cloned.1.call-update) | async-done | bytes 163856 | tf_op jit(solution)/shard_map/reduce_scatter | solution.py:110
  221.0 29.2 %reduce-scatter.7.cloned.1.call-done = f32[320,128]{1,0:T(8,128)} async-done(((f32[320,512]{1,0:T(8,128)}), f32[320,128]{1,0:T(8,128)}) %reduce-scatter.7.cloned.1.call-update) | async-done | bytes 163856 | tf_op jit(solution)/shard_map/reduce_scatter | solution.py:109
  250.1 29.7 %reduce-scatter.9.cloned.1.call-done = f32[320,128]{1,0:T(8,128)} async-done(((f32[320,512]{1,0:T(8,128)}), f32[320,128]{1,0:T(8,128)}) %reduce-scatter.9.cloned.1.call-update) | async-done | bytes 163856 | tf_op jit(solution)/shard_map/reduce_scatter | solution.py:108
  281.2 11.5 %all_gather.21 = bf16[320,512]{1,0:T(8,128)(2,1)S(1)} all-gather(bf16[320,128]{1,0:T(8,128)(2,1)S(1)} %get-tuple-element.17), channel_id=1, replica_groups=mesh['section'=64,'tensor'=4] {'tensor'}, dimensions={1}, use_global_device_ids=true | all-gather | bytes 409600 | tf_op jit(solution)/shard_map/all_gather | solution.py:122
  293.4 11.5 %all_gather.22 = bf16[320,512]{1,0:T(8,128)(2,1)S(1)} all-gather(bf16[320,128]{1,0:T(8,128)(2,1)S(1)} %get-tuple-element.19), channel_id=1, replica_groups=mesh['section'=64,'tensor'=4] {'tensor'}, dimensions={1}, use_global_device_ids=true | all-gather | bytes 409600 | tf_op jit(solution)/shard_map/all_gather | solution.py:123
  304.8 2.0 fusion
  306.8 6.5 scatter_custom_fusion.1
  318.7 80.0 %psum.22 = f32[1280]{0:T(1024)S(1)} all-reduce(f32[1280]{0:T(1024)S(1)} %dynamic_update_slice.3), channel_id=1, replica_groups=mesh['section'=64,'tensor'=4] {'section','tensor'}, use_global_device_ids=true, to_apply=%region_10.12 | all-reduce | flops 1280 | bytes 10240 | tf_op jit(solution)/shard_map/psum | solution.py:129
  400.0 395.5 %psum.23 = f32[4,1536]{1,0:T(4,128)} all-reduce(f32[4,1536]{1,0:T(4,128)S(1)} %fusion.23), channel_id=1, replica_groups=mesh['section'=64,'tensor'=4] {'section'}, use_global_device_ids=true, to_apply=%region_14.16 | all-reduce | flops 6144 | bytes 49152 | tf_op jit(solution)/shard_map/psum | solution.py:156
  795.5 10.7 %all_gather.23 = bf16[320,512]{1,0:T(8,128)(2,1)S(1)} all-gather(bf16[320,128]{1,0:T(8,128)(2,1)S(1)} %get-tuple-element.18), channel_id=1, replica_groups=mesh['section'=64,'tensor'=4] {'tensor'}, dimensions={1}, use_global_device_ids=true | all-gather | bytes 409600 | tf_op jit(solution)/shard_map/all_gather | solution.py:124
  806.2 2.2 convolution_convert_fusion.2
  808.4 2.2 convolution_convert_fusion.1
  810.7 2.2 convolution_convert_fusion
  812.9 1.7 fusion.2
  (95 shorter events, 19.3 us)
Async XLA Ops:
  7.2 199.1 %copy-start = (bf16[512,1536]{1,0:T(8,128)(2,1)S(1)}, bf16[512,1536]{1,0:T(8,128)(2,1)}, u32[]{:S(2)}) copy-start(bf16[512,1536]{1,0:T(8,128)(2,1)} %param.12) | copy-start | bytes 4718596
  7.2 159.8 %all-gather.7.cloned.1.call-start = ((), (), s32[]{:S(2)}) async-start(), calls=%async_computation.9 | async-start | bytes 1597440 | tf_op jit(solution)/shard_map/all_gather | solution.py:86
  7.9 166.4 %all-gather.5.cloned.1.call-start = ((), (), s32[]{:S(2)}) async-start(), calls=%async_computation.4 | async-start | bytes 1597440 | tf_op jit(solution)/shard_map/all_gather | solution.py:85
  8.0 4.4 collective-permute-start
  12.3 2.7 collective-permute-start.1
  15.0 4.2 collective-permute-start.2
  19.2 2.7 collective-permute-start.3
  21.9 4.2 collective-permute-start.4
  26.1 6.6 collective-permute-start.5
  32.7 0.6 copy-start.7
  33.3 187.7 %reduce-scatter.5.cloned.1.call-start = ((), (), s32[]{:S(2)}) async-start(), calls=%async_computation.5 | async-start | bytes 819200 | tf_op jit(solution)/shard_map/reduce_scatter | solution.py:110
  167.0 7.3 copy-start.6
  196.4 3.6 copy-start.1
  199.9 50.3 %reduce-scatter.7.cloned.1.call-start = ((), (), s32[]{:S(2)}) async-start(), calls=%async_computation.6 | async-start | bytes 819200 | tf_op jit(solution)/shard_map/reduce_scatter | solution.py:109
  202.8 3.4 copy-start.4
  206.2 73.7 %reduce-scatter.9.cloned.1.call-start = ((), (), s32[]{:S(2)}) async-start(), calls=%async_computation.7 | async-start | bytes 819200 | tf_op jit(solution)/shard_map/reduce_scatter | solution.py:108
  207.8 605.1 %reduce-scatter.11.cloned.1.call-start = ((), (), s32[]{:S(2)}) async-start(), calls=%async_computation.8 | async-start | bytes 3194880 | tf_op jit(solution)/shard_map/reduce_scatter | solution.py:138
  292.7 12.1 %copy-start.2 = (bf16[512,1536]{1,0:T(8,128)(2,1)S(1)}, bf16[512,1536]{1,0:T(8,128)(2,1)}, u32[]{:S(2)}) copy-start(bf16[512,1536]{1,0:T(8,128)(2,1)} %param.13) | copy-start | bytes 4718596
  313.3 1.8 copy-start.9
  313.3 86.5 %copy-start.8 = (bf16[8,1536]{1,0:T(8,128)(2,1)S(1)}, bf16[8,1536]{1,0:T(8,128)(2,1)}, u32[]{:S(2)}) copy-start(bf16[8,1536]{1,0:T(8,128)(2,1)} %copy-done.7) | copy-start | bytes 73732
  808.4 2.2 copy-start.3
  810.7 2.2 copy-start.5
Sparse Core Ops, SparseCore 0:
  11.7 84.2 all-gather.6
  100.4 73.8 all-gather.4
  200.0 20.9 reduce-scatter.4
  223.4 26.7 reduce-scatter.6
  253.1 26.7 reduce-scatter.8
  313.4 169.8 reduce-scatter.10
where the time goes:
time: 832 us; the launch traced here: 821 us
  blocking collectives  642 us (77%)
  waiting for transfers between devices  88.1 us (11%)
  local copies, waits for them, and re-layouts  29.1 us (3%)
  matrix products  21.5 us (3%)
  between operations  15.7 us (2%)
  other arithmetic  13.6 us (2%)
  starting transfers between devices  11.1 us (1%)
    psum x1, blocking collectives, shards(): router_grad = lax.psum(router_part, 'section')  395 us
    all_gather x1, blocking collectives, shards(): chosen_all = lax.all_gather(expert_ids[0], 'section', axis=0, tiled=True)  124 us
    psum x1, blocking collectives, shards(): dgate_all = lax.psum(dgate_holder, ('section', 'tensor'))  80 us
    reduce_scatter x1, waiting for transfers between devices, shards(): lax.psum_scatter(gate_part, 'tensor', scatter_dimension=1, tiled=True)  29.7 us
    reduce_scatter x1, waiting for transfers between devices, shards(): lax.psum_scatter(up_part, 'tensor', scatter_dimension=1, tiled=True)  29.2 us
  transfers between devices with their start and end apart: 12, of which 10 were waited for; matrix products, arithmetic and copies ran while one was open for 4% of the time, Pallas kernels for 0%

commit v1 on v0

v1 whole, which is shorter than its diff:
```python
import jax
import jax.numpy as jnp
from jax import lax
from jax.sharding import Mesh, PartitionSpec as P

CAP = 5
Z_WEIGHT = 0.25
BALANCE_WEIGHT = 1.0
BF = jnp.bfloat16
F32 = jnp.float32
HIGH = lax.Precision.HIGHEST


def split_pair(value):
    high = lax.reduce_precision(value, 8, 7)
    return high.astype(BF), (value - high).astype(BF)


def spread_out(value, axis):
    count = lax.axis_size(axis)
    return lax.all_to_all(jnp.broadcast_to(value[None], (count, *value.shape)), axis, 0, 0)


def core_swap(value):
    return lax.ppermute(value, "c", [(0, 1), (1, 0)])


def block_slots(ids, expert):
    match = (ids[..., 0] == expert) | (ids[..., 1] == expert)
    counted = match.astype(jnp.int32)
    position = jnp.cumsum(counted, axis=-1) - counted
    return match, position


def shards(stash, out_grad, router_weight, gate_weight, up_weight, down_weight, expert_ids):
    e, q, c = lax.axis_index("e"), lax.axis_index("q"), lax.axis_index("c")
    experts, groups, cores = lax.axis_size("e"), lax.axis_size("q"), lax.axis_size("c")
    ways = lax.axis_size("t")
    tokens, width = stash.shape[1], stash.shape[2]
    hidden = gate_weight.shape[0]
    share = hidden // ways
    blocks = cores * groups * experts
    slots = blocks * CAP
    ids = expert_ids[0]
    x_here, g_own = stash[0], out_grad[0]

    id_columns = jnp.pad(ids.astype(BF), ((tokens, 0), (0, 126)))
    own = jnp.concatenate([jnp.concatenate([x_here, g_own], 0), id_columns], 1)
    first = spread_out(own, "e")
    x_quad = first[:, :tokens, :width].reshape(experts * tokens, width)
    g_quad = first[:, tokens:].reshape(experts * tokens, width + 128)
    x_near = spread_out(x_quad, "q").reshape(-1, width)
    g_near = spread_out(g_quad, "q").reshape(-1, width + 128)
    x_far, g_far = core_swap(x_near), core_swap(g_near)

    all_ids = jnp.concatenate([g_near[:, width : width + 2], g_far[:, width : width + 2]], 0)
    all_ids = all_ids.astype(jnp.int32).reshape(blocks, tokens, 2)
    match, position = block_slots(all_ids, e)
    slot = jnp.arange(blocks, dtype=jnp.int32)[:, None] * CAP + position
    slot = jnp.where(match, slot, -1)
    labels = jnp.arange(slots, dtype=jnp.int32)[None, :]
    pick_g = (slot.reshape(-1, 1) == labels).astype(BF)
    pick_x = (slot[::-1].reshape(-1, 1) == labels).astype(BF)
    half = blocks * tokens // 2

    def choose(pick, near, far):
        dims = (((0,), (0,)), ((), ()))
        picked = lax.dot_general(pick[:half], near, dims, preferred_element_type=F32)
        picked += lax.dot_general(pick[half:], far, dims, preferred_element_type=F32)
        return picked.astype(BF)

    x_slot = choose(pick_x, x_near, x_far)
    g_slot = choose(pick_g, g_near[:, :width], g_far[:, :width])
    expert_labels = jnp.arange(experts, dtype=jnp.int32)
    other = all_ids[..., 0] + all_ids[..., 1] - e
    toward_token = (expert_labels == e).astype(BF) - (
        other.reshape(-1, 1) == expert_labels
    ).astype(BF)
    toward = lax.dot_general(pick_g, toward_token, (((0,), (0,)), ((), ())), preferred_element_type=F32)
    used = jnp.sum(jnp.abs(toward), axis=1) > 0.5

    dims = (((1,), (1,)), ((), ()))
    gate_part = lax.dot_general(x_slot, gate_weight, dims, preferred_element_type=F32).astype(BF)
    up_part = lax.dot_general(x_slot, up_weight, dims, preferred_element_type=F32).astype(BF)
    back_part = lax.dot_general(g_slot, down_weight, dims, preferred_element_type=F32).astype(BF)
    slot_logits = lax.dot_general(x_slot, router_weight, dims, preferred_element_type=F32)
    lead_part = jnp.sum(slot_logits * toward, axis=1)
    x_far_blocks = x_far.reshape(groups, experts, tokens, width)
    x_own = lax.dynamic_slice(
        x_far_blocks, (groups - 1 - q, experts - 1 - e, 0, 0), (1, 1, tokens, width)
    )[0, 0]
    own_part = lax.dot_general(router_weight, x_own, dims, preferred_element_type=F32)
    notes = jnp.concatenate([lead_part, own_part.reshape(-1)])
    note_high, note_low = split_pair(notes)
    note_rows = jnp.pad(
        jnp.stack([note_high, note_low]), ((0, 14), (0, 3 * share - notes.shape[0]))
    )
    pieces = [
        jnp.concatenate(
            [
                jnp.concatenate(
                    [part[:, k * share : (k + 1) * share] for part in (gate_part, up_part, back_part)], 1
                ),
                note_rows,
            ],
            0,
        )
        for k in range(ways)
    ]
    summed = lax.all_to_all(jnp.stack(pieces), "t", 0, 0).astype(F32).sum(0)
    gate_proj, up_proj, back_proj = (
        summed[:slots, k * share : (k + 1) * share] for k in range(3)
    )
    notes = summed[slots] + summed[slots + 1]
    lead = notes[:slots]
    own_logits = notes[slots : slots + experts * tokens].reshape(experts, tokens).T
    w_slot = jnp.where(used, jax.nn.sigmoid(lead), 0.0)
    w_column = w_slot[:, None]

    gate_sig = jax.nn.sigmoid(gate_proj)
    silu_gate = gate_proj * gate_sig
    dgate_part = jnp.sum(silu_gate * up_proj * back_proj, axis=1)
    scaled = w_column * back_proj
    d_gate = (scaled * up_proj * gate_sig * (1.0 + gate_proj * (1.0 - gate_sig))).astype(BF)
    d_up = (scaled * silu_gate).astype(BF)
    weighted = (w_column * silu_gate * up_proj).astype(BF)
    dgate_high, dgate_low = split_pair(dgate_part)
    dgate_rows = jnp.pad(jnp.stack([dgate_high, dgate_low]), ((0, 14), (0, 3 * share - slots)))
    packed = jnp.concatenate([jnp.concatenate([d_gate, d_up, weighted], 1), dgate_rows], 0)
    whole = lax.all_gather(packed, "t", axis=0)
    d_gate, d_up, weighted = (
        whole[:, :slots, k * share : (k + 1) * share].transpose(1, 0, 2).reshape(slots, hidden)
        for k in range(3)
    )
    dgate = whole[:, slots : slots + 2, :slots].astype(F32).sum((0, 1))

    exp_logits = jnp.exp(own_logits)
    exp_total = jnp.sum(exp_logits, axis=1, keepdims=True)
    log_total = jnp.log(exp_total)
    prob_rows = exp_logits / exp_total
    counts = jnp.sum((ids.reshape(-1, 1) == expert_labels).astype(F32), axis=0)
    fraction = counts / (2.0 * tokens)
    balance_pull = BALANCE_WEIGHT * experts * fraction[None, :]
    local_part = 2.0 * Z_WEIGHT * log_total * prob_rows + prob_rows * (
        balance_pull - jnp.sum(prob_rows * balance_pull, axis=1, keepdims=True)
    )
    losses = jnp.stack(
        [
            jnp.mean(log_total[:, 0] * log_total[:, 0]),
            experts * jnp.sum(fraction * jnp.mean(prob_rows, axis=0)),
        ]
    )
    coefficient = (w_slot * (1.0 - w_slot) * dgate)[:, None] * toward
    router_part = jnp.dot(coefficient.T, x_slot.astype(F32), precision=HIGH) + jnp.dot(
        local_part.T, x_own.astype(F32), precision=HIGH
    )

    rw = router_weight.astype(F32)
    dx = (
        jnp.dot(d_gate, gate_weight, preferred_element_type=F32)
        + jnp.dot(d_up, up_weight, preferred_element_type=F32)
        + jnp.dot(coefficient, rw, precision=HIGH)
    )
    router_rows = jnp.concatenate(split_pair(router_part), 0)
    sent = jnp.concatenate([dx[slots // 2 :].astype(BF), router_rows], 0)
    got = core_swap(sent).astype(F32)
    pair_rows = (dx[: slots // 2] + got[: slots // 2]).astype(BF)
    got_router = got[slots // 2 : slots // 2 + experts] + got[slots // 2 + experts :]
    router_rows = jnp.concatenate(split_pair(router_part + got_router), 0)
    pair_rows = pair_rows.reshape(groups, experts * CAP, width)
    router_all = jnp.broadcast_to(router_rows[None], (groups, *router_rows.shape))
    sent = jnp.concatenate([pair_rows, router_all], 1)
    got = lax.all_to_all(sent, "q", 0, 0).astype(F32).sum(0)
    quad_rows = got[: experts * CAP].astype(BF).reshape(experts, CAP, width)
    router_part = got[experts * CAP : experts * CAP + experts] + got[experts * CAP + experts :]
    router_rows = jnp.concatenate(split_pair(router_part), 0)
    router_all = jnp.broadcast_to(router_rows[None], (experts, *router_rows.shape))
    padded = jnp.pad(quad_rows, ((0, 0), (0, 8 - CAP), (0, 0)))
    got = lax.all_to_all(jnp.concatenate([padded, router_all], 1), "e", 0, 0).astype(F32)
    router_grad = got[:, 8:].sum(0)
    router_grad = router_grad[:experts] + router_grad[experts:]

    own_match, own_position = block_slots(ids[None], expert_labels[:, None])
    where = jnp.where(own_match, own_position, -1)
    combine = (where[:, :, None] == jnp.arange(8, dtype=jnp.int32)).astype(F32)
    expert_dx = jnp.einsum("etk,ekd->td", combine, got[:, :8], precision=HIGH)
    router_dx = jnp.dot(local_part, rw, precision=HIGH)
    in_grad = (g_own.astype(F32) + expert_dx + router_dx).astype(BF)

    dims = (((0,), (0,)), ((), ()))
    gate_grad = lax.dot_general(d_gate, x_slot, dims, preferred_element_type=F32).astype(BF)
    up_grad = lax.dot_general(d_up, x_slot, dims, preferred_element_type=F32).astype(BF)
    down_grad = lax.dot_general(weighted, g_slot, dims, preferred_element_type=F32).astype(BF)
    return in_grad[None], gate_grad, up_grad, down_grad, router_grad, losses[None]


def solution(mesh):
    sections, ways = mesh.devices.shape
    experts, cores = 4, 2
    groups = sections // (experts * cores)
    fine = Mesh(mesh.devices.reshape(experts, groups, cores, ways), ("e", "q", "c", "t"))
    section = ("e", "q", "c")
    in_specs = (
        P(section, None, "t"),
        P(section, None, "t"),
        P(None, "t"),
        P(section, "t"),
        P(section, "t"),
        P(section, "t"),
        P(section, None, None),
    )
    out_specs = (
        P(section, None, "t"),
        P(section, "t"),
        P(section, "t"),
        P(section, "t"),
        P(None, "t"),
        P(section, None),
    )
    return jax.shard_map(shards, mesh=fine, in_specs=in_specs, out_specs=out_specs, check_vma=False)
```

time: 832 us -> 180 us (0.22); the launches traced: 821 us -> 179 us
  blocking collectives: 642 us -> 40.4 us
  waiting for transfers between devices: 88.1 us -> 64.5 us
  local copies, waits for them, and re-layouts: 29.1 us -> 9.74 us
  starting transfers between devices: 11.1 us -> 25 us
  between operations: 15.7 us -> 2.43 us
    psum x3 -> x0, blocking collectives: 484 us -> none  [the longest x1 395 us: shards(): router_grad = lax.psum(router_part, 'section')]
    all_gather x4 -> x1, blocking collectives: 158 us -> 19 us  [shards(): whole = lax.all_gather(packed, 't', axis=0)]
    reduce_scatter x4 -> x0, waiting for transfers between devices: 72 us -> none  [the longest x1 29.7 us: shards(): lax.psum_scatter(gate_part, 'tensor', scatter_dimension=1, tiled=True)]
    all_to_all x0 -> x5, waiting for transfers between devices: none -> 63.4 us  [the longest x2 25.2 us: spread_out(): lax.all_to_all(jnp.broadcast_to(value[None], (count, *value.shape)), axis...]
    all_to_all x0 -> x1, blocking collectives: none -> 21.4 us  [spread_out(): lax.all_to_all(jnp.broadcast_to(value[None], (count, *value.shape)), axis...]
    gather x10 -> x0, local copies, waits for them, and re-layouts: 20.7 us -> none  [the longest x5 9.69 us: pair_gates(): picked = jnp.take_along_axis(logits, chosen, axis=1)]
    all_to_all x0 -> x5, starting transfers between devices: none -> 20.2 us  [the longest x2 7.68 us: spread_out(): lax.all_to_all(jnp.broadcast_to(value[None], (count, *value.shape)), axis...]
    ppermute x6 -> x3, waiting for transfers between devices: 14 us -> 1.11 us  [core_swap(): return lax.ppermute(value, 'c', [(0, 1), (1, 0)])]
  transfers between devices with their start and end apart: 12 -> 8, of which waited for: 10 -> 7; matrix products, arithmetic and copies ran while one was open for 4% -> 6% of each run, Pallas kernels for 0% -> 0%
where the time goes in v1:
time: 180 us; the launch traced here: 179 us
  waiting for transfers between devices  64.5 us (36%)
  blocking collectives  40.4 us (22%)
  starting transfers between devices  25 us (14%)
  matrix products  23.5 us (13%)
  other arithmetic  13 us (7%)
  local copies, waits for them, and re-layouts  9.74 us (5%)
  between operations  2.43 us (1%)
    all_to_all x2, waiting for transfers between devices, spread_out(): lax.all_to_all(jnp.broadcast_to(value[None], (count, *value.shape)), axis...  25.2 us
    all_to_all x1, waiting for transfers between devices, shards(): summed = lax.all_to_all(jnp.stack(pieces), 't', 0, 0).astype(F32).sum(0)  24.9 us
    all_to_all x1, blocking collectives, spread_out(): lax.all_to_all(jnp.broadcast_to(value[None], (count, *value.shape)), axis...  21.4 us
    all_gather x1, blocking collectives, shards(): whole = lax.all_gather(packed, 't', axis=0)  19 us
    all_to_all x2, starting transfers between devices, spread_out(): lax.all_to_all(jnp.broadcast_to(value[None], (count, *value.shape)), axis...  7.68 us
    all_to_all x1, waiting for transfers between devices, shards(): got = lax.all_to_all(sent, 'q', 0, 0).astype(F32).sum(0)  6.96 us
    all_to_all x1, waiting for transfers between devices, shards(): lax.all_to_all(jnp.concatenate([padded, router_all], 1), 'e', 0, 0)  6.37 us
    ppermute x3, starting transfers between devices, core_swap(): return lax.ppermute(value, 'c', [(0, 1), (1, 0)])  4.81 us
  transfers between devices with their start and end apart: 8, of which 7 were waited for; matrix products, arithmetic and copies ran while one was open for 6% of the time, Pallas kernels for 0%

profile of v1, /device:TPU:1, one launch (start us, length us, event | category | flops | bytes accessed | tf_op | source)
XLA Modules:
  0.0 178.6 jit_solution(17690811084052623374)
XLA Ops:
  2.3 21.4 %all_to_all.30 = bf16[4,16,1664]{2,1,0:T(8,128)(2,1)S(1)} all-to-all(bf16[4,16,1664]{2,1,0:T(8,128)(2,1)S(1)} %broadcast_in_dim.32), channel_id=1, replica_groups=mesh['e'=4,'q'=8,'c'=2,'t'=4] {'e'}, dimensions={0} | all-to-all | bytes 425984 | tf_op jit(solution)/shard_map/all_to_all | solution.py:21
  23.7 0.9 broadcast_in_dim.72
  24.7 4.1 %all-to-all-start.2 = ((bf16[8,32,1536]{2,1,0:T(8,128)(2,1)}), bf16[8,32,1536]{2,1,0:T(8,128)(2,1)S(1)}, u32[]{:S(2)}, u32[]{:S(2)}) async-start(bf16[8,32,1536]{2,1,0:T(8,128)(2,1)} %broadcast_in_dim.72), calls=%async_computation.2 | async-start | bytes 1572864 | tf_op jit(solution)/shard_map/all_to_all | solution.py:21
  28.8 12.7 %all-to-all-done.2 = bf16[8,32,1536]{2,1,0:T(8,128)(2,1)S(1)} async-done(((bf16[8,32,1536]{2,1,0:T(8,128)(2,1)}), bf16[8,32,1536]{2,1,0:T(8,128)(2,1)S(1)}, u32[]{:S(2)}, u32[]{:S(2)}) %all-to-all-start.2) | async-done | bytes 786464 | tf_op jit(solution)/shard_map/all_to_all | solution.py:21
  41.6 1.0 broadcast_in_dim.35
  42.5 3.6 %all-to-all-start.1 = ((bf16[8,32,1664]{2,1,0:T(8,128)(2,1)}), bf16[8,32,1664]{2,1,0:T(8,128)(2,1)S(1)}, u32[]{:S(2)}, u32[]{:S(2)}) async-start(bf16[8,32,1664]{2,1,0:T(8,128)(2,1)} %broadcast_in_dim.35), calls=%async_computation.1 | async-start | bytes 1703936 | tf_op jit(solution)/shard_map/all_to_all | solution.py:21
  46.1 1.2 collective-permute-start.1
  47.3 12.4 %all-to-all-done.1 = bf16[8,32,1664]{2,1,0:T(8,128)(2,1)S(1)} async-done(((bf16[8,32,1664]{2,1,0:T(8,128)(2,1)}), bf16[8,32,1664]{2,1,0:T(8,128)(2,1)S(1)}, u32[]{:S(2)}, u32[]{:S(2)}) %all-to-all-start.1) | async-done | bytes 852000 | tf_op jit(solution)/shard_map/all_to_all | solution.py:21
  64.5 1.8 fusion.14
  67.1 2.3 %fusion = bf16[320,1536]{1,0:T(8,128)(2,1)S(1)} fusion(f32[320,1536]{1,0:T(8,128)} %fusion.14, bf16[256,1536]{1,0:T(8,128)(2,1)} %collective-permute-done.1, pred[512,320]{1,0:T(32,128)(4,1)} %copy-done.9), kind=kOutput, calls=%fused_computation.7 | convolution fusion | flops 252641280 | bytes 3833856 | tf_op jit(solution)/shard_map/dot_general | solution.py:69
  70.3 1.7 fusion.1
  75.6 1.1 pad_maximum_fusion
  76.8 4.2 %all-to-all-start.3 = ((bf16[4,336,384]{2,1,0:T(8,128)(2,1)}), bf16[4,336,384]{2,1,0:T(8,128)(2,1)}, u32[]{:S(2)}, u32[]{:S(2)}) async-start(bf16[4,336,384]{2,1,0:T(8,128)(2,1)} %pad_maximum_fusion), calls=%async_computation.3 | async-start | bytes 2064384 | tf_op jit(solution)/shard_map/all_to_all | solution.py:110
  81.3 24.9 %all-to-all-done.3 = bf16[4,336,384]{2,1,0:T(8,128)(2,1)} async-done(((bf16[4,336,384]{2,1,0:T(8,128)(2,1)}), bf16[4,336,384]{2,1,0:T(8,128)(2,1)}, u32[]{:S(2)}, u32[]{:S(2)}) %all-to-all-start.3) | async-done | bytes 1032224 | tf_op jit(solution)/shard_map/all_to_all | solution.py:110
  106.2 1.4 convert_reduce_fusion
  108.9 19.0 %all-gather = bf16[1344,384]{1,0:T(8,128)(2,1)S(1)} all-gather(bf16[336,384]{1,0:T(8,128)(2,1)S(1)} %pad_maximum_fusion.7), channel_id=2, replica_groups=mesh['e'=4,'q'=8,'c'=2,'t'=4] {'t'}, dimensions={0}, use_global_device_ids=true | all-gather | bytes 1290240 | tf_op jit(solution)/shard_map/all_gather | solution.py:130
  127.9 0.9 slice_bitcast_fusion
  131.4 1.0 convolution_add_fusion.1
  132.5 1.3 copy-done.1
  134.5 1.0 reduce-precision_convert_fusion.2
  136.3 2.8 %collective-permute-start.2 = (bf16[168,1536]{1,0:T(8,128)(2,1)}, bf16[168,1536]{1,0:T(8,128)(2,1)S(1)}, u32[]{:S(2)}, u32[]{:S(2)}) collective-permute-start(bf16[168,1536]{1,0:T(8,128)(2,1)} %pad_maximum_fusion.6), channel_id=1, source_target_pairs={{0,4},{4,0},{1,5},{5,1},{2,6},{6,2},{3,7},{7,3},{8,12},{12,8},{9,1... | collective-permute-start | bytes 1548296 | tf_op jit(solution)/shard_map/ppermute | solution.py:25
  140.9 2.1 %fusion.6 = bf16[160,1536]{1,0:T(8,128)(2,1)} fusion(f32[168,1536]{1,0:T(8,128)S(1)} %convert_element_type.202, f32[320,1536]{1,0:T(8,128)} %copy-done.1), kind=kLoop, calls=%fused_computation.25 | loop fusion | flops 491520 | bytes 2457600 | tf_op jit(solution)/shard_map/convert_element_type | solution.py:167
  143.0 1.1 reshape.323
  144.2 1.0 pad_maximum_fusion.1
  145.2 3.7 %all-to-all-start.4 = ((bf16[8,28,1536]{2,1,0:T(8,128)(2,1)}), bf16[8,28,1536]{2,1,0:T(8,128)(2,1)S(1)}, u32[]{:S(2)}, u32[]{:S(2)}) async-start(bf16[8,28,1536]{2,1,0:T(8,128)(2,1)} %pad_maximum_fusion.1), calls=%async_computation.4 | async-start | bytes 1572864 | tf_op jit(solution)/shard_map/all_to_all | solution.py:173
  149.5 3.1 %convolution_convert_fusion.2 = bf16[512,1536]{1,0:T(8,128)(2,1)} fusion(bf16[320,1536]{1,0:T(8,128)(2,1)S(1)} %fusion, bf16[4,40,8,128]{3,2,1,0:T(8,128)(2,1)} %copy-done.2), kind=kOutput, calls=%fused_computation.2 | convolution fusion | flops 504102912 | bytes 2883584 | tf_op jit(solution)/shard_map/dot_general | solution.py:191
  152.6 2.2 %convolution_convert_fusion.1 = bf16[512,1536]{1,0:T(8,128)(2,1)} fusion(bf16[320,1536]{1,0:T(8,128)(2,1)S(1)} %fusion, bf16[4,40,8,128]{3,2,1,0:T(8,128)(2,1)S(1)} %copy-done.6), kind=kOutput, calls=%fused_computation.1 | convolution fusion | flops 504102912 | bytes 2883584 | tf_op jit(solution)/shard_map/dot_general | solution.py:192
  154.8 7.0 %all-to-all-done.4 = bf16[8,28,1536]{2,1,0:T(8,128)(2,1)S(1)} async-done(((bf16[8,28,1536]{2,1,0:T(8,128)(2,1)}), bf16[8,28,1536]{2,1,0:T(8,128)(2,1)S(1)}, u32[]{:S(2)}, u32[]{:S(2)}) %all-to-all-start.4) | async-done | bytes 688160 | tf_op jit(solution)/shard_map/all_to_all | solution.py:173
  162.7 4.6 %all-to-all-start.5 = ((bf16[4,16,1536]{2,1,0:T(8,128)(2,1)}), bf16[4,16,1536]{2,1,0:T(8,128)(2,1)S(1)}, u32[]{:S(2)}, u32[]{:S(2)}) async-start(bf16[4,16,1536]{2,1,0:T(8,128)(2,1)} %fusion.32), calls=%async_computation.5 | async-start | bytes 393216 | tf_op jit(solution)/shard_map/all_to_all | solution.py:179
  167.3 3.1 %convolution_convert_fusion = bf16[512,1536]{1,0:T(8,128)(2,1)} fusion(bf16[320,1536]{1,0:T(8,128)(2,1)S(1)} %copy-done.8, bf16[4,40,8,128]{3,2,1,0:T(8,128)(2,1)} %get-tuple-element.10), kind=kOutput, calls=%fused_computation | convolution fusion | flops 504102912 | bytes 2883584 | tf_op jit(solution)/shard_map/dot_general | solution.py:193
  170.4 6.4 %all-to-all-done.5 = bf16[4,16,1536]{2,1,0:T(8,128)(2,1)S(1)} async-done(((bf16[4,16,1536]{2,1,0:T(8,128)(2,1)}), bf16[4,16,1536]{2,1,0:T(8,128)(2,1)S(1)}, u32[]{:S(2)}, u32[]{:S(2)}) %all-to-all-start.5) | async-done | bytes 196640 | tf_op jit(solution)/shard_map/all_to_all | solution.py:179
  177.1 0.9 fusion.4
  (120 shorter events, 20.3 us)
Async XLA Ops:
  0.6 72.5 %copy-start = (bf16[512,1536]{1,0:T(8,128)(2,1)S(1)}, bf16[512,1536]{1,0:T(8,128)(2,1)}, u32[]{:S(2)}) copy-start(bf16[512,1536]{1,0:T(8,128)(2,1)} %param.10) | copy-start | bytes 4718596
  24.7 16.9 %all-to-all-start.2 = ((bf16[8,32,1536]{2,1,0:T(8,128)(2,1)}), bf16[8,32,1536]{2,1,0:T(8,128)(2,1)S(1)}, u32[]{:S(2)}, u32[]{:S(2)}) async-start(bf16[8,32,1536]{2,1,0:T(8,128)(2,1)} %broadcast_in_dim.72), calls=%async_computation.2 | async-start | bytes 1572864 | tf_op jit(solution)/shard_map/all_to_all | solution.py:21
  28.8 32.1 %copy-start.10 = (bf16[4,1536]{1,0:T(4,128)(2,1)S(1)}, bf16[4,1536]{1,0:T(4,128)(2,1)}, u32[]{:S(2)}) copy-start(bf16[4,1536]{1,0:T(4,128)(2,1)} %param.9) | copy-start | bytes 36868
  42.5 17.2 %all-to-all-start.1 = ((bf16[8,32,1664]{2,1,0:T(8,128)(2,1)}), bf16[8,32,1664]{2,1,0:T(8,128)(2,1)S(1)}, u32[]{:S(2)}, u32[]{:S(2)}) async-start(bf16[8,32,1664]{2,1,0:T(8,128)(2,1)} %broadcast_in_dim.35), calls=%async_computation.1 | async-start | bytes 1703936 | tf_op jit(solution)/shard_map/all_to_all | solution.py:21
  46.1 14.8 %collective-permute-start.1 = (bf16[256,1536]{1,0:T(8,128)(2,1)S(1)}, bf16[256,1536]{1,0:T(8,128)(2,1)}, u32[]{:S(2)}, u32[]{:S(2)}) collective-permute-start(bf16[256,1536]{1,0:T(8,128)(2,1)S(1)} %bitcast.110), channel_id=1, source_target_pairs={{0,4},{4,0},{1,5},{5,1},{2,6},{6,2},{3,7},{7,3},{8,12},{12,8},{9,1... | collective-permute-start | bytes 2359304 | tf_op jit(solution)/shard_map/ppermute | solution.py:25
  59.7 3.0 %collective-permute-start = (bf16[256,1664]{1,0:T(8,128)(2,1)S(1)}, bf16[256,1664]{1,0:T(8,128)(2,1)}, u32[]{:S(2)}, u32[]{:S(2)}) collective-permute-start(bf16[256,1664]{1,0:T(8,128)(2,1)S(1)} %bitcast.107), channel_id=1, source_target_pairs={{0,4},{4,0},{1,5},{5,1},{2,6},{6,2},{3,7},{7,3},{8,12},{12,8},{9,1... | collective-permute-start | bytes 2555912 | tf_op jit(solution)/shard_map/ppermute | solution.py:25
  64.5 2.1 %copy-start.9 = (pred[512,320]{1,0:T(32,128)(4,1)}, pred[512,320]{1,0:T(32,128)(4,1)S(1)}, u32[]{:S(2)}) copy-start(pred[512,320]{1,0:T(32,128)(4,1)S(1)} %iota_compare_fusion) | copy-start | bytes 491524
  70.3 1.8 copy-start.13
  72.1 1.0 copy-start.7
  73.1 1.4 copy-start.3
  75.6 5.4 %copy-start.12 = (s32[1,8,2]{1,2,0:T(2,128)S(1)}, s32[1,8,2]{1,2,0:T(2,128)}, u32[]{:S(2)}) copy-start(s32[1,8,2]{1,2,0:T(2,128)} %param.13) | copy-start | bytes 196
  76.8 29.4 %all-to-all-start.3 = ((bf16[4,336,384]{2,1,0:T(8,128)(2,1)}), bf16[4,336,384]{2,1,0:T(8,128)(2,1)}, u32[]{:S(2)}, u32[]{:S(2)}) async-start(bf16[4,336,384]{2,1,0:T(8,128)(2,1)} %pad_maximum_fusion), calls=%async_computation.3 | async-start | bytes 2064384 | tf_op jit(solution)/shard_map/all_to_all | solution.py:110
  128.8 1.2 copy-start.2
  128.8 1.2 copy-start.5
  129.3 1.4 copy-start.4
  132.5 1.3 copy-start.1
  136.3 4.5 %collective-permute-start.2 = (bf16[168,1536]{1,0:T(8,128)(2,1)}, bf16[168,1536]{1,0:T(8,128)(2,1)S(1)}, u32[]{:S(2)}, u32[]{:S(2)}) collective-permute-start(bf16[168,1536]{1,0:T(8,128)(2,1)} %pad_maximum_fusion.6), channel_id=1, source_target_pairs={{0,4},{4,0},{1,5},{5,1},{2,6},{6,2},{3,7},{7,3},{8,12},{12,8},{9,1... | collective-permute-start | bytes 1548296 | tf_op jit(solution)/shard_map/ppermute | solution.py:25
  145.2 16.6 %all-to-all-start.4 = ((bf16[8,28,1536]{2,1,0:T(8,128)(2,1)}), bf16[8,28,1536]{2,1,0:T(8,128)(2,1)S(1)}, u32[]{:S(2)}, u32[]{:S(2)}) async-start(bf16[8,28,1536]{2,1,0:T(8,128)(2,1)} %pad_maximum_fusion.1), calls=%async_computation.4 | async-start | bytes 1572864 | tf_op jit(solution)/shard_map/all_to_all | solution.py:173
  148.9 3.7 %copy-start.6 = (bf16[4,40,8,128]{3,2,1,0:T(8,128)(2,1)S(1)}, bf16[4,40,8,128]{3,2,1,0:T(8,128)(2,1)}, u32[]{:S(2)}) copy-start(bf16[4,40,8,128]{3,2,1,0:T(8,128)(2,1)} %copy-done.5) | copy-start | bytes 983044
  154.8 12.5 %copy-start.8 = (bf16[320,1536]{1,0:T(8,128)(2,1)S(1)}, bf16[320,1536]{1,0:T(8,128)(2,1)}, u32[]{:S(2)}) copy-start(bf16[320,1536]{1,0:T(8,128)(2,1)} %copy-done.7) | copy-start | bytes 2949124
  162.7 14.1 %all-to-all-start.5 = ((bf16[4,16,1536]{2,1,0:T(8,128)(2,1)}), bf16[4,16,1536]{2,1,0:T(8,128)(2,1)S(1)}, u32[]{:S(2)}, u32[]{:S(2)}) async-start(bf16[4,16,1536]{2,1,0:T(8,128)(2,1)} %fusion.32), calls=%async_computation.5 | async-start | bytes 393216 | tf_op jit(solution)/shard_map/all_to_all | solution.py:179
  167.3 9.5 %copy-start.11 = (bf16[1,8,1536]{2,1,0:T(8,128)(2,1)S(1)}, bf16[1,8,1536]{2,1,0:T(8,128)(2,1)}, u32[]{:S(2)}) copy-start(bf16[1,8,1536]{2,1,0:T(8,128)(2,1)} %param.8) | copy-start | bytes 73732

commit v2 on v1

v2 whole, which is shorter than its diff:
```python
import functools

import jax
import jax.numpy as jnp
from jax import lax
from jax.experimental import pallas as pl
from jax.experimental.pallas import tpu as pltpu
from jax.sharding import Mesh, PartitionSpec as P

CAP = 5
Z_WEIGHT = 0.25
BALANCE_WEIGHT = 1.0
BF = jnp.bfloat16
F32 = jnp.float32
HIGH = lax.Precision.HIGHEST
PARTS = ((0, 3), (1, 2))
VMEM = pl.BlockSpec(memory_space=pltpu.VMEM)
SMEM = pl.BlockSpec(memory_space=pltpu.SMEM)
NT = (((1,), (1,)), ((), ()))
TN = (((0,), (0,)), ((), ()))


def matmul(a, b, dims=(((1,), (0,)), ((), ()))):
    return lax.dot_general(a, b, dims, preferred_element_type=F32)


def split_pair(value):
    high = value.astype(BF)
    return high, (value - high.astype(F32)).astype(BF)


def up_to(count, step):
    return -(-count // step) * step


def to_row(value):
    count = value.shape[0]
    padded = up_to(count, 128)
    if padded > count:
        value = jnp.concatenate([value, jnp.zeros((padded - count, 128), F32)], 0)
    return jnp.sum(value.T, axis=0, keepdims=True)


def to_column(row, count):
    padded = up_to(count, 128)
    return jnp.broadcast_to(row[:, :padded], (128, padded)).T[:count]


def project_kernel(
    chunks, width, share, has_own,
    place, near, far, gate_w, up_w, down_w, router_w,
    own, send1, send2, send3, x_slot, g_slot, toward, scatter, x_own, notes,
):
    e, q, t = place[0], place[1], place[2]
    e_value = e.astype(F32)
    rows = chunks * 16
    half = chunks * CAP
    row = lax.broadcasted_iota(jnp.int32, (rows, rows), 0)
    col = lax.broadcasted_iota(jnp.int32, (rows, rows), 1)
    earlier = ((row >> 4 == col >> 4) & (col < row)).astype(F32).astype(BF)
    mirror = (
        ((row >> 4) + (col >> 4) == chunks - 1) & ((row & 15) + 8 == (col & 15))
    ).astype(F32).astype(BF)
    compact = (
        (lax.broadcasted_iota(jnp.int32, (chunks * 8, rows), 0) >> 3
         == lax.broadcasted_iota(jnp.int32, (chunks * 8, rows), 1) >> 4)
        & ((lax.broadcasted_iota(jnp.int32, (chunks * 8, rows), 0) & 7) + 8
           == (lax.broadcasted_iota(jnp.int32, (chunks * 8, rows), 1) & 15))
    ).astype(F32).astype(BF)
    tall = lax.broadcasted_iota(jnp.int32, (rows, 128), 0)
    lane = lax.broadcasted_iota(jnp.int32, (rows, 128), 1).astype(F32)
    is_grad = (tall & 15) >= 8
    labels = lax.broadcasted_iota(jnp.int32, (rows, half), 1).astype(F32)

    def routes(block):
        ids = block[:, width:].astype(F32)
        first = jnp.broadcast_to(ids[:, 0:1], (rows, 128))
        second = jnp.broadcast_to(ids[:, 1:2], (rows, 128))
        match = is_grad & ((first == e_value) | (second == e_value))
        matched = match.astype(F32)
        position = matmul(earlier, matched.astype(BF))
        slot = jnp.where(match, (tall >> 4).astype(F32) * CAP + position, -1.0)
        pick = (jnp.broadcast_to(slot[:, 0:1], (rows, half)) == labels).astype(F32).astype(BF)
        other = first + second - e_value
        sign = matched * ((lane == e_value).astype(F32) - (lane == other).astype(F32))
        return pick, sign.astype(BF)

    pick_near, sign_near = routes(near)
    pick_far, sign_far = routes(far)
    mirror_near = matmul(mirror, pick_far).astype(BF)
    mirror_far = matmul(mirror, pick_near).astype(BF)
    x_slot[:half] = matmul(mirror_far, far[:, :width], TN).astype(BF)
    x_slot[half:] = matmul(mirror_near, near[:, :width], TN).astype(BF)
    g_slot[:half] = matmul(pick_near, near[:, :width], TN).astype(BF)
    g_slot[half:] = matmul(pick_far, far[:, :width], TN).astype(BF)
    toward[:half] = matmul(pick_near, sign_near, TN)
    toward[half:] = matmul(pick_far, sign_far, TN)
    scatter[: chunks * 8] = matmul(compact, pick_near).astype(BF)
    scatter[chunks * 8 :] = matmul(compact, pick_far).astype(BF)

    slots = 2 * half
    lead = to_row(matmul(x_slot[...], router_w[...], NT) * toward[...])
    notes[...] = jnp.zeros_like(notes)
    lead_high, lead_low = split_pair(lead)
    notes[0:1, : lead.shape[1]] = lead_high.astype(F32)
    notes[1:2, : lead.shape[1]] = lead_low.astype(F32)
    if has_own:
        groups = chunks // len(PARTS[0])
        per = chunks // groups
        start = pl.multiple_of(((groups - 1 - q) * per + per - 1) * 16, 16)
        block = far[pl.ds(start, 16), :width]
        x_own[...] = block
        own_high, own_low = split_pair(matmul(router_w[:16], block, NT))
        notes[8:16, 0:16] = own_high[:8].astype(F32)
        notes[8:16, 128:144] = own_low[:8].astype(F32)
    for step, out in enumerate((own, send1, send2, send3)):
        rows_of = pl.ds(pl.multiple_of((t ^ step) * share, share), share)
        both = jnp.concatenate([gate_w[rows_of, :], up_w[rows_of, :]], 0)
        out[:slots, : 2 * share] = matmul(x_slot[...], both, NT).astype(out.dtype)
        out[:slots, 2 * share :] = matmul(g_slot[...], down_w[rows_of, :], NT).astype(out.dtype)
        out[slots:] = notes[...].astype(out.dtype)


def act_kernel(slots, share, own, got1, got2, got3, toward, packed, weight, own_logits):
    total = own[...] + got1[...].astype(F32) + got2[...].astype(F32) + got3[...].astype(F32)
    notes = total[slots:]
    own_logits[...] = notes[8:16, :128] + notes[8:16, 128:256]
    used = jnp.sum(jnp.abs(toward[...]), axis=1, keepdims=True) > 0.5
    lead = to_column(notes[0:1] + notes[1:2], slots)
    w = jnp.where(used, jax.nn.sigmoid(lead), 0.0)
    weight[...] = w
    gate_proj, up_proj, back_proj = (
        total[:slots, k * share : (k + 1) * share] for k in range(3)
    )
    gate_sig = jax.nn.sigmoid(gate_proj)
    silu_gate = gate_proj * gate_sig
    scaled = w * back_proj
    packed[:slots, :share] = (
        scaled * up_proj * gate_sig * (1.0 + gate_proj * (1.0 - gate_sig))
    ).astype(BF)
    packed[:slots, share : 2 * share] = (scaled * silu_gate).astype(BF)
    packed[:slots, 2 * share :] = (w * silu_gate * up_proj).astype(BF)
    dgate_high, dgate_low = split_pair(to_row(silu_gate * up_proj * back_proj))
    lanes = dgate_high.shape[1]
    zero = jnp.zeros((14, lanes), F32)
    rows = jnp.concatenate([dgate_high.astype(F32), dgate_low.astype(F32), zero], 0)
    if lanes < 3 * share:
        rows = jnp.concatenate([rows, jnp.zeros((16, 3 * share - lanes), F32)], 1)
    packed[slots:] = rows.astype(BF)


def back_kernel(
    slots, share, has_own, place, p0, p1, p2, p3, gate_w, up_w, router_w, toward, weight, scatter,
    x_slot, extra, x_own, kept, sent, router_part,
):
    t = place[2]
    half = slots // 2
    tokens = scatter.shape[0] // 2
    pieces = (p0, p1, p2, p3)
    notes = sum(p[slots : slots + 16, :].astype(F32) for p in pieces)
    dgate = to_column(notes[0:1] + notes[1:2], slots)
    w = weight[...]
    coefficient = w * (1.0 - w) * dgate * toward[...]
    high, low = split_pair(coefficient)

    def gradient(part):
        pick = scatter[part * tokens : (part + 1) * tokens, :]
        rows = slice(part * half, (part + 1) * half)
        total = matmul(matmul(pick, high[rows]).astype(BF), router_w[...])
        total += matmul(matmul(pick, low[rows]).astype(BF), router_w[...])
        for step, piece in enumerate(pieces):
            rows_of = pl.ds(pl.multiple_of((t ^ step) * share, share), share)
            both = jnp.concatenate([gate_w[rows_of, :], up_w[rows_of, :]], 0)
            spread = matmul(pick, piece[rows, : 2 * share]).astype(BF)
            total += matmul(spread, both)
        return total

    sent[:tokens] = gradient(1).astype(BF)
    kept[...] = gradient(0)
    router = matmul(high, x_slot[...], TN)[:8] + matmul(low, x_slot[...], TN)[:8]
    if has_own:
        local_high, local_low = split_pair(extra[...])
        router += matmul(local_high, x_own[...], TN)[:8] + matmul(local_low, x_own[...], TN)[:8]
        router_part[...] = router
    else:
        router += extra[...]
        router_part[...] = router
        router_high, router_low = split_pair(router)
        sent[tokens : tokens + 8] = router_high
        sent[tokens + 8 :] = router_low


def pair_kernel(groups, has_router, kept, got, router_part, out):
    tokens = kept.shape[0]
    per = tokens // groups
    pair = (kept[...] + got[:tokens].astype(F32)).astype(BF)
    for j in range(groups):
        out[j, :per] = pair[j * per : (j + 1) * per]
    if has_router:
        router = router_part[...] + got[tokens : tokens + 8].astype(F32)
        router += got[tokens + 8 :].astype(F32)
        high, low = split_pair(router)
        both = jnp.concatenate([high, low], 0)
        for j in range(groups):
            out[j, per:] = both


def weight_kernel(parts, slots, share, place, *refs):
    t = place[2]
    inputs, (gate_grad, up_grad, down_grad) = refs[:-3], refs[-3:]
    for step in range(4):
        rows_of = pl.ds(pl.multiple_of((t ^ step) * share, share), share)
        both = down = 0.0
        for part in range(parts):
            block = inputs[part * 6 : part * 6 + 6]
            piece, x_slot, g_slot = block[step], block[4], block[5]
            both += matmul(piece[:slots, : 2 * share], x_slot[...], TN)
            down += matmul(piece[:slots, 2 * share :], g_slot[...], TN)
        gate_grad[rows_of, :] = both[:share].astype(BF)
        up_grad[rows_of, :] = both[share:].astype(BF)
        down_grad[rows_of, :] = down.astype(BF)


def call(body, ins, outs, flops, scratch=()):
    bytes_moved = sum(v.size * v.dtype.itemsize for v in ins)
    return pl.pallas_call(
        body,
        in_specs=[SMEM if v.ndim == 1 else VMEM for v in ins],
        out_specs=[VMEM] * len(outs),
        out_shape=[jax.ShapeDtypeStruct(shape, dtype) for shape, dtype in outs],
        scratch_shapes=list(scratch),
        cost_estimate=pl.CostEstimate(
            flops=flops, bytes_accessed=bytes_moved, transcendentals=0
        ),
        compiler_params=pltpu.CompilerParams(vmem_limit_bytes=40 * 2**20),
    )(*ins)


def exchange(value, axis, step):
    count = lax.axis_size(axis)
    return lax.ppermute(value, axis, [(k, k ^ step) for k in range(count)])


def spread_out(value, axis):
    count = lax.axis_size(axis)
    return lax.all_to_all(jnp.broadcast_to(value[None], (count, *value.shape)), axis, 0, 0)


def shards(stash, out_grad, router_weight, gate_weight, up_weight, down_weight, expert_ids):
    e, q = lax.axis_index("e"), lax.axis_index("q")
    experts, groups, ways = lax.axis_size("e"), lax.axis_size("q"), lax.axis_size("t")
    tokens, width = stash.shape[1], stash.shape[2]
    hidden = gate_weight.shape[0]
    share = hidden // ways
    ids = expert_ids[0]
    x_here, g_own = stash[0], out_grad[0]
    place = jnp.stack([e, q, lax.axis_index("t")]).astype(jnp.int32)
    router_tall = jnp.pad(router_weight, ((0, 128 - experts), (0, 0)))
    per = len(PARTS[0])
    chunks = groups * per
    slots = 2 * chunks * CAP

    id_columns = jnp.pad(ids.astype(BF), ((tokens, 0), (0, 126)))
    own = jnp.concatenate([jnp.concatenate([x_here, g_own], 0), id_columns], 1)
    quad = [own] + [exchange(own, "e", step) for step in range(1, experts)]
    work = []
    for index, part in enumerate(PARTS):
        near = spread_out(jnp.concatenate([quad[k] for k in part], 0), "q")
        near = near.reshape(chunks * 16, width + 128)
        work.append((near, exchange(near, "c", 1)))

    sums = []
    for index, (near, far) in enumerate(work):
        height = slots + 16
        outs = (
            [((height, 3 * share), F32)]
            + [((height, 3 * share), BF)] * 3
            + [((slots, width), BF)] * 2
            + [((slots, 128), F32), ((chunks * 16, slots // 2), BF), ((16, width), BF)]
        )
        mine, *sends, x_slot, g_slot, toward, scatter, x_own = call(
            functools.partial(project_kernel, chunks, width, share, index == 0),
            [place, near, far, gate_weight, up_weight, down_weight, router_tall],
            outs,
            2 * slots * width * (3 * hidden + 4 * chunks * 16),
            [pltpu.VMEM((16, 3 * share), F32)],
        )
        got = [exchange(value, "t", step + 1) for step, value in enumerate(sends)]
        sums.append((mine, got, x_slot, g_slot, toward, scatter, x_own))

    packs = []
    for index, (mine, got, x_slot, g_slot, toward, scatter, x_own) in enumerate(sums):
        packed, weight, own_logits = call(
            functools.partial(act_kernel, slots, share),
            [mine, *got, toward],
            [((slots + 16, 3 * share), BF), ((slots, 128), F32), ((8, 128), F32)],
            slots * share * 40,
        )
        pieces = [packed] + [exchange(packed, "t", step) for step in range(1, ways)]
        packs.append((pieces, weight, own_logits))

    own_logits = packs[0][2][:experts, :tokens].T
    expert_labels = jnp.arange(experts, dtype=jnp.int32)
    exp_logits = jnp.exp(own_logits)
    exp_total = jnp.sum(exp_logits, axis=1, keepdims=True)
    log_total = jnp.log(exp_total)
    prob_rows = exp_logits / exp_total
    counts = jnp.sum((ids.reshape(-1, 1) == expert_labels).astype(F32), axis=0)
    fraction = counts / (2.0 * tokens)
    balance_pull = BALANCE_WEIGHT * experts * fraction[None, :]
    local_part = 2.0 * Z_WEIGHT * log_total * prob_rows + prob_rows * (
        balance_pull - jnp.sum(prob_rows * balance_pull, axis=1, keepdims=True)
    )
    losses = jnp.stack(
        [
            jnp.mean(log_total[:, 0] * log_total[:, 0]),
            experts * jnp.sum(fraction * jnp.mean(prob_rows, axis=0)),
        ]
    )
    extra = jnp.pad(local_part, ((0, 16 - tokens), (0, 128 - experts)))

    x_own = sums[0][6]
    rows_back = []
    last = len(PARTS) - 1
    for index, (pieces, weight, _) in enumerate(packs):
        _, _, x_slot, _, toward, scatter, _ = sums[index]
        has_own, has_router = index == 0, index == last
        kept, sent, extra = call(
            functools.partial(back_kernel, slots, share, has_own),
            [place, *pieces, gate_weight, up_weight, router_tall, toward, weight, scatter, x_slot, extra, x_own],
            [
                ((chunks * 8, width), F32),
                ((chunks * 8 + 16 * (not has_own), width), BF),
                ((8, width), F32),
            ],
            2 * chunks * 16 * width * 2 * hidden,
        )
        got = exchange(sent, "c", 1)
        (pair,) = call(
            functools.partial(pair_kernel, groups, has_router),
            [kept, got, extra],
            [((groups, per * 8 + 16 * has_router, width), BF)],
            chunks * 8 * width * 2,
        )
        rows_back.append(lax.all_to_all(pair, "q", 0, 0).astype(F32).sum(0))

    router_part = rows_back[last][per * 8 : per * 8 + 8] + rows_back[last][per * 8 + 8 :]
    router_high = lax.reduce_precision(router_part, 8, 7)
    router_rows = jnp.concatenate([router_high, router_part - router_high], 0)
    dx_rows = {
        k: rows_back[index][j * 8 : j * 8 + 8]
        for index, part in enumerate(PARTS)
        for j, k in enumerate(part)
    }
    expert_dx = dx_rows[0]
    router_grad = router_part
    for step in range(1, experts):
        sent = jnp.concatenate([dx_rows[step], router_rows], 0).astype(BF)
        got = exchange(sent, "e", step).astype(F32)
        expert_dx = expert_dx + got[:8]
        router_grad = router_grad + (got[8:16] + got[16:])
    rw = router_weight.astype(F32)
    router_dx = jnp.dot(local_part, rw, precision=HIGH)
    in_grad = (g_own.astype(F32) + expert_dx + router_dx).astype(BF)

    inputs = [place]
    for (pieces, _, _), part in zip(packs, sums):
        inputs += [*pieces, part[2], part[3]]
    gate_grad, up_grad, down_grad = call(
        functools.partial(weight_kernel, len(PARTS), slots, share),
        inputs,
        [((hidden, width), BF)] * 3,
        2 * len(PARTS) * slots * width * hidden * 3,
    )
    return in_grad[None], gate_grad, up_grad, down_grad, router_grad[:experts], losses[None]


def solution(mesh):
    sections, ways = mesh.devices.shape
    experts, cores = 4, 2
    groups = sections // (experts * cores)
    fine = Mesh(mesh.devices.reshape(experts, groups, cores, ways), ("e", "q", "c", "t"))
    section = ("e", "q", "c")
    in_specs = (
        P(section, None, "t"),
        P(section, None, "t"),
        P(None, "t"),
        P(section, "t"),
        P(section, "t"),
        P(section, "t"),
        P(section, None, None),
    )
    out_specs = (
        P(section, None, "t"),
        P(section, "t"),
        P(section, "t"),
        P(section, "t"),
        P(None, "t"),
        P(section, None),
    )
    return jax.shard_map(shards, mesh=fine, in_specs=in_specs, out_specs=out_specs, check_vma=False)
```

time: 180 us -> 184 us (1.022)
  starting transfers between devices: 25 us -> 67.2 us
  blocking collectives: 40.4 us -> 0 us
  Pallas kernels: 0 us -> 26.5 us
  matrix products: 23.5 us -> 0.77 us
  local copies, waits for them, and re-layouts: 9.74 us -> 17.6 us
  waiting for transfers between devices: 64.5 us -> 58.9 us
  other arithmetic: 13 us -> 9.39 us
    ppermute x3 -> x22, starting transfers between devices: 4.81 us -> 50.9 us  [exchange(): return lax.ppermute(value, axis, [(k, k ^ step) for k in range(count)])]
    pallas_call x0 -> x9, Pallas kernels: none -> 26.5 us  [call(): pl.pallas_call(body, in_specs=[SMEM if v.ndim == 1 else VMEM for v in ins...]
    ppermute x3 -> x22, waiting for transfers between devices: 1.11 us -> 24.8 us  [exchange(): return lax.ppermute(value, axis, [(k, k ^ step) for k in range(count)])]
    dot_general x19 -> x0, matrix products: 22.6 us -> none  [the longest x2 4.06 us: choose(): lax.dot_general(pick[half:], far, dims, preferred_element_type=F32)]
    all_to_all x1 -> x0, blocking collectives: 21.4 us -> none  [spread_out(): lax.all_to_all(jnp.broadcast_to(value[None], (count, *value.shape)), axis...]
    all_to_all x3 -> x2, waiting for transfers between devices: 38.2 us -> 18.7 us  [shards(): rows_back.append(lax.all_to_all(pair, 'q', 0, 0).astype(F32).sum(0))]
    all_gather x1 -> x0, blocking collectives: 19 us -> none  [shards(): whole = lax.all_gather(packed, 't', axis=0)]
    unnamed x30 -> x113, local copies, waits for them, and re-layouts: 3.95 us -> 14.2 us
  transfers between devices with their start and end apart: 8 -> 26, of which waited for: 7 -> 10; matrix products, arithmetic and copies ran while one was open for 6% -> 4% of each run, Pallas kernels for 0% -> 14%
where the time goes in v2:
time: 184 us; the launch traced here: 183 us
  starting transfers between devices  67.2 us (37%)
  waiting for transfers between devices  58.9 us (32%)
  Pallas kernels  26.5 us (14%)
  local copies, waits for them, and re-layouts  17.6 us (10%)
  other arithmetic  9.39 us (5%)
  between operations  2.69 us (1%)
    ppermute x22, starting transfers between devices, exchange(): return lax.ppermute(value, axis, [(k, k ^ step) for k in range(count)])  50.9 us
    pallas_call x9, Pallas kernels, call(): pl.pallas_call(body, in_specs=[SMEM if v.ndim == 1 else VMEM for v in ins...  26.5 us
    ppermute x22, waiting for transfers between devices, exchange(): return lax.ppermute(value, axis, [(k, k ^ step) for k in range(count)])  24.8 us
    all_to_all x2, waiting for transfers between devices, shards(): rows_back.append(lax.all_to_all(pair, 'q', 0, 0).astype(F32).sum(0))  18.7 us
    all_to_all x2, waiting for transfers between devices, spread_out(): lax.all_to_all(jnp.broadcast_to(value[None], (count, *value.shape)), axis...  15.4 us
    unnamed x113, local copies, waits for them, and re-layouts  14.2 us
    all_to_all x2, starting transfers between devices, spread_out(): lax.all_to_all(jnp.broadcast_to(value[None], (count, *value.shape)), axis...  8.44 us
    all_to_all x2, starting transfers between devices, shards(): rows_back.append(lax.all_to_all(pair, 'q', 0, 0).astype(F32).sum(0))  7.79 us
  transfers between devices with their start and end apart: 26, of which 10 were waited for; matrix products, arithmetic and copies ran while one was open for 4% of the time, Pallas kernels for 14%

profile of v2, /device:TPU:1, one launch (start us, length us, event | category | flops | bytes accessed | tf_op | source)
XLA Modules:
  0.0 183.0 jit_solution(7864306856125605154)
XLA Ops:
  2.2 10.4 %collective-permute-start = (bf16[16,1664]{1,0:T(8,128)(2,1)S(1)}, bf16[16,1664]{1,0:T(8,128)(2,1)S(1)}, u32[]{:S(2)}, u32[]{:S(2)}) collective-permute-start(bf16[16,1664]{1,0:T(8,128)(2,1)S(1)} %pad_maximum_fusion.8), channel_id=1, source_target_pairs={{0,192},{64,128},{128,64},{192,0},{1,193},{65,129},{129,65},{193,1... | collective-permute-start | bytes 159752 | tf_op jit(solution)/shard_map/ppermute | solution.py:241
  12.6 2.0 %collective-permute-done = bf16[16,1664]{1,0:T(8,128)(2,1)S(1)} collective-permute-done((bf16[16,1664]{1,0:T(8,128)(2,1)S(1)}, bf16[16,1664]{1,0:T(8,128)(2,1)S(1)}, u32[]{:S(2)}, u32[]{:S(2)}) %collective-permute-start) | collective-permute-done | bytes 53280 | tf_op jit(solution)/shard_map/ppermute | solution.py:241
  16.3 4.2 %all-to-all-start = ((bf16[8,32,1664]{2,1,0:T(8,128)(2,1)}), bf16[8,32,1664]{2,1,0:T(8,128)(2,1)}, u32[]{:S(2)}, u32[]{:S(2)}) async-start(bf16[8,32,1664]{2,1,0:T(8,128)(2,1)} %broadcast_in_dim.8), calls=%async_computation | async-start | bytes 1703936 | tf_op jit(solution)/shard_map/all_to_all | solution.py:246
  21.8 8.2 %collective-permute-start.10 = (bf16[16,1664]{1,0:T(8,128)(2,1)S(1)}, bf16[16,1664]{1,0:T(8,128)(2,1)S(1)}, u32[]{:S(2)}, u32[]{:S(2)}) collective-permute-start(bf16[16,1664]{1,0:T(8,128)(2,1)S(1)} %pad_maximum_fusion.8), channel_id=1, source_target_pairs={{0,128},{64,192},{128,0},{192,64},{1,129},{65,193},{129,1},{193,65... | collective-permute-start | bytes 159752 | tf_op jit(solution)/shard_map/ppermute | solution.py:241
  30.0 1.5 collective-permute-done.10
  31.6 2.6 %all-to-all-done = bf16[8,32,1664]{2,1,0:T(8,128)(2,1)} async-done(((bf16[8,32,1664]{2,1,0:T(8,128)(2,1)}), bf16[8,32,1664]{2,1,0:T(8,128)(2,1)}, u32[]{:S(2)}, u32[]{:S(2)}) %all-to-all-start) | async-done | bytes 852000 | tf_op jit(solution)/shard_map/all_to_all | solution.py:246
  35.2 4.2 %all-to-all-start.2 = ((bf16[8,32,1664]{2,1,0:T(8,128)(2,1)}), bf16[8,32,1664]{2,1,0:T(8,128)(2,1)}, u32[]{:S(2)}, u32[]{:S(2)}) async-start(bf16[8,32,1664]{2,1,0:T(8,128)(2,1)} %broadcast_in_dim.9), calls=%async_computation.2 | async-start | bytes 1703936 | tf_op jit(solution)/shard_map/all_to_all | solution.py:246
  40.3 12.8 %all-to-all-done.2 = bf16[8,32,1664]{2,1,0:T(8,128)(2,1)} async-done(((bf16[8,32,1664]{2,1,0:T(8,128)(2,1)}), bf16[8,32,1664]{2,1,0:T(8,128)(2,1)}, u32[]{:S(2)}, u32[]{:S(2)}) %all-to-all-start.2) | async-done | bytes 852000 | tf_op jit(solution)/shard_map/all_to_all | solution.py:246
  56.2 4.5 %shard_map.118 = (f32[176,384]{1,0:T(8,128)S(1)}, bf16[176,384]{1,0:T(8,128)(2,1)S(1)}, bf16[176,384]{1,0:T(8,128)(2,1)S(1)}, bf16[176,384]{1,0:T(8,128)(2,1)S(1...) custom-call(s32[3]{0:T(128)S(1)} %pad_add_fusion.place, ...), custom_call_target="tpu_custom_call" | custom-call | flops 1258291200 | bytes 6815756 | tf_op jit(solution)/shard_map/pallas_call | solution.py:226
  63.6 2.8 %collective-permute-start.3 = (bf16[176,384]{1,0:T(8,128)(2,1)S(1)}, bf16[176,384]{1,0:T(8,128)(2,1)S(1)}, u32[]{:S(2)}, u32[]{:S(2)}) collective-permute-start(bf16[176,384]{1,0:T(8,128)(2,1)S(1)} %get-tuple-element.39), channel_id=1, source_target_pairs={{0,2},{1,3},{2,0},{3,1},{4,6},{5,7},{6,4},{7,5},{8,10},{9,11},{10,... | collective-permute-start | bytes 405512 | tf_op jit(solution)/shard_map/ppermute | solution.py:241
  67.5 4.9 %shard_map.122 = (f32[176,384]{1,0:T(8,128)S(1)}, bf16[176,384]{1,0:T(8,128)(2,1)}, bf16[176,384]{1,0:T(8,128)(2,1)}, bf16[176,384]{1,0:T(8,128)(2,1)S(1)}, bf16...) custom-call(s32[3]{0:T(128)S(1)} %pad_add_fusion.place, ...), custom_call_target="tpu_custom_call" | custom-call | flops 1258291200 | bytes 6815756 | tf_op jit(solution)/shard_map/pallas_call | solution.py:226
  74.9 2.2 %collective-permute-start.13 = (bf16[176,384]{1,0:T(8,128)(2,1)}, bf16[176,384]{1,0:T(8,128)(2,1)}, u32[]{:S(2)}, u32[]{:S(2)}) collective-permute-start(bf16[176,384]{1,0:T(8,128)(2,1)} %get-tuple-element.53), channel_id=1, source_target_pairs={{0,2},{1,3},{2,0},{3,1},{4,6},{5,7},{6,4},{7,5},{8,10},{9,11},{10,... | collective-permute-start | bytes 405512 | tf_op jit(solution)/shard_map/ppermute | solution.py:241
  81.5 2.4 %collective-permute-start.7 = (bf16[176,384]{1,0:T(8,128)(2,1)}, bf16[176,384]{1,0:T(8,128)(2,1)S(1)}, u32[]{:S(2)}, u32[]{:S(2)}) collective-permute-start(bf16[176,384]{1,0:T(8,128)(2,1)} %copy-done.21), channel_id=1, source_target_pairs={{0,3},{1,2},{2,1},{3,0},{4,7},{5,6},{6,5},{7,4},{8,11},{9,10},{10,... | collective-permute-start | bytes 405512 | tf_op jit(solution)/shard_map/ppermute | solution.py:241
  83.9 2.6 %collective-permute-start.6 = (bf16[176,384]{1,0:T(8,128)(2,1)}, bf16[176,384]{1,0:T(8,128)(2,1)S(1)}, u32[]{:S(2)}, u32[]{:S(2)}) collective-permute-start(bf16[176,384]{1,0:T(8,128)(2,1)} %copy-done.21), channel_id=1, source_target_pairs={{0,2},{1,3},{2,0},{3,1},{4,6},{5,7},{6,4},{7,5},{8,10},{9,11},{10,... | collective-permute-start | bytes 405512 | tf_op jit(solution)/shard_map/ppermute | solution.py:241
  89.0 2.2 %collective-permute-start.14 = (bf16[176,384]{1,0:T(8,128)(2,1)}, bf16[176,384]{1,0:T(8,128)(2,1)S(1)}, u32[]{:S(2)}, u32[]{:S(2)}) collective-permute-start(bf16[176,384]{1,0:T(8,128)(2,1)} %copy-done.50), channel_id=1, source_target_pairs={{0,3},{1,2},{2,1},{3,0},{4,7},{5,6},{6,5},{7,4},{8,11},{9,10},{10,... | collective-permute-start | bytes 405512 | tf_op jit(solution)/shard_map/ppermute | solution.py:241
  91.2 8.7 %collective-permute-done.6.p2.refs_2_ = bf16[176,384]{1,0:T(8,128)(2,1)S(1)} collective-permute-done((bf16[176,384]{1,0:T(8,128)(2,1)}, bf16[176,384]{1,0:T(8,128)(2,1)S(1)}, u32[]{:S(2)}, u32[]{:S(2)}) %collective-permute-start.6) | collective-permute-done | bytes 135200 | tf_op jit(solution)/shard_map/ppermute | solution.py:241
  105.4 3.8 %shard_map.120 = (f32[128,1536]{1,0:T(8,128)S(1)}, bf16[128,1536]{1,0:T(8,128)(2,1)S(1)}, f32[8,1536]{1,0:T(8,128)S(1)}) custom-call(s32[3]{0:T(128)S(1)} %pad_add_fusion.place, bf16[176,384]{1,0:T(8,128)(2,1)S(1)} %copy-done.22, bf16[176,384]{1,0:T(8,128)(2,1)S(1)} %collective-permute-done.5.p1.refs_1_, ...), custom_call_target="tpu_custom_call" | custom-call | flops 805306368 | bytes 4833292 | tf_op jit(solution)/shard_map/pallas_call | solution.py:226
  109.3 2.6 %collective-permute-start.8 = (bf16[128,1536]{1,0:T(8,128)(2,1)S(1)}, bf16[128,1536]{1,0:T(8,128)(2,1)S(1)}, u32[]{:S(2)}, u32[]{:S(2)}) collective-permute-start(bf16[128,1536]{1,0:T(8,128)(2,1)S(1)} %get-tuple-element.49), channel_id=1, source_target_pairs={{0,4},{4,0},{1,5},{5,1},{2,6},{6,2},{3,7},{7,3},{8,12},{12,8},{9,1... | collective-permute-start | bytes 1179656 | tf_op jit(solution)/shard_map/ppermute | solution.py:241
  112.0 1.7 shard_map.123
  113.7 1.8 %collective-permute-start.17 = (bf16[176,384]{1,0:T(8,128)(2,1)S(1)}, bf16[176,384]{1,0:T(8,128)(2,1)S(1)}, u32[]{:S(2)}, u32[]{:S(2)}) collective-permute-start(bf16[176,384]{1,0:T(8,128)(2,1)S(1)} %get-tuple-element.56.p0.refs_6_), channel_id=1, source_target_pairs={{0,3},{1,2},{2,1},{3,0},{4,7},{5,6},{6,5},{7,4},{8,11},{9,10},{10,... | collective-permute-start | bytes 405512 | tf_op jit(solution)/shard_map/ppermute | solution.py:241
  115.5 1.7 collective-permute-start.15
  117.2 3.4 %collective-permute-done.17.p3.refs_9_ = bf16[176,384]{1,0:T(8,128)(2,1)S(1)} collective-permute-done((bf16[176,384]{1,0:T(8,128)(2,1)S(1)}, bf16[176,384]{1,0:T(8,128)(2,1)S(1)}, u32[]{:S(2)}, u32[]{:S(2)}) %collective-permute-start.17) | collective-permute-done | bytes 135200 | tf_op jit(solution)/shard_map/ppermute | solution.py:241
  120.7 6.2 %collective-permute-done.16.p2.refs_8_ = bf16[176,384]{1,0:T(8,128)(2,1)S(1)} collective-permute-done((bf16[176,384]{1,0:T(8,128)(2,1)S(1)}, bf16[176,384]{1,0:T(8,128)(2,1)S(1)}, u32[]{:S(2)}, u32[]{:S(2)}) %collective-permute-start.16) | collective-permute-done | bytes 135200 | tf_op jit(solution)/shard_map/ppermute | solution.py:241
  126.9 4.4 %shard_map.124 = (f32[128,1536]{1,0:T(8,128)S(1)}, bf16[144,1536]{1,0:T(8,128)(2,1)}, f32[8,1536]{1,0:T(8,128)S(1)}) custom-call(s32[3]{0:T(128)S(1)} %pad_add_fusion.place, bf16[176,384]{1,0:T(8,128)(2,1)S(1)} %get-tuple-element.56.p0.refs_6_, bf16[176,384]{1,0:T(8,128)(2,1)S(1)} %collective-permute-done.15.p1.refs_7_, ...), custom_call_target="tpu_custom_call" | custom-call | flops 805306368 | bytes 4874252 | tf_op jit(solution)/shard_map/pallas_call | solution.py:226
  134.1 3.5 %all-to-all-start.1 = ((bf16[8,16,1536]{2,1,0:T(8,128)(2,1)}), bf16[8,16,1536]{2,1,0:T(8,128)(2,1)S(1)}, u32[]{:S(2)}, u32[]{:S(2)}) async-start(bf16[8,16,1536]{2,1,0:T(8,128)(2,1)} %shard_map.121), calls=%async_computation.1 | async-start | bytes 786432 | tf_op jit(solution)/shard_map/all_to_all | solution.py:345
  138.5 7.8 %all-to-all-done.1 = bf16[8,16,1536]{2,1,0:T(8,128)(2,1)S(1)} async-done(((bf16[8,16,1536]{2,1,0:T(8,128)(2,1)}), bf16[8,16,1536]{2,1,0:T(8,128)(2,1)S(1)}, u32[]{:S(2)}, u32[]{:S(2)}) %all-to-all-start.1) | async-done | bytes 393248 | tf_op jit(solution)/shard_map/all_to_all | solution.py:345
  146.4 4.3 %all-to-all-start.3 = ((bf16[8,32,1536]{2,1,0:T(8,128)(2,1)}), bf16[8,32,1536]{2,1,0:T(8,128)(2,1)}, u32[]{:S(2)}, u32[]{:S(2)}) async-start(bf16[8,32,1536]{2,1,0:T(8,128)(2,1)} %shard_map.125), calls=%async_computation.3 | async-start | bytes 1572864 | tf_op jit(solution)/shard_map/all_to_all | solution.py:345
  152.9 10.9 %all-to-all-done.3 = bf16[8,32,1536]{2,1,0:T(8,128)(2,1)} async-done(((bf16[8,32,1536]{2,1,0:T(8,128)(2,1)}), bf16[8,32,1536]{2,1,0:T(8,128)(2,1)}, u32[]{:S(2)}, u32[]{:S(2)}) %all-to-all-start.3) | async-done | bytes 786464 | tf_op jit(solution)/shard_map/all_to_all | solution.py:345
  165.2 1.7 collective-permute-start.19
  166.8 5.0 %collective-permute-start.20 = (bf16[24,1536]{1,0:T(8,128)(2,1)S(1)}, bf16[24,1536]{1,0:T(8,128)(2,1)S(1)}, u32[]{:S(2)}, u32[]{:S(2)}) collective-permute-start(bf16[24,1536]{1,0:T(8,128)(2,1)S(1)} %get-tuple-element.79), channel_id=1, source_target_pairs={{0,128},{64,192},{128,0},{192,64},{1,129},{65,193},{129,1},{193,65... | collective-permute-start | bytes 221192 | tf_op jit(solution)/shard_map/ppermute | solution.py:241
  173.4 5.1 %shard_map.126 = (bf16[512,1536]{1,0:T(8,128)(2,1)}, bf16[512,1536]{1,0:T(8,128)(2,1)}, bf16[512,1536]{1,0:T(8,128)(2,1)}) custom-call(s32[3]{0:T(128)S(1)} %pad_add_fusion.place, bf16[176,384]{1,0:T(8,128)(2,1)S(1)} %copy-done.23, bf16[176,384]{1,0:T(8,128)(2,1)S(1)} %copy-done.29, bf16[176,384]{1,0:T(8,128)(2,1)S(1)} %copy-done.27, ...), custom_call_target="tpu_custom_call" | custom-call | flops 1509949440 | bytes 3047436 | tf_op jit(solution)/shard_map/pallas_call | solution.py:226
  178.5 2.9 %collective-permute-done.21 = bf16[24,1536]{1,0:T(8,128)(2,1)S(1)} collective-permute-done((bf16[24,1536]{1,0:T(8,128)(2,1)S(1)}, bf16[24,1536]{1,0:T(8,128)(2,1)S(1)}, u32[]{:S(2)}, u32[]{:S(2)}) %collective-permute-start.21) | collective-permute-done | bytes 73760 | tf_op jit(solution)/shard_map/ppermute | solution.py:241
  (179 shorter events, 37.1 us)
Async XLA Ops:
  2.2 12.3 %collective-permute-start = (bf16[16,1664]{1,0:T(8,128)(2,1)S(1)}, bf16[16,1664]{1,0:T(8,128)(2,1)S(1)}, u32[]{:S(2)}, u32[]{:S(2)}) collective-permute-start(bf16[16,1664]{1,0:T(8,128)(2,1)S(1)} %pad_maximum_fusion.8), channel_id=1, source_target_pairs={{0,192},{64,128},{128,64},{192,0},{1,193},{65,129},{129,65},{193,1... | collective-permute-start | bytes 159752 | tf_op jit(solution)/shard_map/ppermute | solution.py:241
  16.3 18.0 %all-to-all-start = ((bf16[8,32,1664]{2,1,0:T(8,128)(2,1)}), bf16[8,32,1664]{2,1,0:T(8,128)(2,1)}, u32[]{:S(2)}, u32[]{:S(2)}) async-start(bf16[8,32,1664]{2,1,0:T(8,128)(2,1)} %broadcast_in_dim.8), calls=%async_computation | async-start | bytes 1703936 | tf_op jit(solution)/shard_map/all_to_all | solution.py:246
  20.5 33.5 %copy-start.54 = (s32[1,8,2]{1,2,0:T(2,128)S(1)}, s32[1,8,2]{1,2,0:T(2,128)}, u32[]{:S(2)}) copy-start(s32[1,8,2]{1,2,0:T(2,128)} %param.13) | copy-start | bytes 196
  20.5 34.1 %copy-start.52 = (bf16[4,1536]{1,0:T(4,128)(2,1)S(1)}, bf16[4,1536]{1,0:T(4,128)(2,1)}, u32[]{:S(2)}) copy-start(bf16[4,1536]{1,0:T(4,128)(2,1)} %param.9) | copy-start | bytes 36868
  20.5 9.5 %collective-permute-start.9 = (bf16[16,1664]{1,0:T(8,128)(2,1)S(1)}, bf16[16,1664]{1,0:T(8,128)(2,1)S(1)}, u32[]{:S(2)}, u32[]{:S(2)}) collective-permute-start(bf16[16,1664]{1,0:T(8,128)(2,1)S(1)} %pad_maximum_fusion.8), channel_id=1, source_target_pairs={{0,64},{64,0},{128,192},{192,128},{1,65},{65,1},{129,193},{193,129... | collective-permute-start | bytes 159752 | tf_op jit(solution)/shard_map/ppermute | solution.py:241
  21.8 9.8 %collective-permute-start.10 = (bf16[16,1664]{1,0:T(8,128)(2,1)S(1)}, bf16[16,1664]{1,0:T(8,128)(2,1)S(1)}, u32[]{:S(2)}, u32[]{:S(2)}) collective-permute-start(bf16[16,1664]{1,0:T(8,128)(2,1)S(1)} %pad_maximum_fusion.8), channel_id=1, source_target_pairs={{0,128},{64,192},{128,0},{192,64},{1,129},{65,193},{129,1},{193,65... | collective-permute-start | bytes 159752 | tf_op jit(solution)/shard_map/ppermute | solution.py:241
  31.6 23.2 %copy-start.1 = (bf16[512,1536]{1,0:T(8,128)(2,1)S(1)}, bf16[512,1536]{1,0:T(8,128)(2,1)}, u32[]{:S(2)}) copy-start(bf16[512,1536]{1,0:T(8,128)(2,1)} %up_w.7) | copy-start | bytes 4718596
  31.6 23.2 %copy-start = (bf16[512,1536]{1,0:T(8,128)(2,1)S(1)}, bf16[512,1536]{1,0:T(8,128)(2,1)}, u32[]{:S(2)}) copy-start(bf16[512,1536]{1,0:T(8,128)(2,1)} %gate_w.7) | copy-start | bytes 4718596
  35.2 18.0 %all-to-all-start.2 = ((bf16[8,32,1664]{2,1,0:T(8,128)(2,1)}), bf16[8,32,1664]{2,1,0:T(8,128)(2,1)}, u32[]{:S(2)}, u32[]{:S(2)}) async-start(bf16[8,32,1664]{2,1,0:T(8,128)(2,1)} %broadcast_in_dim.9), calls=%async_computation.2 | async-start | bytes 1703936 | tf_op jit(solution)/shard_map/all_to_all | solution.py:246
  39.4 15.4 %collective-permute-start.1 = (bf16[256,1664]{1,0:T(8,128)(2,1)}, bf16[256,1664]{1,0:T(8,128)(2,1)}, u32[]{:S(2)}, u32[]{:S(2)}) collective-permute-start(bf16[256,1664]{1,0:T(8,128)(2,1)} %bitcast.6.near), channel_id=1, source_target_pairs={{0,4},{4,0},{1,5},{5,1},{2,6},{6,2},{3,7},{7,3},{8,12},{12,8},{9,1... | collective-permute-start | bytes 2555912 | tf_op jit(solution)/shard_map/ppermute | solution.py:241
  53.1 14.4 %collective-permute-start.11 = (bf16[256,1664]{1,0:T(8,128)(2,1)}, bf16[256,1664]{1,0:T(8,128)(2,1)}, u32[]{:S(2)}, u32[]{:S(2)}) collective-permute-start(bf16[256,1664]{1,0:T(8,128)(2,1)} %bitcast.8.near), channel_id=1, source_target_pairs={{0,4},{4,0},{1,5},{5,1},{2,6},{6,2},{3,7},{7,3},{8,12},{12,8},{9,1... | collective-permute-start | bytes 2555912 | tf_op jit(solution)/shard_map/ppermute | solution.py:241
  62.9 14.3 %collective-permute-start.2 = (bf16[176,384]{1,0:T(8,128)(2,1)S(1)}, bf16[176,384]{1,0:T(8,128)(2,1)S(1)}, u32[]{:S(2)}, u32[]{:S(2)}) collective-permute-start(bf16[176,384]{1,0:T(8,128)(2,1)S(1)} %get-tuple-element.38), channel_id=1, source_target_pairs={{0,1},{1,0},{2,3},{3,2},{4,5},{5,4},{6,7},{7,6},{8,9},{9,8},{10,11... | collective-permute-start | bytes 405512 | tf_op jit(solution)/shard_map/ppermute | solution.py:241
  63.6 13.5 %collective-permute-start.3 = (bf16[176,384]{1,0:T(8,128)(2,1)S(1)}, bf16[176,384]{1,0:T(8,128)(2,1)S(1)}, u32[]{:S(2)}, u32[]{:S(2)}) collective-permute-start(bf16[176,384]{1,0:T(8,128)(2,1)S(1)} %get-tuple-element.39), channel_id=1, source_target_pairs={{0,2},{1,3},{2,0},{3,1},{4,6},{5,7},{6,4},{7,5},{8,10},{9,11},{10,... | collective-permute-start | bytes 405512 | tf_op jit(solution)/shard_map/ppermute | solution.py:241
  66.3 10.8 %collective-permute-start.4 = (bf16[176,384]{1,0:T(8,128)(2,1)S(1)}, bf16[176,384]{1,0:T(8,128)(2,1)S(1)}, u32[]{:S(2)}, u32[]{:S(2)}) collective-permute-start(bf16[176,384]{1,0:T(8,128)(2,1)S(1)} %get-tuple-element.40), channel_id=1, source_target_pairs={{0,3},{1,2},{2,1},{3,0},{4,7},{5,6},{6,5},{7,4},{8,11},{9,10},{10,... | collective-permute-start | bytes 405512 | tf_op jit(solution)/shard_map/ppermute | solution.py:241
  74.6 37.3 %collective-permute-start.12 = (bf16[176,384]{1,0:T(8,128)(2,1)}, bf16[176,384]{1,0:T(8,128)(2,1)}, u32[]{:S(2)}, u32[]{:S(2)}) collective-permute-start(bf16[176,384]{1,0:T(8,128)(2,1)} %get-tuple-element.52), channel_id=1, source_target_pairs={{0,1},{1,0},{2,3},{3,2},{4,5},{5,4},{6,7},{7,6},{8,9},{9,8},{10,11... | collective-permute-start | bytes 405512 | tf_op jit(solution)/shard_map/ppermute | solution.py:241
  74.9 37.1 %collective-permute-start.13 = (bf16[176,384]{1,0:T(8,128)(2,1)}, bf16[176,384]{1,0:T(8,128)(2,1)}, u32[]{:S(2)}, u32[]{:S(2)}) collective-permute-start(bf16[176,384]{1,0:T(8,128)(2,1)} %get-tuple-element.53), channel_id=1, source_target_pairs={{0,2},{1,3},{2,0},{3,1},{4,6},{5,7},{6,4},{7,5},{8,10},{9,11},{10,... | collective-permute-start | bytes 405512 | tf_op jit(solution)/shard_map/ppermute | solution.py:241
  81.5 7.5 %collective-permute-start.7 = (bf16[176,384]{1,0:T(8,128)(2,1)}, bf16[176,384]{1,0:T(8,128)(2,1)S(1)}, u32[]{:S(2)}, u32[]{:S(2)}) collective-permute-start(bf16[176,384]{1,0:T(8,128)(2,1)} %copy-done.21), channel_id=1, source_target_pairs={{0,3},{1,2},{2,1},{3,0},{4,7},{5,6},{6,5},{7,4},{8,11},{9,10},{10,... | collective-permute-start | bytes 405512 | tf_op jit(solution)/shard_map/ppermute | solution.py:241
  83.9 16.0 %collective-permute-start.6 = (bf16[176,384]{1,0:T(8,128)(2,1)}, bf16[176,384]{1,0:T(8,128)(2,1)S(1)}, u32[]{:S(2)}, u32[]{:S(2)}) collective-permute-start(bf16[176,384]{1,0:T(8,128)(2,1)} %copy-done.21), channel_id=1, source_target_pairs={{0,2},{1,3},{2,0},{3,1},{4,6},{5,7},{6,4},{7,5},{8,10},{9,11},{10,... | collective-permute-start | bytes 405512 | tf_op jit(solution)/shard_map/ppermute | solution.py:241
  86.5 13.4 %collective-permute-start.5 = (bf16[176,384]{1,0:T(8,128)(2,1)}, bf16[176,384]{1,0:T(8,128)(2,1)S(1)}, u32[]{:S(2)}, u32[]{:S(2)}) collective-permute-start(bf16[176,384]{1,0:T(8,128)(2,1)} %copy-done.21), channel_id=1, source_target_pairs={{0,1},{1,0},{2,3},{3,2},{4,5},{5,4},{6,7},{7,6},{8,9},{9,8},{10,11... | collective-permute-start | bytes 405512 | tf_op jit(solution)/shard_map/ppermute | solution.py:241
  89.0 22.9 %collective-permute-start.14 = (bf16[176,384]{1,0:T(8,128)(2,1)}, bf16[176,384]{1,0:T(8,128)(2,1)S(1)}, u32[]{:S(2)}, u32[]{:S(2)}) collective-permute-start(bf16[176,384]{1,0:T(8,128)(2,1)} %copy-done.50), channel_id=1, source_target_pairs={{0,3},{1,2},{2,1},{3,0},{4,7},{5,6},{6,5},{7,4},{8,11},{9,10},{10,... | collective-permute-start | bytes 405512 | tf_op jit(solution)/shard_map/ppermute | solution.py:241
  109.3 24.0 %collective-permute-start.8 = (bf16[128,1536]{1,0:T(8,128)(2,1)S(1)}, bf16[128,1536]{1,0:T(8,128)(2,1)S(1)}, u32[]{:S(2)}, u32[]{:S(2)}) collective-permute-start(bf16[128,1536]{1,0:T(8,128)(2,1)S(1)} %get-tuple-element.49), channel_id=1, source_target_pairs={{0,4},{4,0},{1,5},{5,1},{2,6},{6,2},{3,7},{7,3},{8,12},{12,8},{9,1... | collective-permute-start | bytes 1179656 | tf_op jit(solution)/shard_map/ppermute | solution.py:241
  113.7 7.0 %collective-permute-start.17 = (bf16[176,384]{1,0:T(8,128)(2,1)S(1)}, bf16[176,384]{1,0:T(8,128)(2,1)S(1)}, u32[]{:S(2)}, u32[]{:S(2)}) collective-permute-start(bf16[176,384]{1,0:T(8,128)(2,1)S(1)} %get-tuple-element.56.p0.refs_6_), channel_id=1, source_target_pairs={{0,3},{1,2},{2,1},{3,0},{4,7},{5,6},{6,5},{7,4},{8,11},{9,10},{10,... | collective-permute-start | bytes 405512 | tf_op jit(solution)/shard_map/ppermute | solution.py:241
  115.5 11.3 %collective-permute-start.16 = (bf16[176,384]{1,0:T(8,128)(2,1)S(1)}, bf16[176,384]{1,0:T(8,128)(2,1)S(1)}, u32[]{:S(2)}, u32[]{:S(2)}) collective-permute-start(bf16[176,384]{1,0:T(8,128)(2,1)S(1)} %get-tuple-element.56.p0.refs_6_), channel_id=1, source_target_pairs={{0,2},{1,3},{2,0},{3,1},{4,6},{5,7},{6,4},{7,5},{8,10},{9,11},{10,... | collective-permute-start | bytes 405512 | tf_op jit(solution)/shard_map/ppermute | solution.py:241
  115.5 11.3 %collective-permute-start.15 = (bf16[176,384]{1,0:T(8,128)(2,1)S(1)}, bf16[176,384]{1,0:T(8,128)(2,1)S(1)}, u32[]{:S(2)}, u32[]{:S(2)}) collective-permute-start(bf16[176,384]{1,0:T(8,128)(2,1)S(1)} %get-tuple-element.56.p0.refs_6_), channel_id=1, source_target_pairs={{0,1},{1,0},{2,3},{3,2},{4,5},{5,4},{6,7},{7,6},{8,9},{9,8},{10,11... | collective-permute-start | bytes 405512 | tf_op jit(solution)/shard_map/ppermute | solution.py:241
  132.8 4.7 %collective-permute-start.18 = (bf16[144,1536]{1,0:T(8,128)(2,1)}, bf16[144,1536]{1,0:T(8,128)(2,1)S(1)}, u32[]{:S(2)}, u32[]{:S(2)}) collective-permute-start(bf16[144,1536]{1,0:T(8,128)(2,1)} %get-tuple-element.61), channel_id=1, source_target_pairs={{0,4},{4,0},{1,5},{5,1},{2,6},{6,2},{3,7},{7,3},{8,12},{12,8},{9,1... | collective-permute-start | bytes 1327112 | tf_op jit(solution)/shard_map/ppermute | solution.py:241
  134.1 12.3 %all-to-all-start.1 = ((bf16[8,16,1536]{2,1,0:T(8,128)(2,1)}), bf16[8,16,1536]{2,1,0:T(8,128)(2,1)S(1)}, u32[]{:S(2)}, u32[]{:S(2)}) async-start(bf16[8,16,1536]{2,1,0:T(8,128)(2,1)} %shard_map.121), calls=%async_computation.1 | async-start | bytes 786432 | tf_op jit(solution)/shard_map/all_to_all | solution.py:345
  146.4 26.9 %copy-start.47 = (bf16[160,1536]{1,0:T(8,128)(2,1)S(1)}, bf16[160,1536]{1,0:T(8,128)(2,1)}, u32[]{:S(2)}) copy-start(bf16[160,1536]{1,0:T(8,128)(2,1)} %copy-done.46) | copy-start | bytes 1474564
  146.4 26.9 %copy-start.49 = (bf16[160,1536]{1,0:T(8,128)(2,1)S(1)}, bf16[160,1536]{1,0:T(8,128)(2,1)}, u32[]{:S(2)}) copy-start(bf16[160,1536]{1,0:T(8,128)(2,1)} %copy-done.48) | copy-start | bytes 1474564
  146.4 17.4 %all-to-all-start.3 = ((bf16[8,32,1536]{2,1,0:T(8,128)(2,1)}), bf16[8,32,1536]{2,1,0:T(8,128)(2,1)}, u32[]{:S(2)}, u32[]{:S(2)}) async-start(bf16[8,32,1536]{2,1,0:T(8,128)(2,1)} %shard_map.125), calls=%async_computation.3 | async-start | bytes 1572864 | tf_op jit(solution)/shard_map/all_to_all | solution.py:345
  165.2 16.4 %collective-permute-start.19 = (bf16[24,1536]{1,0:T(8,128)(2,1)S(1)}, bf16[24,1536]{1,0:T(8,128)(2,1)S(1)}, u32[]{:S(2)}, u32[]{:S(2)}) collective-permute-start(bf16[24,1536]{1,0:T(8,128)(2,1)S(1)} %get-tuple-element.78), channel_id=1, source_target_pairs={{0,64},{64,0},{128,192},{192,128},{1,65},{65,1},{129,193},{193,129... | collective-permute-start | bytes 221192 | tf_op jit(solution)/shard_map/ppermute | solution.py:241
  166.8 14.6 %collective-permute-start.20 = (bf16[24,1536]{1,0:T(8,128)(2,1)S(1)}, bf16[24,1536]{1,0:T(8,128)(2,1)S(1)}, u32[]{:S(2)}, u32[]{:S(2)}) collective-permute-start(bf16[24,1536]{1,0:T(8,128)(2,1)S(1)} %get-tuple-element.79), channel_id=1, source_target_pairs={{0,128},{64,192},{128,0},{192,64},{1,129},{65,193},{129,1},{193,65... | collective-permute-start | bytes 221192 | tf_op jit(solution)/shard_map/ppermute | solution.py:241
  171.8 9.6 %collective-permute-start.21 = (bf16[24,1536]{1,0:T(8,128)(2,1)S(1)}, bf16[24,1536]{1,0:T(8,128)(2,1)S(1)}, u32[]{:S(2)}, u32[]{:S(2)}) collective-permute-start(bf16[24,1536]{1,0:T(8,128)(2,1)S(1)} %get-tuple-element.80), channel_id=1, source_target_pairs={{0,192},{64,128},{128,64},{192,0},{1,193},{65,129},{129,65},{193,1... | collective-permute-start | bytes 221192 | tf_op jit(solution)/shard_map/ppermute | solution.py:241
  (50 other events, 473.5 us)

commit v3 on v1

v3 whole, which is shorter than its diff:
```python
import functools

import jax
import jax.numpy as jnp
import numpy as np
from jax import lax
from jax.experimental import pallas as pl
from jax.experimental.pallas import tpu as pltpu
from jax.sharding import Mesh, PartitionSpec as P

CAP = 5
Z_WEIGHT = 0.25
BALANCE_WEIGHT = 1.0
BF = jnp.bfloat16
F32 = jnp.float32
GROUPS = 8
VMEM_LIMIT = 16 * 2**20
VMEM = pl.BlockSpec(memory_space=pltpu.VMEM)
NT = (((1,), (1,)), ((), ()))
TN = (((0,), (0,)), ((), ()))


def matmul(a, b, dims=(((1,), (0,)), ((), ()))):
    return lax.dot_general(a, b, dims, preferred_element_type=F32)


def split_pair(value):
    high = value.astype(BF)
    return high, (value - high.astype(F32)).astype(BF)


def up_to(count, step):
    return -(-count // step) * step


def to_row(value):
    count = value.shape[0]
    padded = up_to(count, 128)
    if padded > count:
        value = jnp.concatenate([value, jnp.zeros((padded - count, 128), F32)], 0)
    return jnp.sum(value.T, axis=0, keepdims=True)


def to_column(row, count):
    padded = up_to(count, 128)
    return jnp.broadcast_to(row[:, :padded], (128, padded)).T[:count]


def row_pair(value, lanes):
    high, low = split_pair(to_row(value))
    rows = jnp.concatenate([high.astype(F32), low.astype(F32), jnp.zeros((6, high.shape[1]), F32)], 0)
    if rows.shape[1] < lanes:
        rows = jnp.concatenate([rows, jnp.zeros((8, lanes - rows.shape[1]), F32)], 1)
    return rows


def spots(ids, expert, row):
    first = jnp.broadcast_to(ids[:, 0:1], ids.shape)
    second = jnp.broadcast_to(ids[:, 1:2], ids.shape)
    match = (first == expert) | (second == expert)
    matched = match.astype(F32)
    position = matched
    for step in (1, 2, 4):
        moved = pltpu.roll(position, step, 0)
        position = position + jnp.where((row & 7) >= step, moved, 0.0)
    return match, position - matched, first + second - expert


def pick_kernel(width, b0, b1, b2, b3, out):
    e_value = lax.axis_index("e").astype(F32)
    blocks = jnp.concatenate([b0[...], b1[...], b2[...], b3[...]], 0)
    rows = blocks.shape[0]
    row = lax.broadcasted_iota(jnp.int32, (rows, 128), 0)
    lane = lax.broadcasted_iota(jnp.int32, (rows, 128), 1).astype(F32)
    match, position, other = spots(blocks[:, width:].astype(F32), e_value, row)
    is_grad = (row & 8) > 0
    slot = (row >> 4).astype(F32) * CAP + position + jnp.where(is_grad, 4.0 * CAP, 0.0)
    slot = jnp.where(match, slot, -1.0)
    labels = lax.broadcasted_iota(jnp.int32, (rows, 8 * CAP), 1).astype(F32)
    pick = (jnp.broadcast_to(slot[:, 0:1], (rows, 8 * CAP)) == labels).astype(F32).astype(BF)
    sign = (lane == e_value).astype(F32) - (lane == other).astype(F32)
    sign = jnp.where(match & jnp.logical_not(is_grad), sign, 0.0).astype(BF)
    values = matmul(pick, blocks[:, :width], TN).astype(BF)
    signs = matmul(pick, sign, TN).astype(BF)
    for j in range(GROUPS):
        out[j, :, :width] = values
        out[j, :, width:] = signs


def project_kernel(
    width, share, has_own, block, gate_w, up_w, down_w, router_w, packer, own_block,
    own, send1, send2, send3, chosen, notes,
):
    t = lax.axis_index("t")
    slots = packer.shape[0] // 2
    taken = matmul(packer[:slots, :], block[...])
    x_slot, toward = taken[:, :width].astype(BF), taken[:, width:]
    g_slot = matmul(packer[slots:, :], block[:, :width]).astype(BF)
    chosen[:slots] = x_slot
    chosen[slots:] = g_slot
    lead = matmul(x_slot, router_w[...], NT) * toward
    notes[0:8] = row_pair(lead, 3 * share)
    notes[8:16] = jnp.zeros((8, 3 * share), F32)
    if has_own:
        own_high, own_low = split_pair(matmul(router_w[:16], own_block[:, :width], NT))
        notes[8:16, 0:16] = own_high[:8].astype(F32)
        notes[8:16, 128:144] = own_low[:8].astype(F32)
    own[:slots, 3 * share :] = toward
    own[slots:, 3 * share :] = jnp.zeros((16, 128), F32)
    for step, out in enumerate((own, send1, send2, send3)):
        rows_of = pl.ds(pl.multiple_of((t ^ step) * share, share), share)
        both = jnp.concatenate([gate_w[rows_of, :], up_w[rows_of, :]], 0)
        out[:slots, : 2 * share] = matmul(x_slot, both, NT).astype(out.dtype)
        out[:slots, 2 * share : 3 * share] = matmul(g_slot, down_w[rows_of, :], NT).astype(out.dtype)
        out[slots:, : 3 * share] = notes[...].astype(out.dtype)


def act_kernel(
    width, slots, share, experts, has_own, own_block, own, got1, got2, got3,
    packed, weight, local, losses,
):
    total = own[:, : 3 * share] + got1[...].astype(F32) + got2[...].astype(F32) + got3[...].astype(F32)
    toward = own[:slots, 3 * share :]
    used = jnp.sum(jnp.abs(toward), axis=1, keepdims=True) > 0.5
    lead = to_column(total[slots : slots + 1] + total[slots + 1 : slots + 2], slots)
    w = jnp.where(used, jax.nn.sigmoid(lead), 0.0)
    weight[...] = w * (1.0 - w) * toward
    gate_proj, up_proj, back_proj = (
        total[:slots, k * share : (k + 1) * share] for k in range(3)
    )
    gate_sig = jax.nn.sigmoid(gate_proj)
    silu_gate = gate_proj * gate_sig
    scaled = w * back_proj
    packed[:slots, :share] = (
        scaled * up_proj * gate_sig * (1.0 + gate_proj * (1.0 - gate_sig))
    ).astype(BF)
    packed[:slots, share : 2 * share] = (scaled * silu_gate).astype(BF)
    packed[:slots, 2 * share :] = (w * silu_gate * up_proj).astype(BF)
    rows = row_pair(silu_gate * up_proj * back_proj, 3 * share)
    packed[slots:] = jnp.concatenate([rows, jnp.zeros((8, 3 * share), F32)], 0).astype(BF)
    if not has_own:
        local[...] = jnp.zeros_like(local)
        losses[...] = jnp.zeros_like(losses)
        return

    logits = total[slots + 8 :, :128] + total[slots + 8 :, 128:256]
    expert = lax.broadcasted_iota(jnp.int32, (8, 128), 0)
    real = lax.broadcasted_iota(jnp.int32, (8, 128), 1) < 8
    exp_logits = jnp.where(expert < experts, jnp.exp(logits), 0.0)
    exp_total = jnp.sum(exp_logits, axis=0, keepdims=True)
    log_total = jnp.log(exp_total)
    prob = exp_logits / exp_total
    fraction = jnp.zeros((8, 128), F32)
    ids = own_block[:, width:].astype(F32)[:8]
    for k in range(experts):
        named = (ids[:, 0:1] == k).astype(F32) + (ids[:, 1:2] == k).astype(F32)
        count = jnp.sum(named, axis=0, keepdims=True)
        fraction = jnp.where(expert == k, count / 16.0, fraction)
    pull = BALANCE_WEIGHT * experts * fraction
    inner = jnp.sum(prob * pull, axis=0, keepdims=True)
    rows = 2.0 * Z_WEIGHT * log_total * prob + prob * (pull - inner)
    local[:8] = jnp.where(real, rows, 0.0)
    local[8:] = jnp.zeros((8, 128), F32)
    z_term = jnp.where(real[:1], log_total * log_total, 0.0)
    z_loss = jnp.sum(z_term, axis=1, keepdims=True) / 8.0
    mean_prob = jnp.sum(jnp.where(real, prob, 0.0), axis=1, keepdims=True) / 8.0
    balance = experts * jnp.sum(fraction[:, :1] * mean_prob, axis=0, keepdims=True)
    losses[0:1, 0:1] = z_loss
    losses[0:1, 1:2] = balance


def pair_rows(router):
    high, low = split_pair(router)
    return jnp.concatenate([high.astype(F32), low.astype(F32)], 0).astype(BF)


def slot_gradient(share, pieces, gate_w, up_w, router_w, weight):
    t = lax.axis_index("t")
    slots = weight.shape[0]
    notes = sum(p[slots : slots + 16, :].astype(F32) for p in pieces)
    high, low = split_pair(to_column(notes[0:1] + notes[1:2], slots) * weight[...])
    total = matmul(high, router_w[...]) + matmul(low, router_w[...])
    for step, piece in enumerate(pieces):
        rows_of = pl.ds(pl.multiple_of((t ^ step) * share, share), share)
        both = jnp.concatenate([gate_w[rows_of, :], up_w[rows_of, :]], 0)
        total += matmul(piece[:slots, : 2 * share], both)
    return total, high, low


def near_kernel(
    width, share, p0, p1, p2, p3, gate_w, up_w, router_w, weight, chosen, local, own_block,
    kept, router_part,
):
    total, high, low = slot_gradient(
        share, (p0, p1, p2, p3), gate_w, up_w, router_w, weight
    )
    slots = total.shape[0]
    kept[...] = total
    x_slot = chosen[:slots]
    router = matmul(high, x_slot, TN)[:8] + matmul(low, x_slot, TN)[:8]
    local_high, local_low = split_pair(local[...])
    router += matmul(local_high[:, :16], own_block[:, :width])[:8]
    router += matmul(local_low[:, :16], own_block[:, :width])[:8]
    router_part[...] = router


def far_kernel(
    share, p0, p1, p2, p3, gate_w, up_w, router_w, weight, chosen, router_near,
    sent, router_part,
):
    total, high, low = slot_gradient(
        share, (p0, p1, p2, p3), gate_w, up_w, router_w, weight
    )
    slots = total.shape[0]
    sent[:slots] = total.astype(BF)
    x_slot = chosen[:slots]
    router = router_near[...]
    router += matmul(high, x_slot, TN)[:8] + matmul(low, x_slot, TN)[:8]
    router_part[...] = router
    sent[slots:] = pair_rows(router)


def pair_kernel(kept, got, router_part, unpacker, out):
    half = kept.shape[0]
    pair = (kept[...] + got[:half].astype(F32)).astype(BF)
    rows = got[half:].astype(F32)
    router = (router_part[...] + rows[:8] + rows[8:]).astype(BF).astype(F32)
    router = jnp.concatenate([router, jnp.zeros_like(router)], 0).astype(BF)
    out[...] = matmul(unpacker[...], jnp.concatenate([pair, router], 0)).astype(BF)


def group_kernel(got, own, router_part, send1, send2, send3):
    total = got[0].astype(F32)
    for j in range(1, GROUPS):
        total += got[j].astype(F32)
    count = total.shape[0]
    row = lax.broadcasted_iota(jnp.int32, (8, total.shape[1]), 0)
    router = jnp.where(row < 4, pltpu.roll(total, 4, 0)[:8], 0.0)
    router_part[...] = router
    own[...] = total[:8]
    high = router.astype(BF).astype(F32)
    both = high + pltpu.roll(router - high, 4, 0)
    for step, out in enumerate((send1, send2, send3)):
        shifted = pltpu.roll(total, count - CAP * (step + 1), 0)
        out[...] = jnp.concatenate([shifted[:8], both], 0).astype(BF)


def final_kernel(
    width, experts, own, router_part, got1, got2, got3, own_block, local, router_w,
    in_grad, router_grad,
):
    e = lax.axis_index("e")
    ids = own_block[:, width:].astype(F32)[:8]
    row = lax.broadcasted_iota(jnp.int32, (8, 128), 0)
    total = own_block[8:, :width].astype(F32)
    router = router_part[...]
    for step in range(4):
        if step == 0:
            rows = own[...]
        else:
            both = (got1, got2, got3)[step - 1][...].astype(F32)
            rows = both[:8]
            router += both[8:] + pltpu.roll(both[8:], 4, 0)
        match, position, _ = spots(ids, (e ^ step).astype(F32), row)
        for k in range(CAP):
            chosen = (match & (position == k)).astype(F32)[:, 0:1]
            total += chosen * rows[k : k + 1]
    high, low = split_pair(local[...])
    rw = router_w[:16]
    total += matmul(high, rw, TN)[:8] + matmul(low, rw, TN)[:8]
    in_grad[...] = total.astype(BF)
    router_grad[...] = router[:experts]


def weight_kernel(slots, share, *refs):
    t = lax.axis_index("t")
    near, far, (gate_grad, up_grad, down_grad) = refs[:5], refs[5:10], refs[10:]
    for step in range(4):
        rows_of = pl.ds(pl.multiple_of((t ^ step) * share, share), share)
        both = down = 0.0
        for part in (near, far):
            piece, chosen = part[step], part[4]
            both += matmul(piece[:slots, : 2 * share], chosen[:slots], TN)
            down += matmul(piece[:slots, 2 * share :], chosen[slots:], TN)
        gate_grad[rows_of, :] = both[:share].astype(BF)
        up_grad[rows_of, :] = both[share:].astype(BF)
        down_grad[rows_of, :] = down.astype(BF)


def call(body, ins, outs, flops, scratch=()):
    bytes_moved = sum(v.size * v.dtype.itemsize for v in ins)
    return pl.pallas_call(
        body,
        in_specs=[VMEM] * len(ins),
        out_specs=[VMEM] * len(outs),
        out_shape=[jax.ShapeDtypeStruct(shape, dtype) for shape, dtype in outs],
        scratch_shapes=list(scratch),
        cost_estimate=pl.CostEstimate(
            flops=flops, bytes_accessed=bytes_moved, transcendentals=0
        ),
        compiler_params=pltpu.CompilerParams(vmem_limit_bytes=VMEM_LIMIT),
    )(*ins)


def exchange(value, axis, step):
    count = lax.axis_size(axis)
    return lax.ppermute(value, axis, [(k, k ^ step) for k in range(count)])


def packers(experts):
    per = experts * CAP
    pack = np.zeros((2, GROUPS, per, GROUPS, 2 * per), np.float32)
    unpack = np.zeros((GROUPS, per + 4, GROUPS * per + 16), np.float32)
    for j in range(GROUPS):
        for k in range(per):
            pack[0, j, k, j, k] = 1.0
            pack[1, j, k, j, per + k] = 1.0
            unpack[j, k, j * per + k] = 1.0
        for k in range(4):
            unpack[j, per + k, GROUPS * per + k] = 1.0
    pack = pack.reshape(2 * GROUPS * per, GROUPS * 2 * per)
    unpack = unpack.reshape(GROUPS * (per + 4), GROUPS * per + 16)
    return jnp.asarray(pack, BF), jnp.asarray(unpack, BF)


def shards(stash, out_grad, router_weight, gate_weight, up_weight, down_weight, expert_ids):
    experts, ways = lax.axis_size("e"), lax.axis_size("t")
    tokens, width = stash.shape[1], stash.shape[2]
    hidden = gate_weight.shape[0]
    share = hidden // ways
    router_tall = jnp.pad(router_weight, ((0, 128 - experts), (0, 0)))
    packer, unpacker = packers(experts)
    slots = GROUPS * experts * CAP
    height = slots + 16

    sections = experts * GROUPS * 2
    x_own = lax.ppermute(stash[0], ("e", "q", "c"), [(k, sections - 1 - k) for k in range(sections)])
    id_columns = jnp.pad(jnp.concatenate([expert_ids[0]] * 2, 0).astype(BF), ((0, 0), (0, 126)))
    own_block = jnp.concatenate([jnp.concatenate([x_own, out_grad[0]], 0), id_columns], 1)
    quad = [own_block] + [exchange(own_block, "e", step) for step in range(1, experts)]
    (chosen,) = call(
        functools.partial(pick_kernel, width),
        quad,
        [((GROUPS, 2 * experts * CAP, width + 128), BF)],
        4 * width * 64 * 40,
    )
    near = lax.all_to_all(chosen, "q", 0, 0).reshape(2 * slots, width + 128)
    far = exchange(near, "c", 1)

    halves = []
    for index, block in enumerate((near, far)):
        if index == 1:
            block, _ = lax.optimization_barrier((block, halves[0][2]))
        mine, *sends, taken = call(
            functools.partial(project_kernel, width, share, index == 0),
            [block, gate_weight, up_weight, down_weight, router_tall, packer, own_block],
            [((height, 3 * share + 128), F32)]
            + [((height, 3 * share), BF)] * 3
            + [((2 * slots, width), BF)],
            2 * slots * width * (3 * hidden + 4 * slots),
            [pltpu.VMEM((16, 3 * share), F32)],
        )
        got = [exchange(value, "t", step + 1) for step, value in enumerate(sends)]
        halves.append((mine, got, taken))
    gradients = []
    for index, (mine, got, taken) in enumerate(halves):
        packed, weight, local, losses = call(
            functools.partial(act_kernel, width, slots, share, experts, index == 0),
            [own_block, mine, *got],
            [((height, 3 * share), BF), ((slots, 128), F32), ((16, 128), F32), ((1, 2), F32)],
            slots * share * 40,
        )
        pieces = [packed] + [exchange(packed, "t", step) for step in range(1, ways)]
        gradients.append((pieces, weight, local, losses))
    _, _, local, losses = gradients[0]

    pieces, weight, _, _ = gradients[0]
    kept, router_near = call(
        functools.partial(near_kernel, width, share),
        [*pieces, gate_weight, up_weight, router_tall, weight, halves[0][2], local, own_block],
        [((slots, width), F32), ((8, width), F32)],
        2 * slots * width * 2 * hidden,
    )
    pieces, weight, _, _ = gradients[1]
    sent, router_part = call(
        functools.partial(far_kernel, share),
        [*pieces, gate_weight, up_weight, router_tall, weight, halves[1][2], router_near],
        [((height, width), BF), ((8, width), F32)],
        2 * slots * width * 2 * hidden,
    )
    got = exchange(sent, "c", 1)
    (pair,) = call(
        pair_kernel,
        [kept, got, router_part, unpacker],
        [((unpacker.shape[0], width), BF)],
        2 * slots * slots * width,
    )
    got = lax.all_to_all(pair.reshape(GROUPS, -1, width), "q", 0, 0)
    own_rows, router_part, *sends = call(
        group_kernel,
        [got],
        [((8, width), F32), ((8, width), F32)] + [((16, width), BF)] * 3,
        slots * width * 2,
    )
    gate_grad, up_grad, down_grad = call(
        functools.partial(weight_kernel, slots, share),
        [*gradients[0][0], halves[0][2], *gradients[1][0], halves[1][2]],
        [((hidden, width), BF)] * 3,
        4 * slots * width * hidden * 3,
    )
    got = [exchange(value, "e", step + 1) for step, value in enumerate(sends)]
    in_grad, router_grad = call(
        functools.partial(final_kernel, width, experts),
        [own_rows, router_part, *got, own_block, local, router_tall],
        [((tokens, width), BF), ((experts, width), F32)],
        tokens * width * 50,
    )
    return in_grad[None], gate_grad, up_grad, down_grad, router_grad, losses


def solution(mesh):
    ways = mesh.devices.shape[1]
    experts, cores = 4, 2
    fine = Mesh(mesh.devices.reshape(experts, GROUPS, cores, ways), ("e", "q", "c", "t"))
    section = ("e", "q", "c")
    in_specs = (
        P(section, None, "t"),
        P(section, None, "t"),
        P(None, "t"),
        P(section, "t"),
        P(section, "t"),
        P(section, "t"),
        P(section, None, None),
    )
    out_specs = (
        P(section, None, "t"),
        P(section, "t"),
        P(section, "t"),
        P(section, "t"),
        P(None, "t"),
        P(section, None),
    )
    return jax.shard_map(shards, mesh=fine, in_specs=in_specs, out_specs=out_specs, check_vma=False)
```

time: 180 us -> 139 us (0.77)
  waiting for transfers between devices: 64.5 us -> 21.6 us
  starting transfers between devices: 25 us -> 65.4 us
  matrix products: 23.5 us -> 0 us
  Pallas kernels: 0 us -> 14.9 us
  other arithmetic: 13 us -> 1.5 us
  local copies, waits for them, and re-layouts: 9.74 us -> 1.55 us
  blocking collectives: 40.4 us -> 32.6 us
    all_to_all x5 -> x0, waiting for transfers between devices: 63.4 us -> none  [the longest x2 25.2 us: spread_out(): lax.all_to_all(jnp.broadcast_to(value[None], (count, *value.shape)), axis...]
    ppermute x3 -> x21, starting transfers between devices: 4.81 us -> 65.4 us  [the longest x20 52.4 us: exchange(): return lax.ppermute(value, axis, [(k, k ^ step) for k in range(count)])]
    dot_general x20 -> x0, matrix products: 23.5 us -> none  [the longest x2 4.06 us: choose(): lax.dot_general(pick[half:], far, dims, preferred_element_type=F32)]
    ppermute x3 -> x21, waiting for transfers between devices: 1.11 us -> 21.6 us  [the longest x20 20.7 us: exchange(): return lax.ppermute(value, axis, [(k, k ^ step) for k in range(count)])]
    all_to_all x5 -> x0, starting transfers between devices: 20.2 us -> none  [the longest x2 7.68 us: spread_out(): lax.all_to_all(jnp.broadcast_to(value[None], (count, *value.shape)), axis...]
    all_gather x1 -> x0, blocking collectives: 19 us -> none  [shards(): whole = lax.all_gather(packed, 't', axis=0)]
    pallas_call x0 -> x11, Pallas kernels: none -> 14.9 us  [call(): pl.pallas_call(body, in_specs=[VMEM] * len(ins), out_specs=[VMEM] * len(o...]
    all_to_all x1 -> x2, blocking collectives: 21.4 us -> 32.6 us  [the longest x1 19.4 us: shards(): near = lax.all_to_all(chosen, 'q', 0, 0).reshape(2 * slots, width + 128)]
  transfers between devices with their start and end apart: 8 -> 21, of which waited for: 7 -> 10; matrix products, arithmetic and copies ran while one was open for 6% -> 1% of each run, Pallas kernels for 0% -> 9%
where the time goes in v3:
time: 139 us; the launch traced here: 138 us
  starting transfers between devices  65.4 us (47%)
  blocking collectives  32.6 us (23%)
  waiting for transfers between devices  21.6 us (16%)
  Pallas kernels  14.9 us (11%)
  local copies, waits for them, and re-layouts  1.55 us (1%)
  other arithmetic  1.5 us (1%)
    ppermute x20, starting transfers between devices, exchange(): return lax.ppermute(value, axis, [(k, k ^ step) for k in range(count)])  52.4 us
    ppermute x20, waiting for transfers between devices, exchange(): return lax.ppermute(value, axis, [(k, k ^ step) for k in range(count)])  20.7 us
    all_to_all x1, blocking collectives, shards(): near = lax.all_to_all(chosen, 'q', 0, 0).reshape(2 * slots, width + 128)  19.4 us
    pallas_call x11, Pallas kernels, call(): pl.pallas_call(body, in_specs=[VMEM] * len(ins), out_specs=[VMEM] * len(o...  14.9 us
    all_to_all x1, blocking collectives, shards(): got = lax.all_to_all(pair.reshape(GROUPS, -1, width), 'q', 0, 0)  13.2 us
    ppermute x1, starting transfers between devices, shards(): lax.ppermute(stash[0], ('e', 'q', 'c'), [(k, sections - 1 - k) for k in r...  13 us
  transfers between devices with their start and end apart: 21, of which 10 were waited for; matrix products, arithmetic and copies ran while one was open for 1% of the time, Pallas kernels for 9%

profile of v3, /device:TPU:1, one launch (start us, length us, event | category | flops | bytes accessed | tf_op | source)
XLA Modules:
  0.0 138.3 jit_solution(3114344063883795413)
XLA Ops:
  0.6 13.0 %collective-permute-start = (bf16[8,1536]{1,0:T(8,128)(2,1)}, bf16[8,1536]{1,0:T(8,128)(2,1)S(1)}, u32[]{:S(2)}, u32[]{:S(2)}) collective-permute-start(bf16[8,1536]{1,0:T(8,128)(2,1)} %bitcast.11), channel_id=1, source_target_pairs={{0,252},{4,248},{8,244},{12,240},{16,236},{20,232},{24,228},{28,22... | collective-permute-start | bytes 73736 | tf_op jit(solution)/shard_map/ppermute | solution.py:337
  14.5 0.9 collective-permute-done
  16.1 6.6 %collective-permute-start.3 = (bf16[16,1664]{1,0:T(8,128)(2,1)S(1)}, bf16[16,1664]{1,0:T(8,128)(2,1)S(1)}, u32[]{:S(2)}, u32[]{:S(2)}) collective-permute-start(bf16[16,1664]{1,0:T(8,128)(2,1)S(1)} %fusion.1.b0.own_block), channel_id=1, source_target_pairs={{0,192},{64,128},{128,64},{192,0},{1,193},{65,129},{129,65},{193,1... | collective-permute-start | bytes 159752 | tf_op jit(solution)/shard_map/ppermute | solution.py:307
  22.7 1.4 %collective-permute-start.1 = (bf16[16,1664]{1,0:T(8,128)(2,1)S(1)}, bf16[16,1664]{1,0:T(8,128)(2,1)S(1)}, u32[]{:S(2)}, u32[]{:S(2)}) collective-permute-start(bf16[16,1664]{1,0:T(8,128)(2,1)S(1)} %fusion.1.b0.own_block), channel_id=1, source_target_pairs={{0,64},{64,0},{128,192},{192,128},{1,65},{65,1},{129,193},{193,129... | collective-permute-start | bytes 159752 | tf_op jit(solution)/shard_map/ppermute | solution.py:307
  24.2 1.3 collective-permute-done.3.b3
  25.5 5.2 %collective-permute-done.2.b2 = bf16[16,1664]{1,0:T(8,128)(2,1)S(1)} collective-permute-done((bf16[16,1664]{1,0:T(8,128)(2,1)S(1)}, bf16[16,1664]{1,0:T(8,128)(2,1)S(1)}, u32[]{:S(2)}, u32[]{:S(2)}) %collective-permute-start.2) | collective-permute-done | bytes 53280 | tf_op jit(solution)/shard_map/ppermute | solution.py:307
  31.2 19.4 %all_to_all.10 = bf16[8,40,1664]{2,1,0:T(8,128)(2,1)S(1)} all-to-all(bf16[8,40,1664]{2,1,0:T(8,128)(2,1)S(1)} %shard_map.136), channel_id=1, replica_groups=mesh['e'=4,'q'=8,'c'=2,'t'=4] {'q'}, dimensions={0} | all-to-all | bytes 2129920 | tf_op jit(solution)/shard_map/all_to_all | solution.py:347
  50.6 2.5 %collective-permute-start.10 = (bf16[320,1664]{1,0:T(8,128)(2,1)S(1)}, bf16[320,1664]{1,0:T(8,128)(2,1)S(1)}, u32[]{:S(2)}, u32[]{:S(2)}) collective-permute-start(bf16[320,1664]{1,0:T(8,128)(2,1)S(1)} %bitcast.7), channel_id=1, source_target_pairs={{0,4},{4,0},{1,5},{5,1},{2,6},{6,2},{3,7},{7,3},{8,12},{12,8},{9,1... | collective-permute-start | bytes 3194888 | tf_op jit(solution)/shard_map/ppermute | solution.py:307
  53.2 1.4 %copy-done.2 = bf16[512,1536]{1,0:T(8,128)(2,1)S(1)} copy-done((bf16[512,1536]{1,0:T(8,128)(2,1)S(1)}, bf16[512,1536]{1,0:T(8,128)(2,1)}, u32[]{:S(2)}) %copy-start.2) | copy-done | bytes 1572888
  54.6 2.3 %shard_map.137 = (f32[176,512]{1,0:T(8,128)S(1)}, bf16[176,384]{1,0:T(8,128)(2,1)S(1)}, bf16[176,384]{1,0:T(8,128)(2,1)S(1)}, bf16[176,384]{1,0:T(8,128)(2,1)S(1)}, bf16[320,1536]{1,0:T(8,128)(2,1)S(1)}) custom-call(bf16[320,1664]{1,0:T(8,128)(2,1)S(1)} %bitcast.8, bf16[512,1536]{1,0:T(8,128)(2,1)S(1)} %copy-done, bf16[512,1536]{1,0:T(8,128)(2,1)S(1)} %copy-done.1, ...), custom_call_target="tpu_custom_call" | custom-call | flops 1069547520 | bytes 6434816 | tf_op jit(solution)/shard_map/pallas_call | solution.py:292
  57.0 1.2 collective-permute-start.5
  58.2 2.3 %collective-permute-start.6 = (bf16[176,384]{1,0:T(8,128)(2,1)S(1)}, bf16[176,384]{1,0:T(8,128)(2,1)S(1)}, u32[]{:S(2)}, u32[]{:S(2)}) collective-permute-start(bf16[176,384]{1,0:T(8,128)(2,1)S(1)} %get-tuple-element.40), channel_id=1, source_target_pairs={{0,3},{1,2},{2,1},{3,0},{4,7},{5,6},{6,5},{7,4},{8,11},{9,10},{10,... | collective-permute-start | bytes 405512 | tf_op jit(solution)/shard_map/ppermute | solution.py:307
  60.5 2.2 %shard_map.140 = (f32[176,512]{1,0:T(8,128)S(1)}, bf16[176,384]{1,0:T(8,128)(2,1)S(1)}, bf16[176,384]{1,0:T(8,128)(2,1)S(1)}, bf16[176,384]{1,0:T(8,128)(2,1)S(1)}, bf16[320,1536]{1,0:T(8,128)(2,1)S(1)}) custom-call(bf16[320,1664]{1,0:T(8,128)(2,1)S(1)} %collective-permute-done.10.block, bf16[512,1536]{1,0:T(8,128)(2,1)S(1)} %copy-done, ...), custom_call_target="tpu_custom_call" | custom-call | flops 1069547520 | bytes 6434816 | tf_op jit(solution)/shard_map/pallas_call | solution.py:292
  62.9 1.2 collective-permute-start.12
  64.1 2.3 %collective-permute-start.13 = (bf16[176,384]{1,0:T(8,128)(2,1)S(1)}, bf16[176,384]{1,0:T(8,128)(2,1)S(1)}, u32[]{:S(2)}, u32[]{:S(2)}) collective-permute-start(bf16[176,384]{1,0:T(8,128)(2,1)S(1)} %get-tuple-element.50), channel_id=1, source_target_pairs={{0,3},{1,2},{2,1},{3,0},{4,7},{5,6},{6,5},{7,4},{8,11},{9,10},{10,... | collective-permute-start | bytes 405512 | tf_op jit(solution)/shard_map/ppermute | solution.py:307
  66.4 2.6 %collective-permute-done.5.got2 = bf16[176,384]{1,0:T(8,128)(2,1)S(1)} collective-permute-done((bf16[176,384]{1,0:T(8,128)(2,1)S(1)}, bf16[176,384]{1,0:T(8,128)(2,1)S(1)}, u32[]{:S(2)}, u32[]{:S(2)}) %collective-permute-start.5) | collective-permute-done | bytes 135200 | tf_op jit(solution)/shard_map/ppermute | solution.py:307
  69.8 0.9 collective-permute-start.9
  70.7 12.1 %collective-permute-start.8 = (bf16[176,384]{1,0:T(8,128)(2,1)S(1)}, bf16[176,384]{1,0:T(8,128)(2,1)S(1)}, u32[]{:S(2)}, u32[]{:S(2)}) collective-permute-start(bf16[176,384]{1,0:T(8,128)(2,1)S(1)} %get-tuple-element.41.p0.refs_0_), channel_id=1, source_target_pairs={{0,2},{1,3},{2,0},{3,1},{4,6},{5,7},{6,4},{7,5},{8,10},{9,11},{10,... | collective-permute-start | bytes 405512 | tf_op jit(solution)/shard_map/ppermute | solution.py:307
  84.3 1.1 collective-permute-start.16
  85.3 4.8 %collective-permute-start.15 = (bf16[176,384]{1,0:T(8,128)(2,1)S(1)}, bf16[176,384]{1,0:T(8,128)(2,1)S(1)}, u32[]{:S(2)}, u32[]{:S(2)}) collective-permute-start(bf16[176,384]{1,0:T(8,128)(2,1)S(1)} %get-tuple-element.51.p0.refs_5_), channel_id=1, source_target_pairs={{0,2},{1,3},{2,0},{3,1},{4,6},{5,7},{6,4},{7,5},{8,10},{9,11},{10,... | collective-permute-start | bytes 405512 | tf_op jit(solution)/shard_map/ppermute | solution.py:307
  90.1 6.7 %collective-permute-start.14 = (bf16[176,384]{1,0:T(8,128)(2,1)S(1)}, bf16[176,384]{1,0:T(8,128)(2,1)S(1)}, u32[]{:S(2)}, u32[]{:S(2)}) collective-permute-start(bf16[176,384]{1,0:T(8,128)(2,1)S(1)} %get-tuple-element.51.p0.refs_5_), channel_id=1, source_target_pairs={{0,1},{1,0},{2,3},{3,2},{4,5},{5,4},{6,7},{7,6},{8,9},{9,8},{10,11... | collective-permute-start | bytes 405512 | tf_op jit(solution)/shard_map/ppermute | solution.py:307
  96.8 4.1 %collective-permute-done.8.p2.refs_2_ = bf16[176,384]{1,0:T(8,128)(2,1)S(1)} collective-permute-done((bf16[176,384]{1,0:T(8,128)(2,1)S(1)}, bf16[176,384]{1,0:T(8,128)(2,1)S(1)}, u32[]{:S(2)}, u32[]{:S(2)}) %collective-permute-start.8) | collective-permute-done | bytes 135200 | tf_op jit(solution)/shard_map/ppermute | solution.py:307
  100.9 1.2 shard_map.139
  102.2 4.6 %collective-permute-done.15.p2.refs_7_ = bf16[176,384]{1,0:T(8,128)(2,1)S(1)} collective-permute-done((bf16[176,384]{1,0:T(8,128)(2,1)S(1)}, bf16[176,384]{1,0:T(8,128)(2,1)S(1)}, u32[]{:S(2)}, u32[]{:S(2)}) %collective-permute-start.15) | collective-permute-done | bytes 135200 | tf_op jit(solution)/shard_map/ppermute | solution.py:307
  106.7 1.2 shard_map.142
  107.9 0.9 collective-permute-start.17
  108.8 1.6 %collective-permute-done.17.got = bf16[176,1536]{1,0:T(8,128)(2,1)S(1)} collective-permute-done((bf16[176,1536]{1,0:T(8,128)(2,1)S(1)}, bf16[176,1536]{1,0:T(8,128)(2,1)S(1)}, u32[]{:S(2)}, u32[]{:S(2)}) %collective-permute-start.17) | collective-permute-done | bytes 540704 | tf_op jit(solution)/shard_map/ppermute | solution.py:307
  110.7 13.2 %all_to_all.11.got = bf16[8,24,1536]{2,1,0:T(8,128)(2,1)S(1)} all-to-all(bf16[8,24,1536]{2,1,0:T(8,128)(2,1)S(1)} %bitcast.9), channel_id=1, replica_groups=mesh['e'=4,'q'=8,'c'=2,'t'=4] {'q'}, dimensions={0} | all-to-all | bytes 1179648 | tf_op jit(solution)/shard_map/all_to_all | solution.py:398
  124.6 3.4 %collective-permute-start.19 = (bf16[16,1536]{1,0:T(8,128)(2,1)S(1)}, bf16[16,1536]{1,0:T(8,128)(2,1)S(1)}, u32[]{:S(2)}, u32[]{:S(2)}) collective-permute-start(bf16[16,1536]{1,0:T(8,128)(2,1)S(1)} %get-tuple-element.60), channel_id=1, source_target_pairs={{0,128},{64,192},{128,0},{192,64},{1,129},{65,193},{129,1},{193,65... | collective-permute-start | bytes 147464 | tf_op jit(solution)/shard_map/ppermute | solution.py:307
  128.0 4.1 %collective-permute-start.20 = (bf16[16,1536]{1,0:T(8,128)(2,1)S(1)}, bf16[16,1536]{1,0:T(8,128)(2,1)S(1)}, u32[]{:S(2)}, u32[]{:S(2)}) collective-permute-start(bf16[16,1536]{1,0:T(8,128)(2,1)S(1)} %get-tuple-element.61), channel_id=1, source_target_pairs={{0,192},{64,128},{128,64},{192,0},{1,193},{65,129},{129,65},{193,1... | collective-permute-start | bytes 147464 | tf_op jit(solution)/shard_map/ppermute | solution.py:307
  132.2 4.6 %shard_map.146 = (bf16[512,1536]{1,0:T(8,128)(2,1)}, bf16[512,1536]{1,0:T(8,128)(2,1)}, bf16[512,1536]{1,0:T(8,128)(2,1)}) custom-call(bf16[176,384]{1,0:T(8,128)(2,1)S(1)} %get-tuple-element.41.p0.refs_0_, bf16[176,384]{1,0:T(8,128)(2,1)S(1)} %collective-permute-done.7.p1.refs_1_, bf16[176,384]{1,0:T(8,128)(2,1)S(1)} %collective-permute-done.8.p2.refs_2_, ...), custom_call_target="tpu_custom_call" | custom-call | flops 1509949440 | bytes 3047424 | tf_op jit(solution)/shard_map/pallas_call | solution.py:292
  137.3 1.0 shard_map.145
  (40 shorter events, 6.1 us)
Async XLA Ops:
  0.6 14.8 %collective-permute-start = (bf16[8,1536]{1,0:T(8,128)(2,1)}, bf16[8,1536]{1,0:T(8,128)(2,1)S(1)}, u32[]{:S(2)}, u32[]{:S(2)}) collective-permute-start(bf16[8,1536]{1,0:T(8,128)(2,1)} %bitcast.11), channel_id=1, source_target_pairs={{0,252},{4,248},{8,244},{12,240},{16,236},{20,232},{24,228},{28,22... | collective-permute-start | bytes 73736 | tf_op jit(solution)/shard_map/ppermute | solution.py:337
  16.1 37.0 %copy-start.5 = (bf16[4,1536]{1,0:T(4,128)(2,1)S(1)}, bf16[4,1536]{1,0:T(4,128)(2,1)}, u32[]{:S(2)}) copy-start(bf16[4,1536]{1,0:T(4,128)(2,1)} %param.11) | copy-start | bytes 36868
  16.1 9.4 %collective-permute-start.3 = (bf16[16,1664]{1,0:T(8,128)(2,1)S(1)}, bf16[16,1664]{1,0:T(8,128)(2,1)S(1)}, u32[]{:S(2)}, u32[]{:S(2)}) collective-permute-start(bf16[16,1664]{1,0:T(8,128)(2,1)S(1)} %fusion.1.b0.own_block), channel_id=1, source_target_pairs={{0,192},{64,128},{128,64},{192,0},{1,193},{65,129},{129,65},{193,1... | collective-permute-start | bytes 159752 | tf_op jit(solution)/shard_map/ppermute | solution.py:307
  22.7 8.0 %collective-permute-start.2 = (bf16[16,1664]{1,0:T(8,128)(2,1)S(1)}, bf16[16,1664]{1,0:T(8,128)(2,1)S(1)}, u32[]{:S(2)}, u32[]{:S(2)}) collective-permute-start(bf16[16,1664]{1,0:T(8,128)(2,1)S(1)} %fusion.1.b0.own_block), channel_id=1, source_target_pairs={{0,128},{64,192},{128,0},{192,64},{1,129},{65,193},{129,1},{193,65... | collective-permute-start | bytes 159752 | tf_op jit(solution)/shard_map/ppermute | solution.py:307
  22.7 8.0 %collective-permute-start.1 = (bf16[16,1664]{1,0:T(8,128)(2,1)S(1)}, bf16[16,1664]{1,0:T(8,128)(2,1)S(1)}, u32[]{:S(2)}, u32[]{:S(2)}) collective-permute-start(bf16[16,1664]{1,0:T(8,128)(2,1)S(1)} %fusion.1.b0.own_block), channel_id=1, source_target_pairs={{0,64},{64,0},{128,192},{192,128},{1,65},{65,1},{129,193},{193,129... | collective-permute-start | bytes 159752 | tf_op jit(solution)/shard_map/ppermute | solution.py:307
  30.8 22.4 %copy-start.1 = (bf16[512,1536]{1,0:T(8,128)(2,1)S(1)}, bf16[512,1536]{1,0:T(8,128)(2,1)}, u32[]{:S(2)}) copy-start(bf16[512,1536]{1,0:T(8,128)(2,1)} %up_w.7) | copy-start | bytes 4718596
  31.2 21.9 %copy-start = (bf16[512,1536]{1,0:T(8,128)(2,1)S(1)}, bf16[512,1536]{1,0:T(8,128)(2,1)}, u32[]{:S(2)}) copy-start(bf16[512,1536]{1,0:T(8,128)(2,1)} %gate_w.7) | copy-start | bytes 4718596
  31.2 21.9 %copy-start.3 = (bf16[320,320]{1,0:T(8,128)(2,1)S(1)}, bf16[320,320]{1,0:T(8,128)(2,1)}, u32[]{:S(2)}) copy-start(bf16[320,320]{1,0:T(8,128)(2,1)} %constant.7.clone.packer) | copy-start | bytes 614404
  50.6 9.9 %collective-permute-start.10 = (bf16[320,1664]{1,0:T(8,128)(2,1)S(1)}, bf16[320,1664]{1,0:T(8,128)(2,1)S(1)}, u32[]{:S(2)}, u32[]{:S(2)}) collective-permute-start(bf16[320,1664]{1,0:T(8,128)(2,1)S(1)} %bitcast.7), channel_id=1, source_target_pairs={{0,4},{4,0},{1,5},{5,1},{2,6},{6,2},{3,7},{7,3},{8,12},{12,8},{9,1... | collective-permute-start | bytes 3194888 | tf_op jit(solution)/shard_map/ppermute | solution.py:307
  53.2 1.4 %copy-start.2 = (bf16[512,1536]{1,0:T(8,128)(2,1)S(1)}, bf16[512,1536]{1,0:T(8,128)(2,1)}, u32[]{:S(2)}) copy-start(bf16[512,1536]{1,0:T(8,128)(2,1)} %down_w.3) | copy-start | bytes 4718596
  56.9 7.3 %collective-permute-start.4 = (bf16[176,384]{1,0:T(8,128)(2,1)S(1)}, bf16[176,384]{1,0:T(8,128)(2,1)S(1)}, u32[]{:S(2)}, u32[]{:S(2)}) collective-permute-start(bf16[176,384]{1,0:T(8,128)(2,1)S(1)} %get-tuple-element.38), channel_id=1, source_target_pairs={{0,1},{1,0},{2,3},{3,2},{4,5},{5,4},{6,7},{7,6},{8,9},{9,8},{10,11... | collective-permute-start | bytes 405512 | tf_op jit(solution)/shard_map/ppermute | solution.py:307
  57.0 12.1 %collective-permute-start.5 = (bf16[176,384]{1,0:T(8,128)(2,1)S(1)}, bf16[176,384]{1,0:T(8,128)(2,1)S(1)}, u32[]{:S(2)}, u32[]{:S(2)}) collective-permute-start(bf16[176,384]{1,0:T(8,128)(2,1)S(1)} %get-tuple-element.39), channel_id=1, source_target_pairs={{0,2},{1,3},{2,0},{3,1},{4,6},{5,7},{6,4},{7,5},{8,10},{9,11},{10,... | collective-permute-start | bytes 405512 | tf_op jit(solution)/shard_map/ppermute | solution.py:307
  58.2 10.9 %collective-permute-start.6 = (bf16[176,384]{1,0:T(8,128)(2,1)S(1)}, bf16[176,384]{1,0:T(8,128)(2,1)S(1)}, u32[]{:S(2)}, u32[]{:S(2)}) collective-permute-start(bf16[176,384]{1,0:T(8,128)(2,1)S(1)} %get-tuple-element.40), channel_id=1, source_target_pairs={{0,3},{1,2},{2,1},{3,0},{4,7},{5,6},{6,5},{7,4},{8,11},{9,10},{10,... | collective-permute-start | bytes 405512 | tf_op jit(solution)/shard_map/ppermute | solution.py:307
  62.8 20.1 %collective-permute-start.11 = (bf16[176,384]{1,0:T(8,128)(2,1)S(1)}, bf16[176,384]{1,0:T(8,128)(2,1)S(1)}, u32[]{:S(2)}, u32[]{:S(2)}) collective-permute-start(bf16[176,384]{1,0:T(8,128)(2,1)S(1)} %get-tuple-element.48), channel_id=1, source_target_pairs={{0,1},{1,0},{2,3},{3,2},{4,5},{5,4},{6,7},{7,6},{8,9},{9,8},{10,11... | collective-permute-start | bytes 405512 | tf_op jit(solution)/shard_map/ppermute | solution.py:307
  62.9 20.7 %collective-permute-start.12 = (bf16[176,384]{1,0:T(8,128)(2,1)S(1)}, bf16[176,384]{1,0:T(8,128)(2,1)S(1)}, u32[]{:S(2)}, u32[]{:S(2)}) collective-permute-start(bf16[176,384]{1,0:T(8,128)(2,1)S(1)} %get-tuple-element.49), channel_id=1, source_target_pairs={{0,2},{1,3},{2,0},{3,1},{4,6},{5,7},{6,4},{7,5},{8,10},{9,11},{10,... | collective-permute-start | bytes 405512 | tf_op jit(solution)/shard_map/ppermute | solution.py:307
  64.1 19.4 %collective-permute-start.13 = (bf16[176,384]{1,0:T(8,128)(2,1)S(1)}, bf16[176,384]{1,0:T(8,128)(2,1)S(1)}, u32[]{:S(2)}, u32[]{:S(2)}) collective-permute-start(bf16[176,384]{1,0:T(8,128)(2,1)S(1)} %get-tuple-element.50), channel_id=1, source_target_pairs={{0,3},{1,2},{2,1},{3,0},{4,7},{5,6},{6,5},{7,4},{8,11},{9,10},{10,... | collective-permute-start | bytes 405512 | tf_op jit(solution)/shard_map/ppermute | solution.py:307
  69.8 20.3 %collective-permute-start.9 = (bf16[176,384]{1,0:T(8,128)(2,1)S(1)}, bf16[176,384]{1,0:T(8,128)(2,1)S(1)}, u32[]{:S(2)}, u32[]{:S(2)}) collective-permute-start(bf16[176,384]{1,0:T(8,128)(2,1)S(1)} %get-tuple-element.41.p0.refs_0_), channel_id=1, source_target_pairs={{0,3},{1,2},{2,1},{3,0},{4,7},{5,6},{6,5},{7,4},{8,11},{9,10},{10,... | collective-permute-start | bytes 405512 | tf_op jit(solution)/shard_map/ppermute | solution.py:307
  70.7 30.2 %collective-permute-start.8 = (bf16[176,384]{1,0:T(8,128)(2,1)S(1)}, bf16[176,384]{1,0:T(8,128)(2,1)S(1)}, u32[]{:S(2)}, u32[]{:S(2)}) collective-permute-start(bf16[176,384]{1,0:T(8,128)(2,1)S(1)} %get-tuple-element.41.p0.refs_0_), channel_id=1, source_target_pairs={{0,2},{1,3},{2,0},{3,1},{4,6},{5,7},{6,4},{7,5},{8,10},{9,11},{10,... | collective-permute-start | bytes 405512 | tf_op jit(solution)/shard_map/ppermute | solution.py:307
  82.9 18.1 %collective-permute-start.7 = (bf16[176,384]{1,0:T(8,128)(2,1)S(1)}, bf16[176,384]{1,0:T(8,128)(2,1)S(1)}, u32[]{:S(2)}, u32[]{:S(2)}) collective-permute-start(bf16[176,384]{1,0:T(8,128)(2,1)S(1)} %get-tuple-element.41.p0.refs_0_), channel_id=1, source_target_pairs={{0,1},{1,0},{2,3},{3,2},{4,5},{5,4},{6,7},{7,6},{8,9},{9,8},{10,11... | collective-permute-start | bytes 405512 | tf_op jit(solution)/shard_map/ppermute | solution.py:307
  84.3 17.9 %collective-permute-start.16 = (bf16[176,384]{1,0:T(8,128)(2,1)S(1)}, bf16[176,384]{1,0:T(8,128)(2,1)S(1)}, u32[]{:S(2)}, u32[]{:S(2)}) collective-permute-start(bf16[176,384]{1,0:T(8,128)(2,1)S(1)} %get-tuple-element.51.p0.refs_5_), channel_id=1, source_target_pairs={{0,3},{1,2},{2,1},{3,0},{4,7},{5,6},{6,5},{7,4},{8,11},{9,10},{10,... | collective-permute-start | bytes 405512 | tf_op jit(solution)/shard_map/ppermute | solution.py:307
  85.3 21.4 %collective-permute-start.15 = (bf16[176,384]{1,0:T(8,128)(2,1)S(1)}, bf16[176,384]{1,0:T(8,128)(2,1)S(1)}, u32[]{:S(2)}, u32[]{:S(2)}) collective-permute-start(bf16[176,384]{1,0:T(8,128)(2,1)S(1)} %get-tuple-element.51.p0.refs_5_), channel_id=1, source_target_pairs={{0,2},{1,3},{2,0},{3,1},{4,6},{5,7},{6,4},{7,5},{8,10},{9,11},{10,... | collective-permute-start | bytes 405512 | tf_op jit(solution)/shard_map/ppermute | solution.py:307
  90.1 16.6 %collective-permute-start.14 = (bf16[176,384]{1,0:T(8,128)(2,1)S(1)}, bf16[176,384]{1,0:T(8,128)(2,1)S(1)}, u32[]{:S(2)}, u32[]{:S(2)}) collective-permute-start(bf16[176,384]{1,0:T(8,128)(2,1)S(1)} %get-tuple-element.51.p0.refs_5_), channel_id=1, source_target_pairs={{0,1},{1,0},{2,3},{3,2},{4,5},{5,4},{6,7},{7,6},{8,9},{9,8},{10,11... | collective-permute-start | bytes 405512 | tf_op jit(solution)/shard_map/ppermute | solution.py:307
  106.7 3.6 %copy-start.4 = (bf16[192,176]{1,0:T(8,128)(2,1)S(1)}, bf16[192,176]{1,0:T(8,128)(2,1)}, u32[]{:S(2)}) copy-start(bf16[192,176]{1,0:T(8,128)(2,1)} %constant.8.clone.unpacker) | copy-start | bytes 202756
  107.9 2.5 %collective-permute-start.17 = (bf16[176,1536]{1,0:T(8,128)(2,1)S(1)}, bf16[176,1536]{1,0:T(8,128)(2,1)S(1)}, u32[]{:S(2)}, u32[]{:S(2)}) collective-permute-start(bf16[176,1536]{1,0:T(8,128)(2,1)S(1)} %get-tuple-element.55), channel_id=1, source_target_pairs={{0,4},{4,0},{1,5},{5,1},{2,6},{6,2},{3,7},{7,3},{8,12},{12,8},{9,1... | collective-permute-start | bytes 1622024 | tf_op jit(solution)/shard_map/ppermute | solution.py:307
  124.0 12.7 %collective-permute-start.18 = (bf16[16,1536]{1,0:T(8,128)(2,1)S(1)}, bf16[16,1536]{1,0:T(8,128)(2,1)S(1)}, u32[]{:S(2)}, u32[]{:S(2)}) collective-permute-start(bf16[16,1536]{1,0:T(8,128)(2,1)S(1)} %get-tuple-element.59), channel_id=1, source_target_pairs={{0,64},{64,0},{128,192},{192,128},{1,65},{65,1},{129,193},{193,129... | collective-permute-start | bytes 147464 | tf_op jit(solution)/shard_map/ppermute | solution.py:307
  124.6 12.2 %collective-permute-start.19 = (bf16[16,1536]{1,0:T(8,128)(2,1)S(1)}, bf16[16,1536]{1,0:T(8,128)(2,1)S(1)}, u32[]{:S(2)}, u32[]{:S(2)}) collective-permute-start(bf16[16,1536]{1,0:T(8,128)(2,1)S(1)} %get-tuple-element.60), channel_id=1, source_target_pairs={{0,128},{64,192},{128,0},{192,64},{1,129},{65,193},{129,1},{193,65... | collective-permute-start | bytes 147464 | tf_op jit(solution)/shard_map/ppermute | solution.py:307
  128.0 9.3 %collective-permute-start.20 = (bf16[16,1536]{1,0:T(8,128)(2,1)S(1)}, bf16[16,1536]{1,0:T(8,128)(2,1)S(1)}, u32[]{:S(2)}, u32[]{:S(2)}) collective-permute-start(bf16[16,1536]{1,0:T(8,128)(2,1)S(1)} %get-tuple-element.61), channel_id=1, source_target_pairs={{0,192},{64,128},{128,64},{192,0},{1,193},{65,129},{129,65},{193,1... | collective-permute-start | bytes 147464 | tf_op jit(solution)/shard_map/ppermute | solution.py:307

commit v4 on v3

--- a/solution.py
+++ b/solution.py
@@ -13,7 +13,9 @@
 BALANCE_WEIGHT = 1.0
 BF = jnp.bfloat16
 F32 = jnp.float32
-GROUPS = 8
+CHIPS = 16
+SENT_ROWS = 24
+BACK_ROWS = 16
 VMEM_LIMIT = 16 * 2**20
 VMEM = pl.BlockSpec(memory_space=pltpu.VMEM)
 NT = (((1,), (1,)), ((), ()))
@@ -66,25 +68,36 @@
     return match, position - matched, first + second - expert
 
 
-def pick_kernel(width, b0, b1, b2, b3, out):
-    e_value = lax.axis_index("e").astype(F32)
-    blocks = jnp.concatenate([b0[...], b1[...], b2[...], b3[...]], 0)
-    rows = blocks.shape[0]
+def ready_kernel(x, gate_w, up_w, down_w, out):
+    out[...] = x[:, :128].astype(F32)
+
+
+def pick_kernel(width, x0, x1, g0, g1, ready, out, own_block):
+    first = lax.axis_index("h") * 2
+    parts = []
+    for x, g in ((x0, g0), (x1, g1)):
+        parts += [jnp.concatenate([x[...], g[:, width:]], 1), g[...]]
+    blocks = jnp.concatenate(parts, 0)
+    own_block[...] = blocks[:16]
+    rows, count = blocks.shape[0], out.shape[1]
     row = lax.broadcasted_iota(jnp.int32, (rows, 128), 0)
     lane = lax.broadcasted_iota(jnp.int32, (rows, 128), 1).astype(F32)
-    match, position, other = spots(blocks[:, width:].astype(F32), e_value, row)
     is_grad = (row & 8) > 0
-    slot = (row >> 4).astype(F32) * CAP + position + jnp.where(is_grad, 4.0 * CAP, 0.0)
-    slot = jnp.where(match, slot, -1.0)
-    labels = lax.broadcasted_iota(jnp.int32, (rows, 8 * CAP), 1).astype(F32)
-    pick = (jnp.broadcast_to(slot[:, 0:1], (rows, 8 * CAP)) == labels).astype(F32).astype(BF)
-    sign = (lane == e_value).astype(F32) - (lane == other).astype(F32)
-    sign = jnp.where(match & jnp.logical_not(is_grad), sign, 0.0).astype(BF)
-    values = matmul(pick, blocks[:, :width], TN).astype(BF)
-    signs = matmul(pick, sign, TN).astype(BF)
-    for j in range(GROUPS):
-        out[j, :, :width] = values
-        out[j, :, width:] = signs
+    labels = lax.broadcasted_iota(jnp.int32, (rows, count), 1).astype(F32)
+    ids = blocks[:, width:].astype(F32)
+    for side in range(2):
+        e_value = (first + side).astype(F32)
+        match, position, other = spots(ids, e_value, row)
+        slot = (row >> 4).astype(F32) * CAP + position + jnp.where(is_grad, 2.0 * CAP, 0.0)
+        slot = jnp.where(match, slot, -1.0)
+        pick = (jnp.broadcast_to(slot[:, 0:1], (rows, count)) == labels).astype(F32).astype(BF)
+        sign = (lane == e_value).astype(F32) - (lane == other).astype(F32)
+        sign = jnp.where(match & jnp.logical_not(is_grad), sign, 0.0).astype(BF)
+        values = matmul(pick, blocks[:, :width], TN).astype(BF)
+        signs = matmul(pick, sign, TN).astype(BF)
+        for j in range(side * CHIPS // 2, (side + 1) * CHIPS // 2):
+            out[j, :, :width] = values
+            out[j, :, width:] = signs
 
 
 def project_kernel(
@@ -99,14 +112,13 @@
     chosen[:slots] = x_slot
     chosen[slots:] = g_slot
     lead = matmul(x_slot, router_w[...], NT) * toward
-    notes[0:8] = row_pair(lead, 3 * share)
-    notes[8:16] = jnp.zeros((8, 3 * share), F32)
+    notes[...] = row_pair(lead, 3 * share)
     if has_own:
-        own_high, own_low = split_pair(matmul(router_w[:16], own_block[:, :width], NT))
-        notes[8:16, 0:16] = own_high[:8].astype(F32)
-        notes[8:16, 128:144] = own_low[:8].astype(F32)
+        logits = matmul(router_w[:16], own_block[:, :width], NT)[:8]
+        high = logits.astype(BF).astype(F32)
+        notes[:, 2 * share : 2 * share + 16] = high + pltpu.roll(logits - high, 4, 0)
     own[:slots, 3 * share :] = toward
-    own[slots:, 3 * share :] = jnp.zeros((16, 128), F32)
+    own[slots:, 3 * share :] = jnp.zeros((8, 128), F32)
     for step, out in enumerate((own, send1, send2, send3)):
         rows_of = pl.ds(pl.multiple_of((t ^ step) * share, share), share)
         both = jnp.concatenate([gate_w[rows_of, :], up_w[rows_of, :]], 0)
@@ -137,13 +149,14 @@
     packed[:slots, share : 2 * share] = (scaled * silu_gate).astype(BF)
     packed[:slots, 2 * share :] = (w * silu_gate * up_proj).astype(BF)
     rows = row_pair(silu_gate * up_proj * back_proj, 3 * share)
-    packed[slots:] = jnp.concatenate([rows, jnp.zeros((8, 3 * share), F32)], 0).astype(BF)
+    packed[slots:] = rows.astype(BF)
     if not has_own:
         local[...] = jnp.zeros_like(local)
         losses[...] = jnp.zeros_like(losses)
         return
 
-    logits = total[slots + 8 :, :128] + total[slots + 8 :, 128:256]
+    logits = total[slots:, 2 * share : 3 * share]
+    logits = logits + pltpu.roll(logits, 4, 0)
     expert = lax.broadcasted_iota(jnp.int32, (8, 128), 0)
     real = lax.broadcasted_iota(jnp.int32, (8, 128), 1) < 8
     exp_logits = jnp.where(expert < experts, jnp.exp(logits), 0.0)
@@ -177,7 +190,7 @@
 def slot_gradient(share, pieces, gate_w, up_w, router_w, weight):
     t = lax.axis_index("t")
     slots = weight.shape[0]
-    notes = sum(p[slots : slots + 16, :].astype(F32) for p in pieces)
+    notes = sum(p[slots:, :].astype(F32) for p in pieces)
     high, low = split_pair(to_column(notes[0:1] + notes[1:2], slots) * weight[...])
     total = matmul(high, router_w[...]) + matmul(low, router_w[...])
     for step, piece in enumerate(pieces):
@@ -229,42 +242,42 @@
     out[...] = matmul(unpacker[...], jnp.concatenate([pair, router], 0)).astype(BF)
 
 
-def group_kernel(got, own, router_part, send1, send2, send3):
-    total = got[0].astype(F32)
-    for j in range(1, GROUPS):
-        total += got[j].astype(F32)
+def group_kernel(got, own, router_part, send):
+    sides = []
+    for side in range(2):
+        first = side * CHIPS // 2
+        total = got[first].astype(F32)
+        for j in range(first + 1, first + CHIPS // 2):
+            total += got[j].astype(F32)
+        own[8 * side : 8 * side + 8] = total[:8]
+        sides.append(total)
     count = total.shape[0]
     row = lax.broadcasted_iota(jnp.int32, (8, total.shape[1]), 0)
-    router = jnp.where(row < 4, pltpu.roll(total, 4, 0)[:8], 0.0)
+    router = pltpu.roll(sides[0] + sides[1], count - 2 * CAP, 0)[:8]
+    router = jnp.where(row < 4, router, 0.0)
     router_part[...] = router
-    own[...] = total[:8]
     high = router.astype(BF).astype(F32)
     both = high + pltpu.roll(router - high, 4, 0)
-    for step, out in enumerate((send1, send2, send3)):
-        shifted = pltpu.roll(total, count - CAP * (step + 1), 0)
-        out[...] = jnp.concatenate([shifted[:8], both], 0).astype(BF)
+    moved = [pltpu.roll(total, count - CAP, 0)[:8] for total in sides]
+    send[...] = jnp.concatenate([*moved, both, jnp.zeros_like(both)], 0).astype(BF)
 
 
 def final_kernel(
-    width, experts, own, router_part, got1, got2, got3, own_block, local, router_w,
-    in_grad, router_grad,
+    width, experts, own, router_part, got, own_block, local, router_w, in_grad, router_grad
 ):
-    e = lax.axis_index("e")
+    h = lax.axis_index("h")
     ids = own_block[:, width:].astype(F32)[:8]
     row = lax.broadcasted_iota(jnp.int32, (8, 128), 0)
     total = own_block[8:, :width].astype(F32)
-    router = router_part[...]
-    for step in range(4):
-        if step == 0:
-            rows = own[...]
-        else:
-            both = (got1, got2, got3)[step - 1][...].astype(F32)
-            rows = both[:8]
-            router += both[8:] + pltpu.roll(both[8:], 4, 0)
-        match, position, _ = spots(ids, (e ^ step).astype(F32), row)
-        for k in range(CAP):
-            chosen = (match & (position == k)).astype(F32)[:, 0:1]
-            total += chosen * rows[k : k + 1]
+    other = got[...].astype(F32)
+    router = router_part[...] + other[16:24] + pltpu.roll(other[16:24], 4, 0)
+    for step, blocks in enumerate((own[...], other)):
+        for side in range(2):
+            rows = blocks[8 * side : 8 * side + 8]
+            match, position, _ = spots(ids, ((h ^ step) * 2 + side).astype(F32), row)
+            for k in range(CAP):
+                chosen = (match & (position == k)).astype(F32)[:, 0:1]
+                total += chosen * rows[k : k + 1]
     high, low = split_pair(local[...])
     rw = router_w[:16]
     total += matmul(high, rw, TN)[:8] + matmul(low, rw, TN)[:8]
@@ -307,44 +320,54 @@
     return lax.ppermute(value, axis, [(k, k ^ step) for k in range(count)])
 
 
-def packers(experts):
-    per = experts * CAP
-    pack = np.zeros((2, GROUPS, per, GROUPS, 2 * per), np.float32)
-    unpack = np.zeros((GROUPS, per + 4, GROUPS * per + 16), np.float32)
-    for j in range(GROUPS):
+def packers():
+    per, taken, sent = 2 * CAP, SENT_ROWS, BACK_ROWS
+    pack = np.zeros((2, CHIPS, per, CHIPS, taken), np.float32)
+    unpack = np.zeros((CHIPS, sent, CHIPS * per + 16), np.float32)
+    for j in range(CHIPS):
         for k in range(per):
             pack[0, j, k, j, k] = 1.0
             pack[1, j, k, j, per + k] = 1.0
             unpack[j, k, j * per + k] = 1.0
         for k in range(4):
-            unpack[j, per + k, GROUPS * per + k] = 1.0
-    pack = pack.reshape(2 * GROUPS * per, GROUPS * 2 * per)
-    unpack = unpack.reshape(GROUPS * (per + 4), GROUPS * per + 16)
+            unpack[j, per + k, CHIPS * per + k] = 1.0
+    pack = pack.reshape(2 * CHIPS * per, CHIPS * taken)
+    unpack = unpack.reshape(CHIPS * sent, CHIPS * per + 16)
     return jnp.asarray(pack, BF), jnp.asarray(unpack, BF)
 
 
 def shards(stash, out_grad, router_weight, gate_weight, up_weight, down_weight, expert_ids):
-    experts, ways = lax.axis_size("e"), lax.axis_size("t")
+    experts, ways = router_weight.shape[0], lax.axis_size("t")
     tokens, width = stash.shape[1], stash.shape[2]
     hidden = gate_weight.shape[0]
     share = hidden // ways
     router_tall = jnp.pad(router_weight, ((0, 128 - experts), (0, 0)))
-    packer, unpacker = packers(experts)
-    slots = GROUPS * experts * CAP
-    height = slots + 16
-
-    sections = experts * GROUPS * 2
-    x_own = lax.ppermute(stash[0], ("e", "q", "c"), [(k, sections - 1 - k) for k in range(sections)])
-    id_columns = jnp.pad(jnp.concatenate([expert_ids[0]] * 2, 0).astype(BF), ((0, 0), (0, 126)))
-    own_block = jnp.concatenate([jnp.concatenate([x_own, out_grad[0]], 0), id_columns], 1)
-    quad = [own_block] + [exchange(own_block, "e", step) for step in range(1, experts)]
-    (chosen,) = call(
+    packer, unpacker = packers()
+    slots = 2 * CHIPS * CAP
+    height = slots + 8
+
+    sections = 4 * CHIPS
+    id_columns = jnp.pad(expert_ids[0].astype(BF), ((0, 0), (0, 126)))
+    g_own = jnp.concatenate([out_grad[0], id_columns], 1)
+    g_other = exchange(g_own, "h", 1)
+    x_other, x_own = (
+        lax.ppermute(
+            stash[0],
+            ("h", "p", "c"),
+            [(k, (sections - 1 - k) ^ (step * sections // 2)) for k in range(sections)],
+        )
+        for step in (1, 0)
+    )
+    (ready,) = call(
+        ready_kernel, [x_other, gate_weight, up_weight, down_weight], [((tokens, 128), F32)], 1000
+    )
+    chosen, own_block = call(
         functools.partial(pick_kernel, width),
-        quad,
-        [((GROUPS, 2 * experts * CAP, width + 128), BF)],
-        4 * width * 64 * 40,
-    )
-    near = lax.all_to_all(chosen, "q", 0, 0).reshape(2 * slots, width + 128)
+        [x_own, x_other, g_own, g_other, ready],
+        [((CHIPS, SENT_ROWS, width + 128), BF), ((2 * tokens, width + 128), BF)],
+        8 * width * 32 * SENT_ROWS,
+    )
+    near = lax.all_to_all(chosen, "p", 0, 0).reshape(CHIPS * SENT_ROWS, width + 128)
     far = exchange(near, "c", 1)
 
     halves = []
@@ -358,7 +381,7 @@
             + [((height, 3 * share), BF)] * 3
             + [((2 * slots, width), BF)],
             2 * slots * width * (3 * hidden + 4 * slots),
-            [pltpu.VMEM((16, 3 * share), F32)],
+            [pltpu.VMEM((8, 3 * share), F32)],
         )
         got = [exchange(value, "t", step + 1) for step, value in enumerate(sends)]
         halves.append((mine, got, taken))
@@ -370,7 +393,8 @@
             [((height, 3 * share), BF), ((slots, 128), F32), ((16, 128), F32), ((1, 2), F32)],
             slots * share * 40,
         )
-        pieces = [packed] + [exchange(packed, "t", step) for step in range(1, ways)]
+        pieces = [packed, exchange(packed, "t", 1), exchange(packed, "t", 2)]
+        pieces.append(exchange(pieces[2], "t", 1))
         gradients.append((pieces, weight, local, losses))
     _, _, local, losses = gradients[0]
 
@@ -385,7 +409,7 @@
     sent, router_part = call(
         functools.partial(far_kernel, share),
         [*pieces, gate_weight, up_weight, router_tall, weight, halves[1][2], router_near],
-        [((height, width), BF), ((8, width), F32)],
+        [((slots + 16, width), BF), ((8, width), F32)],
         2 * slots * width * 2 * hidden,
     )
     got = exchange(sent, "c", 1)
@@ -395,11 +419,11 @@
         [((unpacker.shape[0], width), BF)],
         2 * slots * slots * width,
     )
-    got = lax.all_to_all(pair.reshape(GROUPS, -1, width), "q", 0, 0)
-    own_rows, router_part, *sends = call(
+    got = lax.all_to_all(pair.reshape(CHIPS, -1, width), "p", 0, 0)
+    own_rows, router_part, sent = call(
         group_kernel,
         [got],
-        [((8, width), F32), ((8, width), F32)] + [((16, width), BF)] * 3,
+        [((16, width), F32), ((8, width), F32), ((32, width), BF)],
         slots * width * 2,
     )
     gate_grad, up_grad, down_grad = call(
@@ -408,10 +432,9 @@
         [((hidden, width), BF)] * 3,
         4 * slots * width * hidden * 3,
     )
-    got = [exchange(value, "e", step + 1) for step, value in enumerate(sends)]
     in_grad, router_grad = call(
         functools.partial(final_kernel, width, experts),
-        [own_rows, router_part, *got, own_block, local, router_tall],
+        [own_rows, router_part, exchange(sent, "h", 1), own_block, local, router_tall],
         [((tokens, width), BF), ((experts, width), F32)],
         tokens * width * 50,
     )
@@ -420,9 +443,8 @@
 
 def solution(mesh):
     ways = mesh.devices.shape[1]
-    experts, cores = 4, 2
-    fine = Mesh(mesh.devices.reshape(experts, GROUPS, cores, ways), ("e", "q", "c", "t"))
-    section = ("e", "q", "c")
+    fine = Mesh(mesh.devices.reshape(2, CHIPS, 2, ways), ("h", "p", "c", "t"))
+    section = ("h", "p", "c")
     in_specs = (
         P(section, None, "t"),
         P(section, None, "t"),

time: 139 us -> 130 us (0.935)
  starting transfers between devices: 65.4 us -> 32.9 us
  waiting for transfers between devices: 21.6 us -> 34.9 us
  blocking collectives: 32.6 us -> 40.1 us
  local copies, waits for them, and re-layouts: 1.55 us -> 4.38 us
    ppermute x20 -> x16, starting transfers between devices: 52.4 us -> 27.1 us  [exchange(): return lax.ppermute(value, axis, [(k, k ^ step) for k in range(count)])]
    all_to_all x2, blocking collectives: 32.6 us -> 40.1 us  [the longest x1 23.6 us: shards(): lax.all_to_all(chosen, 'p', 0, 0).reshape(CHIPS * SENT_ROWS, width + 128)]
    ppermute x1 -> x2, starting transfers between devices: 13 us -> 5.77 us  [shards(): lax.ppermute(stash[0], ('h', 'p', 'c'), [(k, sections - 1 - k ^ step * se...]
    ppermute x20 -> x16, waiting for transfers between devices: 20.7 us -> 27.6 us  [exchange(): return lax.ppermute(value, axis, [(k, k ^ step) for k in range(count)])]
    ppermute x1 -> x2, waiting for transfers between devices: 0.86 us -> 7.32 us  [shards(): lax.ppermute(stash[0], ('h', 'p', 'c'), [(k, sections - 1 - k ^ step * se...]
    unnamed x12 -> x18, local copies, waits for them, and re-layouts: 1.43 us -> 4.25 us
    pallas_call x11 -> x12, Pallas kernels: 14.9 us -> 15 us  [call(): pl.pallas_call(body, in_specs=[VMEM] * len(ins), out_specs=[VMEM] * len(o...]
  transfers between devices with their start and end apart: 21 -> 18, of which waited for: 10 -> 11; matrix products, arithmetic and copies ran while one was open for 1% -> 0% of each run, Pallas kernels for 9% -> 9%
where the time goes in v4:
time: 130 us; the launch traced here: 129 us
  blocking collectives  40.1 us (31%)
  waiting for transfers between devices  34.9 us (27%)
  starting transfers between devices  32.9 us (25%)
  Pallas kernels  15 us (12%)
  local copies, waits for them, and re-layouts  4.38 us (3%)
  other arithmetic  1.43 us (1%)
    ppermute x16, waiting for transfers between devices, exchange(): return lax.ppermute(value, axis, [(k, k ^ step) for k in range(count)])  27.6 us
    ppermute x16, starting transfers between devices, exchange(): return lax.ppermute(value, axis, [(k, k ^ step) for k in range(count)])  27.1 us
    all_to_all x1, blocking collectives, shards(): lax.all_to_all(chosen, 'p', 0, 0).reshape(CHIPS * SENT_ROWS, width + 128)  23.6 us
    all_to_all x1, blocking collectives, shards(): got = lax.all_to_all(pair.reshape(CHIPS, -1, width), 'p', 0, 0)  16.5 us
    pallas_call x12, Pallas kernels, call(): pl.pallas_call(body, in_specs=[VMEM] * len(ins), out_specs=[VMEM] * len(o...  15 us
    ppermute x2, waiting for transfers between devices, shards(): lax.ppermute(stash[0], ('h', 'p', 'c'), [(k, sections - 1 - k ^ step * se...  7.32 us
    ppermute x2, starting transfers between devices, shards(): lax.ppermute(stash[0], ('h', 'p', 'c'), [(k, sections - 1 - k ^ step * se...  5.77 us
    unnamed x18, local copies, waits for them, and re-layouts  4.25 us
  transfers between devices with their start and end apart: 18, of which 11 were waited for; matrix products, arithmetic and copies ran while one was open for 0% of the time, Pallas kernels for 9%

profile of v4, /device:TPU:1, one launch (start us, length us, event | category | flops | bytes accessed | tf_op | source)
XLA Modules:
  0.0 129.5 jit_solution(17170382913815010437)
XLA Ops:
  2.2 7.7 %collective-permute-start.2 = (bf16[8,1664]{1,0:T(8,128)(2,1)S(1)}, bf16[8,1664]{1,0:T(8,128)(2,1)S(1)}, u32[]{:S(2)}, u32[]{:S(2)}) collective-permute-start(bf16[8,1664]{1,0:T(8,128)(2,1)S(1)} %fusion.1.g0), channel_id=1, source_target_pairs={{0,128},{128,0},{1,129},{129,1},{2,130},{130,2},{3,131},{131,3},{4... | collective-permute-start | bytes 79880 | tf_op jit(solution)/shard_map/ppermute | solution.py:320
  9.9 5.8 %collective-permute-start.1 = (bf16[8,1536]{1,0:T(8,128)(2,1)}, bf16[8,1536]{1,0:T(8,128)(2,1)S(1)}, u32[]{:S(2)}, u32[]{:S(2)}) collective-permute-start(bf16[8,1536]{1,0:T(8,128)(2,1)} %bitcast.11), channel_id=1, source_target_pairs={{0,124},{4,120},{8,116},{12,112},{16,108},{20,104},{24,100},{28,96... | collective-permute-start | bytes 73736 | tf_op jit(solution)/shard_map/ppermute | solution.py:354
  15.7 1.7 %collective-permute-done.1.x.x1 = bf16[8,1536]{1,0:T(8,128)(2,1)S(1)} collective-permute-done((bf16[8,1536]{1,0:T(8,128)(2,1)}, bf16[8,1536]{1,0:T(8,128)(2,1)S(1)}, u32[]{:S(2)}, u32[]{:S(2)}) %collective-permute-start.1) | collective-permute-done | bytes 24608 | tf_op jit(solution)/shard_map/ppermute | solution.py:354
  17.4 1.4 %copy-done = bf16[512,1536]{1,0:T(8,128)(2,1)S(1)} copy-done((bf16[512,1536]{1,0:T(8,128)(2,1)S(1)}, bf16[512,1536]{1,0:T(8,128)(2,1)}, u32[]{:S(2)}) %copy-start) | copy-done | bytes 1572888
  18.8 1.4 %copy-done.2 = bf16[512,1536]{1,0:T(8,128)(2,1)S(1)} copy-done((bf16[512,1536]{1,0:T(8,128)(2,1)S(1)}, bf16[512,1536]{1,0:T(8,128)(2,1)}, u32[]{:S(2)}) %copy-start.2) | copy-done | bytes 1572888
  20.2 1.4 %copy-done.4 = bf16[512,1536]{1,0:T(8,128)(2,1)S(1)} copy-done((bf16[512,1536]{1,0:T(8,128)(2,1)S(1)}, bf16[512,1536]{1,0:T(8,128)(2,1)}, u32[]{:S(2)}) %copy-start.4) | copy-done | bytes 1572888
  21.6 5.6 %collective-permute-done.x0 = bf16[8,1536]{1,0:T(8,128)(2,1)S(1)} collective-permute-done((bf16[8,1536]{1,0:T(8,128)(2,1)}, bf16[8,1536]{1,0:T(8,128)(2,1)S(1)}, u32[]{:S(2)}, u32[]{:S(2)}) %collective-permute-start) | collective-permute-done | bytes 24608 | tf_op jit(solution)/shard_map/ppermute | solution.py:354
  27.7 23.6 %all_to_all.10 = bf16[16,24,1664]{2,1,0:T(8,128)(2,1)S(1)} all-to-all(bf16[16,24,1664]{2,1,0:T(8,128)(2,1)S(1)} %get-tuple-element.38), channel_id=1, replica_groups=mesh['h'=2,'p'=16,'c'=2,'t'=4] {'p'}, dimensions={0} | all-to-all | bytes 2555904 | tf_op jit(solution)/shard_map/all_to_all | solution.py:370
  51.8 2.3 %shard_map.138 = (f32[168,512]{1,0:T(8,128)S(1)}, bf16[168,384]{1,0:T(8,128)(2,1)S(1)}, bf16[168,384]{1,0:T(8,128)(2,1)S(1)}, bf16[168,384]{1,0:T(8,128)(2,1)S(1)}, bf16[320,1536]{1,0:T(8,128)(2,1)S(1)}) custom-call(bf16[384,1664]{1,0:T(8,128)(2,1)S(1)} %bitcast.8, bf16[512,1536]{1,0:T(8,128)(2,1)S(1)} %copy-done.1, bf16[512,1536]{1,0:T(8,128)(2,1)S(1)} %copy-done.3, ...), custom_call_target="tpu_custom_call" | custom-call | flops 1069547520 | bytes 6688768 | tf_op jit(solution)/shard_map/pallas_call | solution.py:305
  54.9 1.2 collective-permute-start.4
  56.2 1.6 %collective-permute-start.5 = (bf16[168,384]{1,0:T(8,128)(2,1)S(1)}, bf16[168,384]{1,0:T(8,128)(2,1)S(1)}, u32[]{:S(2)}, u32[]{:S(2)}) collective-permute-start(bf16[168,384]{1,0:T(8,128)(2,1)S(1)} %get-tuple-element.42), channel_id=1, source_target_pairs={{0,3},{1,2},{2,1},{3,0},{4,7},{5,6},{6,5},{7,4},{8,11},{9,10},{10,... | collective-permute-start | bytes 387080 | tf_op jit(solution)/shard_map/ppermute | solution.py:320
  57.8 2.3 %shard_map.141 = (f32[168,512]{1,0:T(8,128)S(1)}, bf16[168,384]{1,0:T(8,128)(2,1)S(1)}, bf16[168,384]{1,0:T(8,128)(2,1)S(1)}, bf16[168,384]{1,0:T(8,128)(2,1)S(1)}, bf16[320,1536]{1,0:T(8,128)(2,1)S(1)}) custom-call(bf16[384,1664]{1,0:T(8,128)(2,1)S(1)} %collective-permute-done.9.block, bf16[512,1536]{1,0:T(8,128)(2,1)S(1)} %copy-done.1, ...), custom_call_target="tpu_custom_call" | custom-call | flops 1069547520 | bytes 6688768 | tf_op jit(solution)/shard_map/pallas_call | solution.py:305
  60.1 1.9 %collective-permute-start.11 = (bf16[168,384]{1,0:T(8,128)(2,1)S(1)}, bf16[168,384]{1,0:T(8,128)(2,1)S(1)}, u32[]{:S(2)}, u32[]{:S(2)}) collective-permute-start(bf16[168,384]{1,0:T(8,128)(2,1)S(1)} %get-tuple-element.51), channel_id=1, source_target_pairs={{0,2},{1,3},{2,0},{3,1},{4,6},{5,7},{6,4},{7,5},{8,10},{9,11},{10,... | collective-permute-start | bytes 387080 | tf_op jit(solution)/shard_map/ppermute | solution.py:320
  62.1 1.6 %collective-permute-start.12 = (bf16[168,384]{1,0:T(8,128)(2,1)S(1)}, bf16[168,384]{1,0:T(8,128)(2,1)S(1)}, u32[]{:S(2)}, u32[]{:S(2)}) collective-permute-start(bf16[168,384]{1,0:T(8,128)(2,1)S(1)} %get-tuple-element.52), channel_id=1, source_target_pairs={{0,3},{1,2},{2,1},{3,0},{4,7},{5,6},{6,5},{7,4},{8,11},{9,10},{10,... | collective-permute-start | bytes 387080 | tf_op jit(solution)/shard_map/ppermute | solution.py:320
  63.7 2.1 %collective-permute-done.5.got3 = bf16[168,384]{1,0:T(8,128)(2,1)S(1)} collective-permute-done((bf16[168,384]{1,0:T(8,128)(2,1)S(1)}, bf16[168,384]{1,0:T(8,128)(2,1)S(1)}, u32[]{:S(2)}, u32[]{:S(2)}) %collective-permute-start.5) | collective-permute-done | bytes 129056 | tf_op jit(solution)/shard_map/ppermute | solution.py:320
  66.5 4.5 %collective-permute-start.7 = (bf16[168,384]{1,0:T(8,128)(2,1)S(1)}, bf16[168,384]{1,0:T(8,128)(2,1)S(1)}, u32[]{:S(2)}, u32[]{:S(2)}) collective-permute-start(bf16[168,384]{1,0:T(8,128)(2,1)S(1)} %get-tuple-element.43.p0.refs_0_), channel_id=1, source_target_pairs={{0,2},{1,3},{2,0},{3,1},{4,6},{5,7},{6,4},{7,5},{8,10},{9,11},{10,... | collective-permute-start | bytes 387080 | tf_op jit(solution)/shard_map/ppermute | solution.py:320
  71.0 7.5 %collective-permute-done.11.got2 = bf16[168,384]{1,0:T(8,128)(2,1)S(1)} collective-permute-done((bf16[168,384]{1,0:T(8,128)(2,1)S(1)}, bf16[168,384]{1,0:T(8,128)(2,1)S(1)}, u32[]{:S(2)}, u32[]{:S(2)}) %collective-permute-start.11) | collective-permute-done | bytes 129056 | tf_op jit(solution)/shard_map/ppermute | solution.py:320
  79.2 3.6 %collective-permute-start.14 = (bf16[168,384]{1,0:T(8,128)(2,1)S(1)}, bf16[168,384]{1,0:T(8,128)(2,1)S(1)}, u32[]{:S(2)}, u32[]{:S(2)}) collective-permute-start(bf16[168,384]{1,0:T(8,128)(2,1)S(1)} %get-tuple-element.53.p0.refs_5_), channel_id=1, source_target_pairs={{0,2},{1,3},{2,0},{3,1},{4,6},{5,7},{6,4},{7,5},{8,10},{9,11},{10,... | collective-permute-start | bytes 387080 | tf_op jit(solution)/shard_map/ppermute | solution.py:320
  82.9 2.5 %collective-permute-done.7.p2.refs_2_ = bf16[168,384]{1,0:T(8,128)(2,1)S(1)} collective-permute-done((bf16[168,384]{1,0:T(8,128)(2,1)S(1)}, bf16[168,384]{1,0:T(8,128)(2,1)S(1)}, u32[]{:S(2)}, u32[]{:S(2)}) %collective-permute-start.7) | collective-permute-done | bytes 129056 | tf_op jit(solution)/shard_map/ppermute | solution.py:320
  85.4 1.5 %collective-permute-start.13 = (bf16[168,384]{1,0:T(8,128)(2,1)S(1)}, bf16[168,384]{1,0:T(8,128)(2,1)S(1)}, u32[]{:S(2)}, u32[]{:S(2)}) collective-permute-start(bf16[168,384]{1,0:T(8,128)(2,1)S(1)} %get-tuple-element.53.p0.refs_5_), channel_id=1, source_target_pairs={{0,1},{1,0},{2,3},{3,2},{4,5},{5,4},{6,7},{7,6},{8,9},{9,8},{10,11... | collective-permute-start | bytes 387080 | tf_op jit(solution)/shard_map/ppermute | solution.py:320
  86.9 2.7 %collective-permute-done.14.p2.refs_7_ = bf16[168,384]{1,0:T(8,128)(2,1)S(1)} collective-permute-done((bf16[168,384]{1,0:T(8,128)(2,1)S(1)}, bf16[168,384]{1,0:T(8,128)(2,1)S(1)}, u32[]{:S(2)}, u32[]{:S(2)}) %collective-permute-start.14) | collective-permute-done | bytes 129056 | tf_op jit(solution)/shard_map/ppermute | solution.py:320
  89.6 3.5 %collective-permute-done.8.p3.refs_3_ = bf16[168,384]{1,0:T(8,128)(2,1)S(1)} collective-permute-done((bf16[168,384]{1,0:T(8,128)(2,1)S(1)}, bf16[168,384]{1,0:T(8,128)(2,1)S(1)}, u32[]{:S(2)}, u32[]{:S(2)}) %collective-permute-start.8) | collective-permute-done | bytes 129056 | tf_op jit(solution)/shard_map/ppermute | solution.py:320
  93.1 1.2 shard_map.140
  94.3 1.6 %collective-permute-done.13.p1.refs_6_ = bf16[168,384]{1,0:T(8,128)(2,1)S(1)} collective-permute-done((bf16[168,384]{1,0:T(8,128)(2,1)S(1)}, bf16[168,384]{1,0:T(8,128)(2,1)S(1)}, u32[]{:S(2)}, u32[]{:S(2)}) %collective-permute-start.13) | collective-permute-done | bytes 129056 | tf_op jit(solution)/shard_map/ppermute | solution.py:320
  95.9 2.8 %collective-permute-done.15.p3.refs_8_ = bf16[168,384]{1,0:T(8,128)(2,1)S(1)} collective-permute-done((bf16[168,384]{1,0:T(8,128)(2,1)S(1)}, bf16[168,384]{1,0:T(8,128)(2,1)S(1)}, u32[]{:S(2)}, u32[]{:S(2)}) %collective-permute-start.15) | collective-permute-done | bytes 129056 | tf_op jit(solution)/shard_map/ppermute | solution.py:320
  98.6 1.2 shard_map.143
  99.8 2.0 %collective-permute-start.16 = (bf16[176,1536]{1,0:T(8,128)(2,1)S(1)}, bf16[176,1536]{1,0:T(8,128)(2,1)S(1)}, u32[]{:S(2)}, u32[]{:S(2)}) collective-permute-start(bf16[176,1536]{1,0:T(8,128)(2,1)S(1)} %get-tuple-element.57), channel_id=1, source_target_pairs={{0,4},{4,0},{1,5},{5,1},{2,6},{6,2},{3,7},{7,3},{8,12},{12,8},{9,1... | collective-permute-start | bytes 1622024 | tf_op jit(solution)/shard_map/ppermute | solution.py:320
  101.8 1.6 %collective-permute-done.16.got = bf16[176,1536]{1,0:T(8,128)(2,1)S(1)} collective-permute-done((bf16[176,1536]{1,0:T(8,128)(2,1)S(1)}, bf16[176,1536]{1,0:T(8,128)(2,1)S(1)}, u32[]{:S(2)}, u32[]{:S(2)}) %collective-permute-start.16) | collective-permute-done | bytes 540704 | tf_op jit(solution)/shard_map/ppermute | solution.py:320
  103.7 16.5 %all_to_all.11.got = bf16[16,16,1536]{2,1,0:T(8,128)(2,1)S(1)} all-to-all(bf16[16,16,1536]{2,1,0:T(8,128)(2,1)S(1)} %bitcast.9), channel_id=1, replica_groups=mesh['h'=2,'p'=16,'c'=2,'t'=4] {'p'}, dimensions={0} | all-to-all | bytes 1572864 | tf_op jit(solution)/shard_map/all_to_all | solution.py:422
  120.5 4.6 %shard_map.147 = (bf16[512,1536]{1,0:T(8,128)(2,1)}, bf16[512,1536]{1,0:T(8,128)(2,1)}, bf16[512,1536]{1,0:T(8,128)(2,1)}) custom-call(bf16[168,384]{1,0:T(8,128)(2,1)S(1)} %get-tuple-element.43.p0.refs_0_, bf16[168,384]{1,0:T(8,128)(2,1)S(1)} %collective-permute-done.6.p1.refs_1_, bf16[168,384]{1,0:T(8,128)(2,1)S(1)} %collective-permute-done.7.p2.refs_2_, ...), custom_call_target="tpu_custom_call" | custom-call | flops 1509949440 | bytes 2998272 | tf_op jit(solution)/shard_map/pallas_call | solution.py:305
  125.1 3.4 %collective-permute-done.17.got = bf16[32,1536]{1,0:T(8,128)(2,1)S(1)} collective-permute-done((bf16[32,1536]{1,0:T(8,128)(2,1)S(1)}, bf16[32,1536]{1,0:T(8,128)(2,1)S(1)}, u32[]{:S(2)}, u32[]{:S(2)}) %collective-permute-start.17) | collective-permute-done | bytes 98336 | tf_op jit(solution)/shard_map/ppermute | solution.py:320
  128.5 1.0 shard_map.146
  (40 shorter events, 5.5 us)
Async XLA Ops:
  2.2 25.1 %collective-permute-start.2 = (bf16[8,1664]{1,0:T(8,128)(2,1)S(1)}, bf16[8,1664]{1,0:T(8,128)(2,1)S(1)}, u32[]{:S(2)}, u32[]{:S(2)}) collective-permute-start(bf16[8,1664]{1,0:T(8,128)(2,1)S(1)} %fusion.1.g0), channel_id=1, source_target_pairs={{0,128},{128,0},{1,129},{129,1},{2,130},{130,2},{3,131},{131,3},{4... | collective-permute-start | bytes 79880 | tf_op jit(solution)/shard_map/ppermute | solution.py:320
  9.9 7.5 %collective-permute-start.1 = (bf16[8,1536]{1,0:T(8,128)(2,1)}, bf16[8,1536]{1,0:T(8,128)(2,1)S(1)}, u32[]{:S(2)}, u32[]{:S(2)}) collective-permute-start(bf16[8,1536]{1,0:T(8,128)(2,1)} %bitcast.11), channel_id=1, source_target_pairs={{0,124},{4,120},{8,116},{12,112},{16,108},{20,104},{24,100},{28,96... | collective-permute-start | bytes 73736 | tf_op jit(solution)/shard_map/ppermute | solution.py:354
  15.7 11.6 %collective-permute-start = (bf16[8,1536]{1,0:T(8,128)(2,1)}, bf16[8,1536]{1,0:T(8,128)(2,1)S(1)}, u32[]{:S(2)}, u32[]{:S(2)}) collective-permute-start(bf16[8,1536]{1,0:T(8,128)(2,1)} %bitcast.12), channel_id=1, source_target_pairs={{0,252},{4,248},{8,244},{12,240},{16,236},{20,232},{24,228},{28,22... | collective-permute-start | bytes 73736 | tf_op jit(solution)/shard_map/ppermute | solution.py:354
  17.4 1.4 %copy-start = (bf16[512,1536]{1,0:T(8,128)(2,1)S(1)}, bf16[512,1536]{1,0:T(8,128)(2,1)}, u32[]{:S(2)}) copy-start(bf16[512,1536]{1,0:T(8,128)(2,1)} %gate_w.9) | copy-start | bytes 4718596
  18.8 1.4 %copy-start.2 = (bf16[512,1536]{1,0:T(8,128)(2,1)S(1)}, bf16[512,1536]{1,0:T(8,128)(2,1)}, u32[]{:S(2)}) copy-start(bf16[512,1536]{1,0:T(8,128)(2,1)} %up_w.9) | copy-start | bytes 4718596
  20.2 1.4 %copy-start.4 = (bf16[512,1536]{1,0:T(8,128)(2,1)S(1)}, bf16[512,1536]{1,0:T(8,128)(2,1)}, u32[]{:S(2)}) copy-start(bf16[512,1536]{1,0:T(8,128)(2,1)} %down_w.5) | copy-start | bytes 4718596
  21.6 30.1 %copy-start.3 = (bf16[512,1536]{1,0:T(8,128)(2,1)S(1)}, bf16[512,1536]{1,0:T(8,128)(2,1)}, u32[]{:S(2)}) copy-start(bf16[512,1536]{1,0:T(8,128)(2,1)} %up_w.9) | copy-start | bytes 4718596
  21.6 30.1 %copy-start.5 = (bf16[512,1536]{1,0:T(8,128)(2,1)S(1)}, bf16[512,1536]{1,0:T(8,128)(2,1)}, u32[]{:S(2)}) copy-start(bf16[512,1536]{1,0:T(8,128)(2,1)} %down_w.5) | copy-start | bytes 4718596
  21.6 30.1 %copy-start.8 = (bf16[4,1536]{1,0:T(4,128)(2,1)S(1)}, bf16[4,1536]{1,0:T(4,128)(2,1)}, u32[]{:S(2)}) copy-start(bf16[4,1536]{1,0:T(4,128)(2,1)} %param.11) | copy-start | bytes 36868
  21.6 30.1 %copy-start.1 = (bf16[512,1536]{1,0:T(8,128)(2,1)S(1)}, bf16[512,1536]{1,0:T(8,128)(2,1)}, u32[]{:S(2)}) copy-start(bf16[512,1536]{1,0:T(8,128)(2,1)} %gate_w.9) | copy-start | bytes 4718596
  21.6 30.1 %copy-start.6 = (bf16[320,384]{1,0:T(8,128)(2,1)S(1)}, bf16[320,384]{1,0:T(8,128)(2,1)}, u32[]{:S(2)}) copy-start(bf16[320,384]{1,0:T(8,128)(2,1)} %constant.7.clone.packer) | copy-start | bytes 737284
  51.3 6.5 %collective-permute-start.9 = (bf16[384,1664]{1,0:T(8,128)(2,1)S(1)}, bf16[384,1664]{1,0:T(8,128)(2,1)S(1)}, u32[]{:S(2)}, u32[]{:S(2)}) collective-permute-start(bf16[384,1664]{1,0:T(8,128)(2,1)S(1)} %bitcast.7), channel_id=1, source_target_pairs={{0,4},{4,0},{1,5},{5,1},{2,6},{6,2},{3,7},{7,3},{8,12},{12,8},{9,1... | collective-permute-start | bytes 3833864 | tf_op jit(solution)/shard_map/ppermute | solution.py:320
  54.1 7.9 %collective-permute-start.3 = (bf16[168,384]{1,0:T(8,128)(2,1)S(1)}, bf16[168,384]{1,0:T(8,128)(2,1)S(1)}, u32[]{:S(2)}, u32[]{:S(2)}) collective-permute-start(bf16[168,384]{1,0:T(8,128)(2,1)S(1)} %get-tuple-element.40), channel_id=1, source_target_pairs={{0,1},{1,0},{2,3},{3,2},{4,5},{5,4},{6,7},{7,6},{8,9},{9,8},{10,11... | collective-permute-start | bytes 387080 | tf_op jit(solution)/shard_map/ppermute | solution.py:320
  54.9 8.7 %collective-permute-start.4 = (bf16[168,384]{1,0:T(8,128)(2,1)S(1)}, bf16[168,384]{1,0:T(8,128)(2,1)S(1)}, u32[]{:S(2)}, u32[]{:S(2)}) collective-permute-start(bf16[168,384]{1,0:T(8,128)(2,1)S(1)} %get-tuple-element.41), channel_id=1, source_target_pairs={{0,2},{1,3},{2,0},{3,1},{4,6},{5,7},{6,4},{7,5},{8,10},{9,11},{10,... | collective-permute-start | bytes 387080 | tf_op jit(solution)/shard_map/ppermute | solution.py:320
  56.2 9.6 %collective-permute-start.5 = (bf16[168,384]{1,0:T(8,128)(2,1)S(1)}, bf16[168,384]{1,0:T(8,128)(2,1)S(1)}, u32[]{:S(2)}, u32[]{:S(2)}) collective-permute-start(bf16[168,384]{1,0:T(8,128)(2,1)S(1)} %get-tuple-element.42), channel_id=1, source_target_pairs={{0,3},{1,2},{2,1},{3,0},{4,7},{5,6},{6,5},{7,4},{8,11},{9,10},{10,... | collective-permute-start | bytes 387080 | tf_op jit(solution)/shard_map/ppermute | solution.py:320
  60.0 11.0 %collective-permute-start.10 = (bf16[168,384]{1,0:T(8,128)(2,1)S(1)}, bf16[168,384]{1,0:T(8,128)(2,1)S(1)}, u32[]{:S(2)}, u32[]{:S(2)}) collective-permute-start(bf16[168,384]{1,0:T(8,128)(2,1)S(1)} %get-tuple-element.50), channel_id=1, source_target_pairs={{0,1},{1,0},{2,3},{3,2},{4,5},{5,4},{6,7},{7,6},{8,9},{9,8},{10,11... | collective-permute-start | bytes 387080 | tf_op jit(solution)/shard_map/ppermute | solution.py:320
  60.1 18.4 %collective-permute-start.11 = (bf16[168,384]{1,0:T(8,128)(2,1)S(1)}, bf16[168,384]{1,0:T(8,128)(2,1)S(1)}, u32[]{:S(2)}, u32[]{:S(2)}) collective-permute-start(bf16[168,384]{1,0:T(8,128)(2,1)S(1)} %get-tuple-element.51), channel_id=1, source_target_pairs={{0,2},{1,3},{2,0},{3,1},{4,6},{5,7},{6,4},{7,5},{8,10},{9,11},{10,... | collective-permute-start | bytes 387080 | tf_op jit(solution)/shard_map/ppermute | solution.py:320
  62.1 16.4 %collective-permute-start.12 = (bf16[168,384]{1,0:T(8,128)(2,1)S(1)}, bf16[168,384]{1,0:T(8,128)(2,1)S(1)}, u32[]{:S(2)}, u32[]{:S(2)}) collective-permute-start(bf16[168,384]{1,0:T(8,128)(2,1)S(1)} %get-tuple-element.52), channel_id=1, source_target_pairs={{0,3},{1,2},{2,1},{3,0},{4,7},{5,6},{6,5},{7,4},{8,11},{9,10},{10,... | collective-permute-start | bytes 387080 | tf_op jit(solution)/shard_map/ppermute | solution.py:320
  66.5 18.9 %collective-permute-start.7 = (bf16[168,384]{1,0:T(8,128)(2,1)S(1)}, bf16[168,384]{1,0:T(8,128)(2,1)S(1)}, u32[]{:S(2)}, u32[]{:S(2)}) collective-permute-start(bf16[168,384]{1,0:T(8,128)(2,1)S(1)} %get-tuple-element.43.p0.refs_0_), channel_id=1, source_target_pairs={{0,2},{1,3},{2,0},{3,1},{4,6},{5,7},{6,4},{7,5},{8,10},{9,11},{10,... | collective-permute-start | bytes 387080 | tf_op jit(solution)/shard_map/ppermute | solution.py:320
  79.2 10.3 %collective-permute-start.14 = (bf16[168,384]{1,0:T(8,128)(2,1)S(1)}, bf16[168,384]{1,0:T(8,128)(2,1)S(1)}, u32[]{:S(2)}, u32[]{:S(2)}) collective-permute-start(bf16[168,384]{1,0:T(8,128)(2,1)S(1)} %get-tuple-element.53.p0.refs_5_), channel_id=1, source_target_pairs={{0,2},{1,3},{2,0},{3,1},{4,6},{5,7},{6,4},{7,5},{8,10},{9,11},{10,... | collective-permute-start | bytes 387080 | tf_op jit(solution)/shard_map/ppermute | solution.py:320
  82.9 6.7 %collective-permute-start.6 = (bf16[168,384]{1,0:T(8,128)(2,1)S(1)}, bf16[168,384]{1,0:T(8,128)(2,1)S(1)}, u32[]{:S(2)}, u32[]{:S(2)}) collective-permute-start(bf16[168,384]{1,0:T(8,128)(2,1)S(1)} %get-tuple-element.43.p0.refs_0_), channel_id=1, source_target_pairs={{0,1},{1,0},{2,3},{3,2},{4,5},{5,4},{6,7},{7,6},{8,9},{9,8},{10,11... | collective-permute-start | bytes 387080 | tf_op jit(solution)/shard_map/ppermute | solution.py:320
  85.4 7.7 %collective-permute-start.8 = (bf16[168,384]{1,0:T(8,128)(2,1)S(1)}, bf16[168,384]{1,0:T(8,128)(2,1)S(1)}, u32[]{:S(2)}, u32[]{:S(2)}) collective-permute-start(bf16[168,384]{1,0:T(8,128)(2,1)S(1)} %collective-permute-done.7.p2.refs_2_), channel_id=1, source_target_pairs={{0,1},{1,0},{2,3},{3,2},{4,5},{5,4},{6,7},{7,6},{8,9},{9,8},{10,11... | collective-permute-start | bytes 387080 | tf_op jit(solution)/shard_map/ppermute | solution.py:320
  85.4 10.4 %collective-permute-start.13 = (bf16[168,384]{1,0:T(8,128)(2,1)S(1)}, bf16[168,384]{1,0:T(8,128)(2,1)S(1)}, u32[]{:S(2)}, u32[]{:S(2)}) collective-permute-start(bf16[168,384]{1,0:T(8,128)(2,1)S(1)} %get-tuple-element.53.p0.refs_5_), channel_id=1, source_target_pairs={{0,1},{1,0},{2,3},{3,2},{4,5},{5,4},{6,7},{7,6},{8,9},{9,8},{10,11... | collective-permute-start | bytes 387080 | tf_op jit(solution)/shard_map/ppermute | solution.py:320
  89.6 9.1 %collective-permute-start.15 = (bf16[168,384]{1,0:T(8,128)(2,1)S(1)}, bf16[168,384]{1,0:T(8,128)(2,1)S(1)}, u32[]{:S(2)}, u32[]{:S(2)}) collective-permute-start(bf16[168,384]{1,0:T(8,128)(2,1)S(1)} %collective-permute-done.14.p2.refs_7_), channel_id=1, source_target_pairs={{0,1},{1,0},{2,3},{3,2},{4,5},{5,4},{6,7},{7,6},{8,9},{9,8},{10,11... | collective-permute-start | bytes 387080 | tf_op jit(solution)/shard_map/ppermute | solution.py:320
  98.6 4.7 %copy-start.7 = (bf16[256,176]{1,0:T(8,128)(2,1)S(1)}, bf16[256,176]{1,0:T(8,128)(2,1)}, u32[]{:S(2)}) copy-start(bf16[256,176]{1,0:T(8,128)(2,1)} %constant.8.clone.unpacker) | copy-start | bytes 270340
  99.8 3.5 %collective-permute-start.16 = (bf16[176,1536]{1,0:T(8,128)(2,1)S(1)}, bf16[176,1536]{1,0:T(8,128)(2,1)S(1)}, u32[]{:S(2)}, u32[]{:S(2)}) collective-permute-start(bf16[176,1536]{1,0:T(8,128)(2,1)S(1)} %get-tuple-element.57), channel_id=1, source_target_pairs={{0,4},{4,0},{1,5},{5,1},{2,6},{6,2},{3,7},{7,3},{8,12},{12,8},{9,1... | collective-permute-start | bytes 1622024 | tf_op jit(solution)/shard_map/ppermute | solution.py:320
  120.4 8.1 %collective-permute-start.17 = (bf16[32,1536]{1,0:T(8,128)(2,1)S(1)}, bf16[32,1536]{1,0:T(8,128)(2,1)S(1)}, u32[]{:S(2)}, u32[]{:S(2)}) collective-permute-start(bf16[32,1536]{1,0:T(8,128)(2,1)S(1)} %get-tuple-element.61), channel_id=1, source_target_pairs={{0,128},{128,0},{1,129},{129,1},{2,130},{130,2},{3,131},{131,3},{4... | collective-permute-start | bytes 294920 | tf_op jit(solution)/shard_map/ppermute | solution.py:320

commit v5 on v4

--- a/solution.py
+++ b/solution.py
@@ -14,8 +14,8 @@
 BF = jnp.bfloat16
 F32 = jnp.float32
 CHIPS = 16
-SENT_ROWS = 24
-BACK_ROWS = 16
+SENT_ROWS = 16
+BACK_ROWS = 8
 VMEM_LIMIT = 16 * 2**20
 VMEM = pl.BlockSpec(memory_space=pltpu.VMEM)
 NT = (((1,), (1,)), ((), ()))
@@ -72,32 +72,41 @@
     out[...] = x[:, :128].astype(F32)
 
 
-def pick_kernel(width, x0, x1, g0, g1, ready, out, own_block):
+def pick_kernel(width, mine, got, ready, out, own_block):
     first = lax.axis_index("h") * 2
     parts = []
-    for x, g in ((x0, g0), (x1, g1)):
-        parts += [jnp.concatenate([x[...], g[:, width:]], 1), g[...]]
+    for x, g in ((got, mine), (mine, got)):
+        parts += [jnp.concatenate([x[:8, :width], g[8:, width:]], 1), g[8:, :]]
     blocks = jnp.concatenate(parts, 0)
     own_block[...] = blocks[:16]
-    rows, count = blocks.shape[0], out.shape[1]
+    rows, quarter = blocks.shape[0], width // 4
     row = lax.broadcasted_iota(jnp.int32, (rows, 128), 0)
     lane = lax.broadcasted_iota(jnp.int32, (rows, 128), 1).astype(F32)
-    is_grad = (row & 8) > 0
-    labels = lax.broadcasted_iota(jnp.int32, (rows, count), 1).astype(F32)
+    grad = ((row & 8) >> 3).astype(F32)
+    labels = lax.broadcasted_iota(jnp.int32, (rows, SENT_ROWS), 1).astype(F32)
     ids = blocks[:, width:].astype(F32)
+
+    def pick(label):
+        wide = jnp.broadcast_to(label[:, 0:1], (rows, SENT_ROWS))
+        return (wide == labels).astype(F32).astype(BF)
+
     for side in range(2):
         e_value = (first + side).astype(F32)
         match, position, other = spots(ids, e_value, row)
-        slot = (row >> 4).astype(F32) * CAP + position + jnp.where(is_grad, 2.0 * CAP, 0.0)
-        slot = jnp.where(match, slot, -1.0)
-        pick = (jnp.broadcast_to(slot[:, 0:1], (rows, count)) == labels).astype(F32).astype(BF)
+        slot = (row >> 4).astype(F32) * CAP + position
+        slot = jnp.where(match, slot, -100.0)
+        main = jnp.where(slot < 8, slot + 8.0 * grad, -100.0)
+        rest = jnp.where(slot >= 8, (slot - 8.0 + 2.0 * grad) * 4.0, -100.0)
         sign = (lane == e_value).astype(F32) - (lane == other).astype(F32)
-        sign = jnp.where(match & jnp.logical_not(is_grad), sign, 0.0).astype(BF)
-        values = matmul(pick, blocks[:, :width], TN).astype(BF)
-        signs = matmul(pick, sign, TN).astype(BF)
+        values = matmul(pick(main), blocks[:, :width], TN).astype(BF)
+        extra = sum(
+            matmul(pick(rest + m), blocks[:, m * quarter : (m + 1) * quarter], TN) for m in range(4)
+        ).astype(BF)
+        signs = matmul(pick(jnp.where(grad > 0, -100.0, slot)), sign.astype(BF), TN).astype(BF)
         for j in range(side * CHIPS // 2, (side + 1) * CHIPS // 2):
             out[j, :, :width] = values
-            out[j, :, width:] = signs
+            out[j, :, width : width + quarter] = extra
+            out[j, :, width + quarter :] = signs
 
 
 def project_kernel(
@@ -105,10 +114,19 @@
     own, send1, send2, send3, chosen, notes,
 ):
     t = lax.axis_index("t")
-    slots = packer.shape[0] // 2
-    taken = matmul(packer[:slots, :], block[...])
-    x_slot, toward = taken[:, :width].astype(BF), taken[:, width:]
-    g_slot = matmul(packer[slots:, :], block[:, :width]).astype(BF)
+    slots, quarter = packer.shape[0] // 11, width // 4
+    extra = block[:, width : width + quarter]
+
+    def unpack(first):
+        parts = []
+        for m in range(4):
+            taken = matmul(packer[first * slots : (first + 1) * slots, :], block[:, m * quarter : (m + 1) * quarter])
+            rows = slice((first + 1 + m) * slots, (first + 2 + m) * slots)
+            parts.append((taken + matmul(packer[rows, :], extra)).astype(BF))
+        return jnp.concatenate(parts, 1)
+
+    x_slot, g_slot = unpack(0), unpack(5)
+    toward = matmul(packer[10 * slots :, :], block[:, width + quarter :])
     chosen[:slots] = x_slot
     chosen[slots:] = g_slot
     lead = matmul(x_slot, router_w[...], NT) * toward
@@ -233,33 +251,49 @@
     sent[slots:] = pair_rows(router)
 
 
-def pair_kernel(kept, got, router_part, unpacker, out):
-    half = kept.shape[0]
+def pair_kernel(width, kept, got, router_part, unpacker, out):
+    half, quarter, count = kept.shape[0], width // 4, out.shape[0]
     pair = (kept[...] + got[:half].astype(F32)).astype(BF)
     rows = got[half:].astype(F32)
     router = (router_part[...] + rows[:8] + rows[8:]).astype(BF).astype(F32)
     router = jnp.concatenate([router, jnp.zeros_like(router)], 0).astype(BF)
-    out[...] = matmul(unpacker[...], jnp.concatenate([pair, router], 0)).astype(BF)
-
-
-def group_kernel(got, own, router_part, send):
+    pair = jnp.concatenate([pair, router], 0)
+    out[:, :width] = matmul(unpacker[:count, :], pair).astype(BF)
+    for c in range(3):
+        value = 0.0
+        for m in range(4):
+            first = (1 + 4 * c + m) * count
+            value += matmul(
+                unpacker[first : first + count, :], pair[:, m * quarter : (m + 1) * quarter]
+            )
+        out[:, width + c * quarter : width + (c + 1) * quarter] = value.astype(BF)
+
+
+def group_kernel(width, got, own, router_part, send):
+    quarter = width // 4
+    row = lax.broadcasted_iota(jnp.int32, (8, quarter), 0)
     sides = []
     for side in range(2):
         first = side * CHIPS // 2
         total = got[first].astype(F32)
         for j in range(first + 1, first + CHIPS // 2):
             total += got[j].astype(F32)
-        own[8 * side : 8 * side + 8] = total[:8]
-        sides.append(total)
-    count = total.shape[0]
-    row = lax.broadcasted_iota(jnp.int32, (8, total.shape[1]), 0)
-    router = pltpu.roll(sides[0] + sides[1], count - 2 * CAP, 0)[:8]
-    router = jnp.where(row < 4, router, 0.0)
-    router_part[...] = router
-    high = router.astype(BF).astype(F32)
-    both = high + pltpu.roll(router - high, 4, 0)
-    moved = [pltpu.roll(total, count - CAP, 0)[:8] for total in sides]
-    send[...] = jnp.concatenate([*moved, both, jnp.zeros_like(both)], 0).astype(BF)
+        more = []
+        for m in range(4):
+            value = jnp.zeros((8, quarter), F32)
+            for i in range(6):
+                r, c = (4 * i + m) // 3, (4 * i + m) % 3
+                piece = total[r : r + 1, width + c * quarter : width + (c + 1) * quarter]
+                value = jnp.where(row == i, jnp.broadcast_to(piece, (8, quarter)), value)
+            more.append(value)
+        own[8 * side : 8 * side + 8] = total[:, :width]
+        sides.append(jnp.concatenate([total[:, :width], jnp.concatenate(more, 1)], 0))
+    near, far = sides
+    row = lax.broadcasted_iota(jnp.int32, near.shape, 0)
+    router_part[...] = pltpu.roll(near + far, 16 - 2 * CAP, 0)[:8]
+    send[...] = jnp.where(
+        row < CAP, pltpu.roll(near, 16 - CAP, 0), jnp.where(row < 2 * CAP, far, near + far)
+    ).astype(BF)
 
 
 def final_kernel(
@@ -270,14 +304,17 @@
     row = lax.broadcasted_iota(jnp.int32, (8, 128), 0)
     total = own_block[8:, :width].astype(F32)
     other = got[...].astype(F32)
-    router = router_part[...] + other[16:24] + pltpu.roll(other[16:24], 4, 0)
-    for step, blocks in enumerate((own[...], other)):
+    router = router_part[...] + pltpu.roll(other, 16 - 2 * CAP, 0)[:8]
+    for step in range(2):
         for side in range(2):
-            rows = blocks[8 * side : 8 * side + 8]
             match, position, _ = spots(ids, ((h ^ step) * 2 + side).astype(F32), row)
             for k in range(CAP):
                 chosen = (match & (position == k)).astype(F32)[:, 0:1]
-                total += chosen * rows[k : k + 1]
+                if step == 0:
+                    value = own[8 * side + k : 8 * side + k + 1, :]
+                else:
+                    value = other[CAP * side + k : CAP * side + k + 1]
+                total += chosen * value
     high, low = split_pair(local[...])
     rw = router_w[:16]
     total += matmul(high, rw, TN)[:8] + matmul(low, rw, TN)[:8]
@@ -287,7 +324,8 @@
 
 def weight_kernel(slots, share, *refs):
     t = lax.axis_index("t")
-    near, far, (gate_grad, up_grad, down_grad) = refs[:5], refs[5:10], refs[10:]
+    near, far, outs, (held, sems) = refs[:5], refs[5:10], refs[10:13], refs[13:]
+    copies = []
     for step in range(4):
         rows_of = pl.ds(pl.multiple_of((t ^ step) * share, share), share)
         both = down = 0.0
@@ -295,17 +333,21 @@
             piece, chosen = part[step], part[4]
             both += matmul(piece[:slots, : 2 * share], chosen[:slots], TN)
             down += matmul(piece[:slots, 2 * share :], chosen[slots:], TN)
-        gate_grad[rows_of, :] = both[:share].astype(BF)
-        up_grad[rows_of, :] = both[share:].astype(BF)
-        down_grad[rows_of, :] = down.astype(BF)
-
-
-def call(body, ins, outs, flops, scratch=()):
+        for k, value in enumerate((both[:share], both[share:], down)):
+            held[k, step] = value.astype(BF)
+            copy = pltpu.make_async_copy(held.at[k, step], outs[k].at[rows_of, :], sems.at[k, step])
+            copy.start()
+            copies.append(copy)
+    for copy in copies:
+        copy.wait()
+
+
+def call(body, ins, outs, flops, scratch=(), out_spec=VMEM):
     bytes_moved = sum(v.size * v.dtype.itemsize for v in ins)
     return pl.pallas_call(
         body,
         in_specs=[VMEM] * len(ins),
-        out_specs=[VMEM] * len(outs),
+        out_specs=[out_spec] * len(outs),
         out_shape=[jax.ShapeDtypeStruct(shape, dtype) for shape, dtype in outs],
         scratch_shapes=list(scratch),
         cost_estimate=pl.CostEstimate(
@@ -322,17 +364,26 @@
 
 def packers():
     per, taken, sent = 2 * CAP, SENT_ROWS, BACK_ROWS
-    pack = np.zeros((2, CHIPS, per, CHIPS, taken), np.float32)
-    unpack = np.zeros((CHIPS, sent, CHIPS * per + 16), np.float32)
+    pack = np.zeros((11, CHIPS, per, CHIPS, taken), np.float32)
+    unpack = np.zeros((13, CHIPS, sent, CHIPS * per + 16), np.float32)
     for j in range(CHIPS):
         for k in range(per):
-            pack[0, j, k, j, k] = 1.0
-            pack[1, j, k, j, per + k] = 1.0
-            unpack[j, k, j * per + k] = 1.0
-        for k in range(4):
-            unpack[j, per + k, CHIPS * per + k] = 1.0
-    pack = pack.reshape(2 * CHIPS * per, CHIPS * taken)
-    unpack = unpack.reshape(CHIPS * sent, CHIPS * per + 16)
+            pack[10, j, k, j, k] = 1.0
+            if k < 8:
+                unpack[0, j, k, j * per + k] = 1.0
+            for kind in range(2):
+                if k < 8:
+                    pack[5 * kind, j, k, j, 8 * kind + k] = 1.0
+                else:
+                    for m in range(4):
+                        pack[5 * kind + 1 + m, j, k, j, 4 * (k - 8 + 2 * kind) + m] = 1.0
+        for i in range(6):
+            source = j * per + 8 + i if i < 2 else CHIPS * per + i - 2
+            for m in range(4):
+                r, c = (4 * i + m) // 3, (4 * i + m) % 3
+                unpack[1 + 4 * c + m, j, r, source] = 1.0
+    pack = pack.reshape(11 * CHIPS * per, CHIPS * taken)
+    unpack = unpack.reshape(13 * CHIPS * sent, CHIPS * per + 16)
     return jnp.asarray(pack, BF), jnp.asarray(unpack, BF)
 
 
@@ -346,28 +397,20 @@
     slots = 2 * CHIPS * CAP
     height = slots + 8
 
-    sections = 4 * CHIPS
-    id_columns = jnp.pad(expert_ids[0].astype(BF), ((0, 0), (0, 126)))
-    g_own = jnp.concatenate([out_grad[0], id_columns], 1)
-    g_other = exchange(g_own, "h", 1)
-    x_other, x_own = (
-        lax.ppermute(
-            stash[0],
-            ("h", "p", "c"),
-            [(k, (sections - 1 - k) ^ (step * sections // 2)) for k in range(sections)],
-        )
-        for step in (1, 0)
-    )
+    places = 2 * CHIPS
+    x_other = lax.ppermute(stash[0], ("p", "c"), [(k, places - 1 - k) for k in range(places)])
+    id_columns = jnp.pad(jnp.concatenate([expert_ids[0]] * 2, 0).astype(BF), ((0, 0), (0, 126)))
+    block = jnp.concatenate([jnp.concatenate([x_other, out_grad[0]], 0), id_columns], 1)
     (ready,) = call(
         ready_kernel, [x_other, gate_weight, up_weight, down_weight], [((tokens, 128), F32)], 1000
     )
     chosen, own_block = call(
         functools.partial(pick_kernel, width),
-        [x_own, x_other, g_own, g_other, ready],
-        [((CHIPS, SENT_ROWS, width + 128), BF), ((2 * tokens, width + 128), BF)],
+        [block, exchange(block, "h", 1), ready],
+        [((CHIPS, SENT_ROWS, width + width // 4 + 128), BF), ((2 * tokens, width + 128), BF)],
         8 * width * 32 * SENT_ROWS,
     )
-    near = lax.all_to_all(chosen, "p", 0, 0).reshape(CHIPS * SENT_ROWS, width + 128)
+    near = lax.all_to_all(chosen, "p", 0, 0).reshape(CHIPS * SENT_ROWS, -1)
     far = exchange(near, "c", 1)
 
     halves = []
@@ -383,7 +426,7 @@
             2 * slots * width * (3 * hidden + 4 * slots),
             [pltpu.VMEM((8, 3 * share), F32)],
         )
-        got = [exchange(value, "t", step + 1) for step, value in enumerate(sends)]
+        got = [exchange(sends[step - 1], "t", step) for step in (3, 2, 1)]
         halves.append((mine, got, taken))
     gradients = []
     for index, (mine, got, taken) in enumerate(halves):
@@ -414,16 +457,16 @@
     )
     got = exchange(sent, "c", 1)
     (pair,) = call(
-        pair_kernel,
+        functools.partial(pair_kernel, width),
         [kept, got, router_part, unpacker],
-        [((unpacker.shape[0], width), BF)],
+        [((CHIPS * BACK_ROWS, width + 3 * (width // 4)), BF)],
         2 * slots * slots * width,
     )
-    got = lax.all_to_all(pair.reshape(CHIPS, -1, width), "p", 0, 0)
+    got = lax.all_to_all(pair.reshape(CHIPS, BACK_ROWS, -1), "p", 0, 0)
     own_rows, router_part, sent = call(
-        group_kernel,
+        functools.partial(group_kernel, width),
         [got],
-        [((16, width), F32), ((8, width), F32), ((32, width), BF)],
+        [((16, width), F32), ((8, width), F32), ((16, width), BF)],
         slots * width * 2,
     )
     gate_grad, up_grad, down_grad = call(
@@ -431,6 +474,8 @@
         [*gradients[0][0], halves[0][2], *gradients[1][0], halves[1][2]],
         [((hidden, width), BF)] * 3,
         4 * slots * width * hidden * 3,
+        [pltpu.VMEM((3, ways, share, width), BF), pltpu.SemaphoreType.DMA((3, ways))],
+        pl.BlockSpec(memory_space=pl.ANY),
     )
     in_grad, router_grad = call(
         functools.partial(final_kernel, width, experts),

time: 130 us -> 122 us (0.938)
  waiting for transfers between devices: 34.9 us -> 30.4 us
  blocking collectives: 40.1 us -> 38 us
    ppermute x2 -> x1, waiting for transfers between devices: 7.32 us -> 0.86 us  [shards(): lax.ppermute(stash[0], ('p', 'c'), [(k, places - 1 - k) for k in range(pl...]
    all_to_all x2, blocking collectives: 40.1 us -> 38 us  [the longest x1 22.6 us: shards(): near = lax.all_to_all(chosen, 'p', 0, 0).reshape(CHIPS * SENT_ROWS, -1)]
    ppermute x16, waiting for transfers between devices: 27.6 us -> 29.6 us  [exchange(): return lax.ppermute(value, axis, [(k, k ^ step) for k in range(count)])]
    ppermute x16, starting transfers between devices: 27.1 us -> 25.7 us  [exchange(): return lax.ppermute(value, axis, [(k, k ^ step) for k in range(count)])]
    ppermute x2 -> x1, starting transfers between devices: 5.77 us -> 6.41 us  [shards(): lax.ppermute(stash[0], ('p', 'c'), [(k, places - 1 - k) for k in range(pl...]
  transfers between devices with their start and end apart: 18 -> 17, of which waited for: 11 -> 10; matrix products, arithmetic and copies ran while one was open for 0% -> 1% of each run, Pallas kernels for 9% -> 9%
where the time goes in v5:
time: 122 us
  blocking collectives  38 us (31%)
  starting transfers between devices  32.1 us (26%)
  waiting for transfers between devices  30.4 us (25%)
  Pallas kernels  14.6 us (12%)
  local copies, waits for them, and re-layouts  4.38 us (4%)
  other arithmetic  1.5 us (1%)
    ppermute x16, waiting for transfers between devices, exchange(): return lax.ppermute(value, axis, [(k, k ^ step) for k in range(count)])  29.6 us
    ppermute x16, starting transfers between devices, exchange(): return lax.ppermute(value, axis, [(k, k ^ step) for k in range(count)])  25.7 us
    all_to_all x1, blocking collectives, shards(): near = lax.all_to_all(chosen, 'p', 0, 0).reshape(CHIPS * SENT_ROWS, -1)  22.6 us
    all_to_all x1, blocking collectives, shards(): got = lax.all_to_all(pair.reshape(CHIPS, BACK_ROWS, -1), 'p', 0, 0)  15.4 us
    pallas_call x12, Pallas kernels, call(): pl.pallas_call(body, in_specs=[VMEM] * len(ins), out_specs=[out_spec] * l...  14.6 us
    ppermute x1, starting transfers between devices, shards(): lax.ppermute(stash[0], ('p', 'c'), [(k, places - 1 - k) for k in range(pl...  6.41 us
    unnamed x18, local copies, waits for them, and re-layouts  4.25 us
  transfers between devices with their start and end apart: 17, of which 10 were waited for; matrix products, arithmetic and copies ran while one was open for 1% of the time, Pallas kernels for 9%

profile of v5, /device:TPU:1, one launch (start us, length us, event | category | flops | bytes accessed | tf_op | source)
XLA Modules:
  0.0 121.8 jit_solution(3394479222111069902)
XLA Ops:
  0.6 6.4 %collective-permute-start = (bf16[8,1536]{1,0:T(8,128)(2,1)}, bf16[8,1536]{1,0:T(8,128)(2,1)S(1)}, u32[]{:S(2)}, u32[]{:S(2)}) collective-permute-start(bf16[8,1536]{1,0:T(8,128)(2,1)} %bitcast.11), channel_id=1, source_target_pairs={{0,124},{4,120},{8,116},{12,112},{16,108},{20,104},{24,100},{28,96... | collective-permute-start | bytes 73736 | tf_op jit(solution)/shard_map/ppermute | solution.py:401
  7.9 0.9 collective-permute-done.x
  9.5 6.9 %collective-permute-start.1 = (bf16[16,1664]{1,0:T(8,128)(2,1)S(1)}, bf16[16,1664]{1,0:T(8,128)(2,1)S(1)}, u32[]{:S(2)}, u32[]{:S(2)}) collective-permute-start(bf16[16,1664]{1,0:T(8,128)(2,1)S(1)} %fusion.1.mine), channel_id=1, source_target_pairs={{0,128},{128,0},{1,129},{129,1},{2,130},{130,2},{3,131},{131,3},{4... | collective-permute-start | bytes 159752 | tf_op jit(solution)/shard_map/ppermute | solution.py:362
  16.4 1.4 %copy-done = bf16[512,1536]{1,0:T(8,128)(2,1)S(1)} copy-done((bf16[512,1536]{1,0:T(8,128)(2,1)S(1)}, bf16[512,1536]{1,0:T(8,128)(2,1)}, u32[]{:S(2)}) %copy-start) | copy-done | bytes 1572888
  17.8 1.4 %copy-done.2 = bf16[512,1536]{1,0:T(8,128)(2,1)S(1)} copy-done((bf16[512,1536]{1,0:T(8,128)(2,1)S(1)}, bf16[512,1536]{1,0:T(8,128)(2,1)}, u32[]{:S(2)}) %copy-start.2) | copy-done | bytes 1572888
  19.2 1.4 %copy-done.4 = bf16[512,1536]{1,0:T(8,128)(2,1)S(1)} copy-done((bf16[512,1536]{1,0:T(8,128)(2,1)S(1)}, bf16[512,1536]{1,0:T(8,128)(2,1)}, u32[]{:S(2)}) %copy-start.4) | copy-done | bytes 1572888
  21.2 22.6 %all_to_all.10 = bf16[16,16,2048]{2,1,0:T(8,128)(2,1)S(1)} all-to-all(bf16[16,16,2048]{2,1,0:T(8,128)(2,1)S(1)} %get-tuple-element.38), channel_id=1, replica_groups=mesh['h'=2,'p'=16,'c'=2,'t'=4] {'p'}, dimensions={0} | all-to-all | bytes 2097152 | tf_op jit(solution)/shard_map/all_to_all | solution.py:413
  43.8 2.0 %collective-permute-start.8 = (bf16[256,2048]{1,0:T(8,128)(2,1)S(1)}, bf16[256,2048]{1,0:T(8,128)(2,1)S(1)}, u32[]{:S(2)}, u32[]{:S(2)}) collective-permute-start(bf16[256,2048]{1,0:T(8,128)(2,1)S(1)} %bitcast.7), channel_id=1, source_target_pairs={{0,4},{4,0},{1,5},{5,1},{2,6},{6,2},{3,7},{7,3},{8,12},{12,8},{9,1... | collective-permute-start | bytes 3145736 | tf_op jit(solution)/shard_map/ppermute | solution.py:362
  45.8 2.5 %shard_map.138 = (f32[168,512]{1,0:T(8,128)S(1)}, bf16[168,384]{1,0:T(8,128)(2,1)S(1)}, bf16[168,384]{1,0:T(8,128)(2,1)S(1)}, bf16[168,384]{1,0:T(8,128)(2,1)S(1)}, bf16[320,1536]{1,0:T(8,128)(2,1)S(1)}) custom-call(bf16[256,2048]{1,0:T(8,128)(2,1)S(1)} %bitcast.8, bf16[512,1536]{1,0:T(8,128)(2,1)S(1)} %copy-done.1, bf16[512,1536]{1,0:T(8,128)(2,1)S(1)} %copy-done.3, ...), custom_call_target="tpu_custom_call" | custom-call | flops 1069547520 | bytes 7114752 | tf_op jit(solution)/shard_map/pallas_call | solution.py:347
  48.3 1.7 %collective-permute-start.2 = (bf16[168,384]{1,0:T(8,128)(2,1)S(1)}, bf16[168,384]{1,0:T(8,128)(2,1)S(1)}, u32[]{:S(2)}, u32[]{:S(2)}) collective-permute-start(bf16[168,384]{1,0:T(8,128)(2,1)S(1)} %get-tuple-element.40), channel_id=1, source_target_pairs={{0,3},{1,2},{2,1},{3,0},{4,7},{5,6},{6,5},{7,4},{8,11},{9,10},{10,... | collective-permute-start | bytes 387080 | tf_op jit(solution)/shard_map/ppermute | solution.py:362
  50.3 1.6 %collective-permute-start.4 = (bf16[168,384]{1,0:T(8,128)(2,1)S(1)}, bf16[168,384]{1,0:T(8,128)(2,1)S(1)}, u32[]{:S(2)}, u32[]{:S(2)}) collective-permute-start(bf16[168,384]{1,0:T(8,128)(2,1)S(1)} %get-tuple-element.42), channel_id=1, source_target_pairs={{0,1},{1,0},{2,3},{3,2},{4,5},{5,4},{6,7},{7,6},{8,9},{9,8},{10,11... | collective-permute-start | bytes 387080 | tf_op jit(solution)/shard_map/ppermute | solution.py:362
  52.0 2.4 %shard_map.141 = (f32[168,512]{1,0:T(8,128)S(1)}, bf16[168,384]{1,0:T(8,128)(2,1)S(1)}, bf16[168,384]{1,0:T(8,128)(2,1)S(1)}, bf16[168,384]{1,0:T(8,128)(2,1)S(1)}, bf16[320,1536]{1,0:T(8,128)(2,1)S(1)}) custom-call(bf16[256,2048]{1,0:T(8,128)(2,1)S(1)} %collective-permute-done.8.block, bf16[512,1536]{1,0:T(8,128)(2,1)S(1)} %copy-done.1, ...), custom_call_target="tpu_custom_call" | custom-call | flops 1069547520 | bytes 7114752 | tf_op jit(solution)/shard_map/pallas_call | solution.py:347
  54.4 1.7 %collective-permute-start.9 = (bf16[168,384]{1,0:T(8,128)(2,1)S(1)}, bf16[168,384]{1,0:T(8,128)(2,1)S(1)}, u32[]{:S(2)}, u32[]{:S(2)}) collective-permute-start(bf16[168,384]{1,0:T(8,128)(2,1)S(1)} %get-tuple-element.50), channel_id=1, source_target_pairs={{0,3},{1,2},{2,1},{3,0},{4,7},{5,6},{6,5},{7,4},{8,11},{9,10},{10,... | collective-permute-start | bytes 387080 | tf_op jit(solution)/shard_map/ppermute | solution.py:362
  56.1 3.7 %collective-permute-start.11 = (bf16[168,384]{1,0:T(8,128)(2,1)S(1)}, bf16[168,384]{1,0:T(8,128)(2,1)S(1)}, u32[]{:S(2)}, u32[]{:S(2)}) collective-permute-start(bf16[168,384]{1,0:T(8,128)(2,1)S(1)} %get-tuple-element.52), channel_id=1, source_target_pairs={{0,1},{1,0},{2,3},{3,2},{4,5},{5,4},{6,7},{7,6},{8,9},{9,8},{10,11... | collective-permute-start | bytes 387080 | tf_op jit(solution)/shard_map/ppermute | solution.py:362
  59.8 8.1 %collective-permute-done.3.got2 = bf16[168,384]{1,0:T(8,128)(2,1)S(1)} collective-permute-done((bf16[168,384]{1,0:T(8,128)(2,1)S(1)}, bf16[168,384]{1,0:T(8,128)(2,1)S(1)}, u32[]{:S(2)}, u32[]{:S(2)}) %collective-permute-start.3) | collective-permute-done | bytes 129056 | tf_op jit(solution)/shard_map/ppermute | solution.py:362
  67.8 0.8 shard_map.139
  68.6 7.5 %collective-permute-done.10.got2 = bf16[168,384]{1,0:T(8,128)(2,1)S(1)} collective-permute-done((bf16[168,384]{1,0:T(8,128)(2,1)S(1)}, bf16[168,384]{1,0:T(8,128)(2,1)S(1)}, u32[]{:S(2)}, u32[]{:S(2)}) %collective-permute-start.10) | collective-permute-done | bytes 129056 | tf_op jit(solution)/shard_map/ppermute | solution.py:362
  76.9 1.9 %collective-permute-start.5 = (bf16[168,384]{1,0:T(8,128)(2,1)S(1)}, bf16[168,384]{1,0:T(8,128)(2,1)S(1)}, u32[]{:S(2)}, u32[]{:S(2)}) collective-permute-start(bf16[168,384]{1,0:T(8,128)(2,1)S(1)} %get-tuple-element.43.p0.refs_0_), channel_id=1, source_target_pairs={{0,1},{1,0},{2,3},{3,2},{4,5},{5,4},{6,7},{7,6},{8,9},{9,8},{10,11... | collective-permute-start | bytes 387080 | tf_op jit(solution)/shard_map/ppermute | solution.py:362
  78.9 1.5 %collective-permute-start.12 = (bf16[168,384]{1,0:T(8,128)(2,1)S(1)}, bf16[168,384]{1,0:T(8,128)(2,1)S(1)}, u32[]{:S(2)}, u32[]{:S(2)}) collective-permute-start(bf16[168,384]{1,0:T(8,128)(2,1)S(1)} %get-tuple-element.53.p0.refs_5_), channel_id=1, source_target_pairs={{0,1},{1,0},{2,3},{3,2},{4,5},{5,4},{6,7},{7,6},{8,9},{9,8},{10,11... | collective-permute-start | bytes 387080 | tf_op jit(solution)/shard_map/ppermute | solution.py:362
  80.3 4.7 %collective-permute-done.13.p2.refs_7_ = bf16[168,384]{1,0:T(8,128)(2,1)S(1)} collective-permute-done((bf16[168,384]{1,0:T(8,128)(2,1)S(1)}, bf16[168,384]{1,0:T(8,128)(2,1)S(1)}, u32[]{:S(2)}, u32[]{:S(2)}) %collective-permute-start.13) | collective-permute-done | bytes 129056 | tf_op jit(solution)/shard_map/ppermute | solution.py:362
  85.1 1.9 %collective-permute-done.7.p3.refs_3_ = bf16[168,384]{1,0:T(8,128)(2,1)S(1)} collective-permute-done((bf16[168,384]{1,0:T(8,128)(2,1)S(1)}, bf16[168,384]{1,0:T(8,128)(2,1)S(1)}, u32[]{:S(2)}, u32[]{:S(2)}) %collective-permute-start.7) | collective-permute-done | bytes 129056 | tf_op jit(solution)/shard_map/ppermute | solution.py:362
  87.0 1.2 shard_map.140
  88.2 1.6 %collective-permute-done.12.p1.refs_6_ = bf16[168,384]{1,0:T(8,128)(2,1)S(1)} collective-permute-done((bf16[168,384]{1,0:T(8,128)(2,1)S(1)}, bf16[168,384]{1,0:T(8,128)(2,1)S(1)}, u32[]{:S(2)}, u32[]{:S(2)}) %collective-permute-start.12) | collective-permute-done | bytes 129056 | tf_op jit(solution)/shard_map/ppermute | solution.py:362
  89.7 2.8 %collective-permute-done.14.p3.refs_8_ = bf16[168,384]{1,0:T(8,128)(2,1)S(1)} collective-permute-done((bf16[168,384]{1,0:T(8,128)(2,1)S(1)}, bf16[168,384]{1,0:T(8,128)(2,1)S(1)}, u32[]{:S(2)}, u32[]{:S(2)}) %collective-permute-start.14) | collective-permute-done | bytes 129056 | tf_op jit(solution)/shard_map/ppermute | solution.py:362
  92.5 1.2 shard_map.143
  93.7 1.9 %collective-permute-start.15 = (bf16[176,1536]{1,0:T(8,128)(2,1)S(1)}, bf16[176,1536]{1,0:T(8,128)(2,1)S(1)}, u32[]{:S(2)}, u32[]{:S(2)}) collective-permute-start(bf16[176,1536]{1,0:T(8,128)(2,1)S(1)} %get-tuple-element.57), channel_id=1, source_target_pairs={{0,4},{4,0},{1,5},{5,1},{2,6},{6,2},{3,7},{7,3},{8,12},{12,8},{9,1... | collective-permute-start | bytes 1622024 | tf_op jit(solution)/shard_map/ppermute | solution.py:362
  95.6 1.6 %collective-permute-done.15.got = bf16[176,1536]{1,0:T(8,128)(2,1)S(1)} collective-permute-done((bf16[176,1536]{1,0:T(8,128)(2,1)S(1)}, bf16[176,1536]{1,0:T(8,128)(2,1)S(1)}, u32[]{:S(2)}, u32[]{:S(2)}) %collective-permute-start.15) | collective-permute-done | bytes 540704 | tf_op jit(solution)/shard_map/ppermute | solution.py:362
  97.9 15.4 %all_to_all.11.got = bf16[16,8,2688]{2,1,0:T(8,128)(2,1)S(1)} all-to-all(bf16[16,8,2688]{2,1,0:T(8,128)(2,1)S(1)} %bitcast.9), channel_id=1, replica_groups=mesh['h'=2,'p'=16,'c'=2,'t'=4] {'p'}, dimensions={0} | all-to-all | bytes 1376256 | tf_op jit(solution)/shard_map/all_to_all | solution.py:465
  113.4 2.5 %collective-permute-start.16 = (bf16[16,1536]{1,0:T(8,128)(2,1)S(1)}, bf16[16,1536]{1,0:T(8,128)(2,1)S(1)}, u32[]{:S(2)}, u32[]{:S(2)}) collective-permute-start(bf16[16,1536]{1,0:T(8,128)(2,1)S(1)} %get-tuple-element.61), channel_id=1, source_target_pairs={{0,128},{128,0},{1,129},{129,1},{2,130},{130,2},{3,131},{131,3},{4... | collective-permute-start | bytes 147464 | tf_op jit(solution)/shard_map/ppermute | solution.py:362
  115.9 3.5 %shard_map.147 = (bf16[512,1536]{1,0:T(8,128)(2,1)}, bf16[512,1536]{1,0:T(8,128)(2,1)}, bf16[512,1536]{1,0:T(8,128)(2,1)}) custom-call(bf16[168,384]{1,0:T(8,128)(2,1)S(1)} %get-tuple-element.43.p0.refs_0_, bf16[168,384]{1,0:T(8,128)(2,1)S(1)} %collective-permute-done.5.p1.refs_1_, bf16[168,384]{1,0:T(8,128)(2,1)S(1)} %collective-permute-done.6.p2.refs_2_, ...), custom_call_target="tpu_custom_call" | custom-call | flops 1509949440 | bytes 2998272 | tf_op jit(solution)/shard_map/pallas_call | solution.py:347
  119.4 1.4 %collective-permute-done.16.got = bf16[16,1536]{1,0:T(8,128)(2,1)S(1)} collective-permute-done((bf16[16,1536]{1,0:T(8,128)(2,1)S(1)}, bf16[16,1536]{1,0:T(8,128)(2,1)S(1)}, u32[]{:S(2)}, u32[]{:S(2)}) %collective-permute-start.16) | collective-permute-done | bytes 49184 | tf_op jit(solution)/shard_map/ppermute | solution.py:362
  120.8 1.0 shard_map.146
  (39 shorter events, 4.1 us)
Async XLA Ops:
  0.6 8.1 %collective-permute-start = (bf16[8,1536]{1,0:T(8,128)(2,1)}, bf16[8,1536]{1,0:T(8,128)(2,1)S(1)}, u32[]{:S(2)}, u32[]{:S(2)}) collective-permute-start(bf16[8,1536]{1,0:T(8,128)(2,1)} %bitcast.11), channel_id=1, source_target_pairs={{0,124},{4,120},{8,116},{12,112},{16,108},{20,104},{24,100},{28,96... | collective-permute-start | bytes 73736 | tf_op jit(solution)/shard_map/ppermute | solution.py:401
  9.5 11.2 %collective-permute-start.1 = (bf16[16,1664]{1,0:T(8,128)(2,1)S(1)}, bf16[16,1664]{1,0:T(8,128)(2,1)S(1)}, u32[]{:S(2)}, u32[]{:S(2)}) collective-permute-start(bf16[16,1664]{1,0:T(8,128)(2,1)S(1)} %fusion.1.mine), channel_id=1, source_target_pairs={{0,128},{128,0},{1,129},{129,1},{2,130},{130,2},{3,131},{131,3},{4... | collective-permute-start | bytes 159752 | tf_op jit(solution)/shard_map/ppermute | solution.py:362
  16.4 1.4 %copy-start = (bf16[512,1536]{1,0:T(8,128)(2,1)S(1)}, bf16[512,1536]{1,0:T(8,128)(2,1)}, u32[]{:S(2)}) copy-start(bf16[512,1536]{1,0:T(8,128)(2,1)} %gate_w.9) | copy-start | bytes 4718596
  17.8 1.4 %copy-start.2 = (bf16[512,1536]{1,0:T(8,128)(2,1)S(1)}, bf16[512,1536]{1,0:T(8,128)(2,1)}, u32[]{:S(2)}) copy-start(bf16[512,1536]{1,0:T(8,128)(2,1)} %up_w.9) | copy-start | bytes 4718596
  19.2 1.4 %copy-start.4 = (bf16[512,1536]{1,0:T(8,128)(2,1)S(1)}, bf16[512,1536]{1,0:T(8,128)(2,1)}, u32[]{:S(2)}) copy-start(bf16[512,1536]{1,0:T(8,128)(2,1)} %down_w.5) | copy-start | bytes 4718596
  20.6 25.1 %copy-start.8 = (bf16[4,1536]{1,0:T(4,128)(2,1)S(1)}, bf16[4,1536]{1,0:T(4,128)(2,1)}, u32[]{:S(2)}) copy-start(bf16[4,1536]{1,0:T(4,128)(2,1)} %param.11) | copy-start | bytes 36868
  20.6 25.1 %copy-start.3 = (bf16[512,1536]{1,0:T(8,128)(2,1)S(1)}, bf16[512,1536]{1,0:T(8,128)(2,1)}, u32[]{:S(2)}) copy-start(bf16[512,1536]{1,0:T(8,128)(2,1)} %up_w.9) | copy-start | bytes 4718596
  20.6 25.1 %copy-start.5 = (bf16[512,1536]{1,0:T(8,128)(2,1)S(1)}, bf16[512,1536]{1,0:T(8,128)(2,1)}, u32[]{:S(2)}) copy-start(bf16[512,1536]{1,0:T(8,128)(2,1)} %down_w.5) | copy-start | bytes 4718596
  20.6 25.1 %copy-start.1 = (bf16[512,1536]{1,0:T(8,128)(2,1)S(1)}, bf16[512,1536]{1,0:T(8,128)(2,1)}, u32[]{:S(2)}) copy-start(bf16[512,1536]{1,0:T(8,128)(2,1)} %gate_w.9) | copy-start | bytes 4718596
  20.7 25.1 %copy-start.6 = (bf16[1760,256]{1,0:T(8,128)(2,1)S(1)}, bf16[1760,256]{1,0:T(8,128)(2,1)}, u32[]{:S(2)}) copy-start(bf16[1760,256]{1,0:T(8,128)(2,1)} %constant.7.clone.packer) | copy-start | bytes 2703364
  43.8 8.2 %collective-permute-start.8 = (bf16[256,2048]{1,0:T(8,128)(2,1)S(1)}, bf16[256,2048]{1,0:T(8,128)(2,1)S(1)}, u32[]{:S(2)}, u32[]{:S(2)}) collective-permute-start(bf16[256,2048]{1,0:T(8,128)(2,1)S(1)} %bitcast.7), channel_id=1, source_target_pairs={{0,4},{4,0},{1,5},{5,1},{2,6},{6,2},{3,7},{7,3},{8,12},{12,8},{9,1... | collective-permute-start | bytes 3145736 | tf_op jit(solution)/shard_map/ppermute | solution.py:362
  48.3 7.8 %collective-permute-start.2 = (bf16[168,384]{1,0:T(8,128)(2,1)S(1)}, bf16[168,384]{1,0:T(8,128)(2,1)S(1)}, u32[]{:S(2)}, u32[]{:S(2)}) collective-permute-start(bf16[168,384]{1,0:T(8,128)(2,1)S(1)} %get-tuple-element.40), channel_id=1, source_target_pairs={{0,3},{1,2},{2,1},{3,0},{4,7},{5,6},{6,5},{7,4},{8,11},{9,10},{10,... | collective-permute-start | bytes 387080 | tf_op jit(solution)/shard_map/ppermute | solution.py:362
  50.1 17.8 %collective-permute-start.3 = (bf16[168,384]{1,0:T(8,128)(2,1)S(1)}, bf16[168,384]{1,0:T(8,128)(2,1)S(1)}, u32[]{:S(2)}, u32[]{:S(2)}) collective-permute-start(bf16[168,384]{1,0:T(8,128)(2,1)S(1)} %get-tuple-element.41), channel_id=1, source_target_pairs={{0,2},{1,3},{2,0},{3,1},{4,6},{5,7},{6,4},{7,5},{8,10},{9,11},{10,... | collective-permute-start | bytes 387080 | tf_op jit(solution)/shard_map/ppermute | solution.py:362
  50.3 17.5 %collective-permute-start.4 = (bf16[168,384]{1,0:T(8,128)(2,1)S(1)}, bf16[168,384]{1,0:T(8,128)(2,1)S(1)}, u32[]{:S(2)}, u32[]{:S(2)}) collective-permute-start(bf16[168,384]{1,0:T(8,128)(2,1)S(1)} %get-tuple-element.42), channel_id=1, source_target_pairs={{0,1},{1,0},{2,3},{3,2},{4,5},{5,4},{6,7},{7,6},{8,9},{9,8},{10,11... | collective-permute-start | bytes 387080 | tf_op jit(solution)/shard_map/ppermute | solution.py:362
  54.4 14.2 %collective-permute-start.9 = (bf16[168,384]{1,0:T(8,128)(2,1)S(1)}, bf16[168,384]{1,0:T(8,128)(2,1)S(1)}, u32[]{:S(2)}, u32[]{:S(2)}) collective-permute-start(bf16[168,384]{1,0:T(8,128)(2,1)S(1)} %get-tuple-element.50), channel_id=1, source_target_pairs={{0,3},{1,2},{2,1},{3,0},{4,7},{5,6},{6,5},{7,4},{8,11},{9,10},{10,... | collective-permute-start | bytes 387080 | tf_op jit(solution)/shard_map/ppermute | solution.py:362
  56.1 20.0 %collective-permute-start.10 = (bf16[168,384]{1,0:T(8,128)(2,1)S(1)}, bf16[168,384]{1,0:T(8,128)(2,1)S(1)}, u32[]{:S(2)}, u32[]{:S(2)}) collective-permute-start(bf16[168,384]{1,0:T(8,128)(2,1)S(1)} %get-tuple-element.51), channel_id=1, source_target_pairs={{0,2},{1,3},{2,0},{3,1},{4,6},{5,7},{6,4},{7,5},{8,10},{9,11},{10,... | collective-permute-start | bytes 387080 | tf_op jit(solution)/shard_map/ppermute | solution.py:362
  56.1 20.0 %collective-permute-start.11 = (bf16[168,384]{1,0:T(8,128)(2,1)S(1)}, bf16[168,384]{1,0:T(8,128)(2,1)S(1)}, u32[]{:S(2)}, u32[]{:S(2)}) collective-permute-start(bf16[168,384]{1,0:T(8,128)(2,1)S(1)} %get-tuple-element.52), channel_id=1, source_target_pairs={{0,1},{1,0},{2,3},{3,2},{4,5},{5,4},{6,7},{7,6},{8,9},{9,8},{10,11... | collective-permute-start | bytes 387080 | tf_op jit(solution)/shard_map/ppermute | solution.py:362
  68.6 10.3 %collective-permute-start.6 = (bf16[168,384]{1,0:T(8,128)(2,1)S(1)}, bf16[168,384]{1,0:T(8,128)(2,1)S(1)}, u32[]{:S(2)}, u32[]{:S(2)}) collective-permute-start(bf16[168,384]{1,0:T(8,128)(2,1)S(1)} %get-tuple-element.43.p0.refs_0_), channel_id=1, source_target_pairs={{0,2},{1,3},{2,0},{3,1},{4,6},{5,7},{6,4},{7,5},{8,10},{9,11},{10,... | collective-permute-start | bytes 387080 | tf_op jit(solution)/shard_map/ppermute | solution.py:362
  76.8 8.2 %collective-permute-start.13 = (bf16[168,384]{1,0:T(8,128)(2,1)S(1)}, bf16[168,384]{1,0:T(8,128)(2,1)S(1)}, u32[]{:S(2)}, u32[]{:S(2)}) collective-permute-start(bf16[168,384]{1,0:T(8,128)(2,1)S(1)} %get-tuple-element.53.p0.refs_5_), channel_id=1, source_target_pairs={{0,2},{1,3},{2,0},{3,1},{4,6},{5,7},{6,4},{7,5},{8,10},{9,11},{10,... | collective-permute-start | bytes 387080 | tf_op jit(solution)/shard_map/ppermute | solution.py:362
  76.9 8.2 %collective-permute-start.5 = (bf16[168,384]{1,0:T(8,128)(2,1)S(1)}, bf16[168,384]{1,0:T(8,128)(2,1)S(1)}, u32[]{:S(2)}, u32[]{:S(2)}) collective-permute-start(bf16[168,384]{1,0:T(8,128)(2,1)S(1)} %get-tuple-element.43.p0.refs_0_), channel_id=1, source_target_pairs={{0,1},{1,0},{2,3},{3,2},{4,5},{5,4},{6,7},{7,6},{8,9},{9,8},{10,11... | collective-permute-start | bytes 387080 | tf_op jit(solution)/shard_map/ppermute | solution.py:362
  78.9 8.1 %collective-permute-start.7 = (bf16[168,384]{1,0:T(8,128)(2,1)S(1)}, bf16[168,384]{1,0:T(8,128)(2,1)S(1)}, u32[]{:S(2)}, u32[]{:S(2)}) collective-permute-start(bf16[168,384]{1,0:T(8,128)(2,1)S(1)} %collective-permute-done.6.p2.refs_2_), channel_id=1, source_target_pairs={{0,1},{1,0},{2,3},{3,2},{4,5},{5,4},{6,7},{7,6},{8,9},{9,8},{10,11... | collective-permute-start | bytes 387080 | tf_op jit(solution)/shard_map/ppermute | solution.py:362
  78.9 10.9 %collective-permute-start.12 = (bf16[168,384]{1,0:T(8,128)(2,1)S(1)}, bf16[168,384]{1,0:T(8,128)(2,1)S(1)}, u32[]{:S(2)}, u32[]{:S(2)}) collective-permute-start(bf16[168,384]{1,0:T(8,128)(2,1)S(1)} %get-tuple-element.53.p0.refs_5_), channel_id=1, source_target_pairs={{0,1},{1,0},{2,3},{3,2},{4,5},{5,4},{6,7},{7,6},{8,9},{9,8},{10,11... | collective-permute-start | bytes 387080 | tf_op jit(solution)/shard_map/ppermute | solution.py:362
  85.1 7.5 %collective-permute-start.14 = (bf16[168,384]{1,0:T(8,128)(2,1)S(1)}, bf16[168,384]{1,0:T(8,128)(2,1)S(1)}, u32[]{:S(2)}, u32[]{:S(2)}) collective-permute-start(bf16[168,384]{1,0:T(8,128)(2,1)S(1)} %collective-permute-done.13.p2.refs_7_), channel_id=1, source_target_pairs={{0,1},{1,0},{2,3},{3,2},{4,5},{5,4},{6,7},{7,6},{8,9},{9,8},{10,11... | collective-permute-start | bytes 387080 | tf_op jit(solution)/shard_map/ppermute | solution.py:362
  92.5 4.7 %copy-start.7 = (bf16[1664,176]{1,0:T(8,128)(2,1)S(1)}, bf16[1664,176]{1,0:T(8,128)(2,1)}, u32[]{:S(2)}) copy-start(bf16[1664,176]{1,0:T(8,128)(2,1)} %constant.8.clone.unpacker) | copy-start | bytes 1757188
  93.7 3.5 %collective-permute-start.15 = (bf16[176,1536]{1,0:T(8,128)(2,1)S(1)}, bf16[176,1536]{1,0:T(8,128)(2,1)S(1)}, u32[]{:S(2)}, u32[]{:S(2)}) collective-permute-start(bf16[176,1536]{1,0:T(8,128)(2,1)S(1)} %get-tuple-element.57), channel_id=1, source_target_pairs={{0,4},{4,0},{1,5},{5,1},{2,6},{6,2},{3,7},{7,3},{8,12},{12,8},{9,1... | collective-permute-start | bytes 1622024 | tf_op jit(solution)/shard_map/ppermute | solution.py:362
  113.4 7.4 %collective-permute-start.16 = (bf16[16,1536]{1,0:T(8,128)(2,1)S(1)}, bf16[16,1536]{1,0:T(8,128)(2,1)S(1)}, u32[]{:S(2)}, u32[]{:S(2)}) collective-permute-start(bf16[16,1536]{1,0:T(8,128)(2,1)S(1)} %get-tuple-element.61), channel_id=1, source_target_pairs={{0,128},{128,0},{1,129},{129,1},{2,130},{130,2},{3,131},{131,3},{4... | collective-permute-start | bytes 147464 | tf_op jit(solution)/shard_map/ppermute | solution.py:362

commit v6 on v5

--- a/solution.py
+++ b/solution.py
@@ -145,11 +145,20 @@
         out[slots:, : 3 * share] = notes[...].astype(out.dtype)
 
 
-def act_kernel(
-    width, slots, share, experts, has_own, own_block, own, got1, got2, got3,
-    packed, weight, local, losses,
-):
-    total = own[:, : 3 * share] + got1[...].astype(F32) + got2[...].astype(F32) + got3[...].astype(F32)
+def relay_kernel(slots, share, held, got, out):
+    total = held[...] + got[...].astype(F32)
+    high, low = split_pair(total[slots : slots + 1] + total[slots + 1 : slots + 2])
+    zero = jnp.zeros((6, 3 * share), F32)
+    notes = jnp.concatenate([high.astype(F32), low.astype(F32), zero], 0)
+    out[:slots] = total[:slots].astype(BF)
+    out[slots:] = notes.astype(BF)
+
+
+def act_kernel(width, slots, share, experts, has_own, own_block, own, *refs):
+    gots, (packed, weight, local, losses) = refs[:-4], refs[-4:]
+    total = own[:, : 3 * share]
+    for got in gots:
+        total = total + got[...].astype(F32)
     toward = own[:slots, 3 * share :]
     used = jnp.sum(jnp.abs(toward), axis=1, keepdims=True) > 0.5
     lead = to_column(total[slots : slots + 1] + total[slots + 1 : slots + 2], slots)
@@ -421,12 +430,24 @@
             functools.partial(project_kernel, width, share, index == 0),
             [block, gate_weight, up_weight, down_weight, router_tall, packer, own_block],
             [((height, 3 * share + 128), F32)]
-            + [((height, 3 * share), BF)] * 3
-            + [((2 * slots, width), BF)],
+            + [((height, 3 * share), BF), ((height, 3 * share), F32 if index else BF)]
+            + [((height, 3 * share), BF), ((2 * slots, width), BF)],
             2 * slots * width * (3 * hidden + 4 * slots),
             [pltpu.VMEM((8, 3 * share), F32)],
         )
-        got = [exchange(sends[step - 1], "t", step) for step in (3, 2, 1)]
+        if index == 0:
+            got = [exchange(sends[step - 1], "t", step) for step in (3, 2, 1)]
+        else:
+            passed = exchange(sends[2], "t", 1)
+            sends[1], halves[0][1][0] = lax.optimization_barrier((sends[1], halves[0][1][0]))
+            (relayed,) = call(
+                functools.partial(relay_kernel, slots, share),
+                [sends[1], passed],
+                [((height, 3 * share), BF)],
+                slots * share * 6,
+            )
+            beside, relayed = lax.optimization_barrier((sends[0], relayed))
+            got = [exchange(relayed, "t", 2), exchange(beside, "t", 1)]
         halves.append((mine, got, taken))
     gradients = []
     for index, (mine, got, taken) in enumerate(halves):
@@ -436,7 +457,10 @@
             [((height, 3 * share), BF), ((slots, 128), F32), ((16, 128), F32), ((1, 2), F32)],
             slots * share * 40,
         )
-        pieces = [packed, exchange(packed, "t", 1), exchange(packed, "t", 2)]
+        packed_one = packed
+        if index == 1:
+            packed_one, gradients[0][0][1] = lax.optimization_barrier((packed, gradients[0][0][1]))
+        pieces = [packed, exchange(packed_one, "t", 1), exchange(packed, "t", 2)]
         pieces.append(exchange(pieces[2], "t", 1))
         gradients.append((pieces, weight, local, losses))
     _, _, local, losses = gradients[0]

time: 122 us -> 116 us (0.951)
  waiting for transfers between devices: 30.4 us -> 26.9 us
  starting transfers between devices: 32.1 us -> 29.4 us
    ppermute x16, waiting for transfers between devices: 29.6 us -> 26 us  [exchange(): return lax.ppermute(value, axis, [(k, k ^ step) for k in range(count)])]
    ppermute x16, starting transfers between devices: 25.7 us -> 23 us  [exchange(): return lax.ppermute(value, axis, [(k, k ^ step) for k in range(count)])]
    pallas_call x12 -> x13, Pallas kernels: 14.6 us -> 14.5 us  [call(): pl.pallas_call(body, in_specs=[VMEM] * len(ins), out_specs=[out_spec] * l...]
  transfers between devices with their start and end apart: 17 -> 17, of which waited for: 10 -> 14; matrix products, arithmetic and copies ran while one was open for 1% -> 1% of each run, Pallas kernels for 9% -> 10%
where the time goes in v6:
time: 116 us; the launch traced here: 115 us
  blocking collectives  38 us (33%)
  starting transfers between devices  29.4 us (25%)
  waiting for transfers between devices  26.9 us (23%)
  Pallas kernels  14.5 us (12%)
  local copies, waits for them, and re-layouts  4.38 us (4%)
  other arithmetic  1.5 us (1%)
    ppermute x16, waiting for transfers between devices, exchange(): return lax.ppermute(value, axis, [(k, k ^ step) for k in range(count)])  26 us
    ppermute x16, starting transfers between devices, exchange(): return lax.ppermute(value, axis, [(k, k ^ step) for k in range(count)])  23 us
    all_to_all x1, blocking collectives, shards(): near = lax.all_to_all(chosen, 'p', 0, 0).reshape(CHIPS * SENT_ROWS, -1)  22.6 us
    all_to_all x1, blocking collectives, shards(): got = lax.all_to_all(pair.reshape(CHIPS, BACK_ROWS, -1), 'p', 0, 0)  15.4 us
    pallas_call x13, Pallas kernels, call(): pl.pallas_call(body, in_specs=[VMEM] * len(ins), out_specs=[out_spec] * l...  14.5 us
    ppermute x1, starting transfers between devices, shards(): lax.ppermute(stash[0], ('p', 'c'), [(k, places - 1 - k) for k in range(pl...  6.41 us
    unnamed x18, local copies, waits for them, and re-layouts  4.25 us
  transfers between devices with their start and end apart: 17, of which 14 were waited for; matrix products, arithmetic and copies ran while one was open for 1% of the time, Pallas kernels for 10%

profile of v6, /device:TPU:1, one launch (start us, length us, event | category | flops | bytes accessed | tf_op | source)
XLA Modules:
  0.0 115.5 jit_solution(8535412450720356132)
XLA Ops:
  0.6 6.4 %collective-permute-start = (bf16[8,1536]{1,0:T(8,128)(2,1)}, bf16[8,1536]{1,0:T(8,128)(2,1)S(1)}, u32[]{:S(2)}, u32[]{:S(2)}) collective-permute-start(bf16[8,1536]{1,0:T(8,128)(2,1)} %bitcast.11), channel_id=1, source_target_pairs={{0,124},{4,120},{8,116},{12,112},{16,108},{20,104},{24,100},{28,96... | collective-permute-start | bytes 73736 | tf_op jit(solution)/shard_map/ppermute | solution.py:410
  7.9 0.9 collective-permute-done.x
  9.5 6.9 %collective-permute-start.1 = (bf16[16,1664]{1,0:T(8,128)(2,1)S(1)}, bf16[16,1664]{1,0:T(8,128)(2,1)S(1)}, u32[]{:S(2)}, u32[]{:S(2)}) collective-permute-start(bf16[16,1664]{1,0:T(8,128)(2,1)S(1)} %fusion.1.mine), channel_id=1, source_target_pairs={{0,128},{128,0},{1,129},{129,1},{2,130},{130,2},{3,131},{131,3},{4... | collective-permute-start | bytes 159752 | tf_op jit(solution)/shard_map/ppermute | solution.py:371
  16.4 1.4 %copy-done = bf16[512,1536]{1,0:T(8,128)(2,1)S(1)} copy-done((bf16[512,1536]{1,0:T(8,128)(2,1)S(1)}, bf16[512,1536]{1,0:T(8,128)(2,1)}, u32[]{:S(2)}) %copy-start) | copy-done | bytes 1572888
  17.8 1.4 %copy-done.2 = bf16[512,1536]{1,0:T(8,128)(2,1)S(1)} copy-done((bf16[512,1536]{1,0:T(8,128)(2,1)S(1)}, bf16[512,1536]{1,0:T(8,128)(2,1)}, u32[]{:S(2)}) %copy-start.2) | copy-done | bytes 1572888
  19.2 1.4 %copy-done.4 = bf16[512,1536]{1,0:T(8,128)(2,1)S(1)} copy-done((bf16[512,1536]{1,0:T(8,128)(2,1)S(1)}, bf16[512,1536]{1,0:T(8,128)(2,1)}, u32[]{:S(2)}) %copy-start.4) | copy-done | bytes 1572888
  21.2 22.6 %all_to_all.10 = bf16[16,16,2048]{2,1,0:T(8,128)(2,1)S(1)} all-to-all(bf16[16,16,2048]{2,1,0:T(8,128)(2,1)S(1)} %get-tuple-element.44), channel_id=1, replica_groups=mesh['h'=2,'p'=16,'c'=2,'t'=4] {'p'}, dimensions={0} | all-to-all | bytes 2097152 | tf_op jit(solution)/shard_map/all_to_all | solution.py:422
  43.8 2.0 %collective-permute-start.2 = (bf16[256,2048]{1,0:T(8,128)(2,1)S(1)}, bf16[256,2048]{1,0:T(8,128)(2,1)S(1)}, u32[]{:S(2)}, u32[]{:S(2)}) collective-permute-start(bf16[256,2048]{1,0:T(8,128)(2,1)S(1)} %bitcast.7), channel_id=1, source_target_pairs={{0,4},{4,0},{1,5},{5,1},{2,6},{6,2},{3,7},{7,3},{8,12},{12,8},{9,1... | collective-permute-start | bytes 3145736 | tf_op jit(solution)/shard_map/ppermute | solution.py:371
  45.8 2.5 %shard_map.138 = (f32[168,512]{1,0:T(8,128)S(1)}, bf16[168,384]{1,0:T(8,128)(2,1)S(1)}, bf16[168,384]{1,0:T(8,128)(2,1)S(1)}, bf16[168,384]{1,0:T(8,128)(2,1)S(1)}, bf16[320,1536]{1,0:T(8,128)(2,1)S(1)}) custom-call(bf16[256,2048]{1,0:T(8,128)(2,1)S(1)} %bitcast.8, bf16[512,1536]{1,0:T(8,128)(2,1)S(1)} %copy-done.1, bf16[512,1536]{1,0:T(8,128)(2,1)S(1)} %copy-done.3, ...), custom_call_target="tpu_custom_call" | custom-call | flops 1069547520 | bytes 7114752 | tf_op jit(solution)/shard_map/pallas_call | solution.py:356
  48.3 1.7 %collective-permute-start.3 = (bf16[168,384]{1,0:T(8,128)(2,1)S(1)}, bf16[168,384]{1,0:T(8,128)(2,1)S(1)}, u32[]{:S(2)}, u32[]{:S(2)}) collective-permute-start(bf16[168,384]{1,0:T(8,128)(2,1)S(1)} %get-tuple-element.49), channel_id=1, source_target_pairs={{0,3},{1,2},{2,1},{3,0},{4,7},{5,6},{6,5},{7,4},{8,11},{9,10},{10,... | collective-permute-start | bytes 387080 | tf_op jit(solution)/shard_map/ppermute | solution.py:371
  50.0 2.4 %shard_map.139 = (f32[168,512]{1,0:T(8,128)S(1)}, bf16[168,384]{1,0:T(8,128)(2,1)S(1)}, f32[168,384]{1,0:T(8,128)S(1)}, bf16[168,384]{1,0:T(8,128)(2,1)S(1)}, bf16[320,1536]{1,0:T(8,128)(2,1)S(1)}) custom-call(bf16[256,2048]{1,0:T(8,128)(2,1)S(1)} %collective-permute-done.2.block, bf16[512,1536]{1,0:T(8,128)(2,1)S(1)} %copy-done.1, ...), custom_call_target="tpu_custom_call" | custom-call | flops 1069547520 | bytes 7114752 | tf_op jit(solution)/shard_map/pallas_call | solution.py:356
  52.5 1.9 %collective-permute-start.4 = (bf16[168,384]{1,0:T(8,128)(2,1)S(1)}, bf16[168,384]{1,0:T(8,128)(2,1)S(1)}, u32[]{:S(2)}, u32[]{:S(2)}) collective-permute-start(bf16[168,384]{1,0:T(8,128)(2,1)S(1)} %get-tuple-element.51), channel_id=1, source_target_pairs={{0,2},{1,3},{2,0},{3,1},{4,6},{5,7},{6,4},{7,5},{8,10},{9,11},{10,... | collective-permute-start | bytes 387080 | tf_op jit(solution)/shard_map/ppermute | solution.py:371
  54.5 0.8 collective-permute-done.3.refs_0_
  55.3 4.5 %collective-permute-done.6.got = bf16[168,384]{1,0:T(8,128)(2,1)S(1)} collective-permute-done((bf16[168,384]{1,0:T(8,128)(2,1)S(1)}, bf16[168,384]{1,0:T(8,128)(2,1)S(1)}, u32[]{:S(2)}, u32[]{:S(2)}) %collective-permute-start.6) | collective-permute-done | bytes 129056 | tf_op jit(solution)/shard_map/ppermute | solution.py:371
  59.9 1.9 %collective-permute-start.8 = (bf16[168,384]{1,0:T(8,128)(2,1)S(1)}, bf16[168,384]{1,0:T(8,128)(2,1)S(1)}, u32[]{:S(2)}, u32[]{:S(2)}) collective-permute-start(bf16[168,384]{1,0:T(8,128)(2,1)S(1)} %get-tuple-element.59), channel_id=1, source_target_pairs={{0,1},{1,0},{2,3},{3,2},{4,5},{5,4},{6,7},{7,6},{8,9},{9,8},{10,11... | collective-permute-start | bytes 387080 | tf_op jit(solution)/shard_map/ppermute | solution.py:371
  62.2 2.2 %collective-permute-done.5.refs_2_ = bf16[168,384]{1,0:T(8,128)(2,1)S(1)} collective-permute-done((bf16[168,384]{1,0:T(8,128)(2,1)S(1)}, bf16[168,384]{1,0:T(8,128)(2,1)S(1)}, u32[]{:S(2)}, u32[]{:S(2)}) %collective-permute-start.5) | collective-permute-done | bytes 129056 | tf_op jit(solution)/shard_map/ppermute | solution.py:371
  65.2 1.9 %collective-permute-start.9 = (bf16[168,384]{1,0:T(8,128)(2,1)S(1)}, bf16[168,384]{1,0:T(8,128)(2,1)S(1)}, u32[]{:S(2)}, u32[]{:S(2)}) collective-permute-start(bf16[168,384]{1,0:T(8,128)(2,1)S(1)} %get-tuple-element.53.p0.refs_0_), channel_id=1, source_target_pairs={{0,1},{1,0},{2,3},{3,2},{4,5},{5,4},{6,7},{7,6},{8,9},{9,8},{10,11... | collective-permute-start | bytes 387080 | tf_op jit(solution)/shard_map/ppermute | solution.py:371
  67.1 1.4 %collective-permute-done.7.refs_0_ = bf16[168,384]{1,0:T(8,128)(2,1)S(1)} collective-permute-done((bf16[168,384]{1,0:T(8,128)(2,1)S(1)}, bf16[168,384]{1,0:T(8,128)(2,1)S(1)}, u32[]{:S(2)}, u32[]{:S(2)}) %collective-permute-start.7) | collective-permute-done | bytes 129056 | tf_op jit(solution)/shard_map/ppermute | solution.py:371
  68.5 1.3 %collective-permute-done.8.refs_1_ = bf16[168,384]{1,0:T(8,128)(2,1)S(1)} collective-permute-done((bf16[168,384]{1,0:T(8,128)(2,1)S(1)}, bf16[168,384]{1,0:T(8,128)(2,1)S(1)}, u32[]{:S(2)}, u32[]{:S(2)}) %collective-permute-start.8) | collective-permute-done | bytes 129056 | tf_op jit(solution)/shard_map/ppermute | solution.py:371
  70.6 3.5 %collective-permute-done.10.p2.refs_2_ = bf16[168,384]{1,0:T(8,128)(2,1)S(1)} collective-permute-done((bf16[168,384]{1,0:T(8,128)(2,1)S(1)}, bf16[168,384]{1,0:T(8,128)(2,1)S(1)}, u32[]{:S(2)}, u32[]{:S(2)}) %collective-permute-start.10) | collective-permute-done | bytes 129056 | tf_op jit(solution)/shard_map/ppermute | solution.py:371
  74.1 1.2 %collective-permute-done.9.p1.refs_1_ = bf16[168,384]{1,0:T(8,128)(2,1)S(1)} collective-permute-done((bf16[168,384]{1,0:T(8,128)(2,1)S(1)}, bf16[168,384]{1,0:T(8,128)(2,1)S(1)}, u32[]{:S(2)}, u32[]{:S(2)}) %collective-permute-start.9) | collective-permute-done | bytes 129056 | tf_op jit(solution)/shard_map/ppermute | solution.py:371
  75.5 4.1 %collective-permute-done.13.p2.refs_7_ = bf16[168,384]{1,0:T(8,128)(2,1)S(1)} collective-permute-done((bf16[168,384]{1,0:T(8,128)(2,1)S(1)}, bf16[168,384]{1,0:T(8,128)(2,1)S(1)}, u32[]{:S(2)}, u32[]{:S(2)}) %collective-permute-start.13) | collective-permute-done | bytes 129056 | tf_op jit(solution)/shard_map/ppermute | solution.py:371
  80.3 1.2 %shard_map.143 = (f32[160,1536]{1,0:T(8,128)S(1)}, f32[8,1536]{1,0:T(8,128)S(1)}) custom-call(bf16[168,384]{1,0:T(8,128)(2,1)S(1)} %get-tuple-element.53.p0.refs_0_, bf16[168,384]{1,0:T(8,128)(2,1)S(1)} %collective-permute-done.9.p1.refs_1_, bf16[168,384]{1,0:T(8,128)(2,1)S(1)} %collective-permute-done.10.p2.refs_2_, ...), custom_call_target="tpu_custom_call" | custom-call | flops 503316480 | bytes 5181440 | tf_op jit(solution)/shard_map/pallas_call | solution.py:356
  81.5 1.6 %collective-permute-done.12.p1.refs_6_ = bf16[168,384]{1,0:T(8,128)(2,1)S(1)} collective-permute-done((bf16[168,384]{1,0:T(8,128)(2,1)S(1)}, bf16[168,384]{1,0:T(8,128)(2,1)S(1)}, u32[]{:S(2)}, u32[]{:S(2)}) %collective-permute-start.12) | collective-permute-done | bytes 129056 | tf_op jit(solution)/shard_map/ppermute | solution.py:371
  83.1 2.8 %collective-permute-done.14.p3.refs_8_ = bf16[168,384]{1,0:T(8,128)(2,1)S(1)} collective-permute-done((bf16[168,384]{1,0:T(8,128)(2,1)S(1)}, bf16[168,384]{1,0:T(8,128)(2,1)S(1)}, u32[]{:S(2)}, u32[]{:S(2)}) %collective-permute-start.14) | collective-permute-done | bytes 129056 | tf_op jit(solution)/shard_map/ppermute | solution.py:371
  85.8 1.2 %shard_map.144 = (bf16[176,1536]{1,0:T(8,128)(2,1)S(1)}, f32[8,1536]{1,0:T(8,128)S(1)}) custom-call(bf16[168,384]{1,0:T(8,128)(2,1)S(1)} %get-tuple-element.65.p0.refs_5_, bf16[168,384]{1,0:T(8,128)(2,1)S(1)} %collective-permute-done.12.p1.refs_6_, bf16[168,384]{1,0:T(8,128)(2,1)S(1)} %collective-permute-done.13.p2.refs_7_, ...), custom_call_target="tpu_custom_call" | custom-call | flops 503316480 | bytes 5169152 | tf_op jit(solution)/shard_map/pallas_call | solution.py:356
  87.0 1.9 %collective-permute-start.15 = (bf16[176,1536]{1,0:T(8,128)(2,1)S(1)}, bf16[176,1536]{1,0:T(8,128)(2,1)S(1)}, u32[]{:S(2)}, u32[]{:S(2)}) collective-permute-start(bf16[176,1536]{1,0:T(8,128)(2,1)S(1)} %get-tuple-element.69), channel_id=1, source_target_pairs={{0,4},{4,0},{1,5},{5,1},{2,6},{6,2},{3,7},{7,3},{8,12},{12,8},{9,1... | collective-permute-start | bytes 1622024 | tf_op jit(solution)/shard_map/ppermute | solution.py:371
  88.9 1.6 %collective-permute-done.15.got = bf16[176,1536]{1,0:T(8,128)(2,1)S(1)} collective-permute-done((bf16[176,1536]{1,0:T(8,128)(2,1)S(1)}, bf16[176,1536]{1,0:T(8,128)(2,1)S(1)}, u32[]{:S(2)}, u32[]{:S(2)}) %collective-permute-start.15) | collective-permute-done | bytes 540704 | tf_op jit(solution)/shard_map/ppermute | solution.py:371
  91.2 15.4 %all_to_all.11.got = bf16[16,8,2688]{2,1,0:T(8,128)(2,1)S(1)} all-to-all(bf16[16,8,2688]{2,1,0:T(8,128)(2,1)S(1)} %bitcast.9), channel_id=1, replica_groups=mesh['h'=2,'p'=16,'c'=2,'t'=4] {'p'}, dimensions={0} | all-to-all | bytes 1376256 | tf_op jit(solution)/shard_map/all_to_all | solution.py:489
  106.7 4.2 %collective-permute-start.16 = (bf16[16,1536]{1,0:T(8,128)(2,1)S(1)}, bf16[16,1536]{1,0:T(8,128)(2,1)S(1)}, u32[]{:S(2)}, u32[]{:S(2)}) collective-permute-start(bf16[16,1536]{1,0:T(8,128)(2,1)S(1)} %get-tuple-element.73), channel_id=1, source_target_pairs={{0,128},{128,0},{1,129},{129,1},{2,130},{130,2},{3,131},{131,3},{4... | collective-permute-start | bytes 147464 | tf_op jit(solution)/shard_map/ppermute | solution.py:371
  110.9 3.5 %shard_map.148 = (bf16[512,1536]{1,0:T(8,128)(2,1)}, bf16[512,1536]{1,0:T(8,128)(2,1)}, bf16[512,1536]{1,0:T(8,128)(2,1)}) custom-call(bf16[168,384]{1,0:T(8,128)(2,1)S(1)} %get-tuple-element.53.p0.refs_0_, bf16[168,384]{1,0:T(8,128)(2,1)S(1)} %collective-permute-done.9.p1.refs_1_, bf16[168,384]{1,0:T(8,128)(2,1)S(1)} %collective-permute-done.10.p2.refs_2_, ...), custom_call_target="tpu_custom_call" | custom-call | flops 1509949440 | bytes 2998272 | tf_op jit(solution)/shard_map/pallas_call | solution.py:356
  114.5 1.0 shard_map.147
  (40 shorter events, 6.0 us)
Async XLA Ops:
  0.6 8.1 %collective-permute-start = (bf16[8,1536]{1,0:T(8,128)(2,1)}, bf16[8,1536]{1,0:T(8,128)(2,1)S(1)}, u32[]{:S(2)}, u32[]{:S(2)}) collective-permute-start(bf16[8,1536]{1,0:T(8,128)(2,1)} %bitcast.11), channel_id=1, source_target_pairs={{0,124},{4,120},{8,116},{12,112},{16,108},{20,104},{24,100},{28,96... | collective-permute-start | bytes 73736 | tf_op jit(solution)/shard_map/ppermute | solution.py:410
  9.5 11.2 %collective-permute-start.1 = (bf16[16,1664]{1,0:T(8,128)(2,1)S(1)}, bf16[16,1664]{1,0:T(8,128)(2,1)S(1)}, u32[]{:S(2)}, u32[]{:S(2)}) collective-permute-start(bf16[16,1664]{1,0:T(8,128)(2,1)S(1)} %fusion.1.mine), channel_id=1, source_target_pairs={{0,128},{128,0},{1,129},{129,1},{2,130},{130,2},{3,131},{131,3},{4... | collective-permute-start | bytes 159752 | tf_op jit(solution)/shard_map/ppermute | solution.py:371
  16.4 1.4 %copy-start = (bf16[512,1536]{1,0:T(8,128)(2,1)S(1)}, bf16[512,1536]{1,0:T(8,128)(2,1)}, u32[]{:S(2)}) copy-start(bf16[512,1536]{1,0:T(8,128)(2,1)} %gate_w.9) | copy-start | bytes 4718596
  17.8 1.4 %copy-start.2 = (bf16[512,1536]{1,0:T(8,128)(2,1)S(1)}, bf16[512,1536]{1,0:T(8,128)(2,1)}, u32[]{:S(2)}) copy-start(bf16[512,1536]{1,0:T(8,128)(2,1)} %up_w.9) | copy-start | bytes 4718596
  19.2 1.4 %copy-start.4 = (bf16[512,1536]{1,0:T(8,128)(2,1)S(1)}, bf16[512,1536]{1,0:T(8,128)(2,1)}, u32[]{:S(2)}) copy-start(bf16[512,1536]{1,0:T(8,128)(2,1)} %down_w.5) | copy-start | bytes 4718596
  20.6 25.1 %copy-start.8 = (bf16[4,1536]{1,0:T(4,128)(2,1)S(1)}, bf16[4,1536]{1,0:T(4,128)(2,1)}, u32[]{:S(2)}) copy-start(bf16[4,1536]{1,0:T(4,128)(2,1)} %param.11) | copy-start | bytes 36868
  20.6 25.1 %copy-start.3 = (bf16[512,1536]{1,0:T(8,128)(2,1)S(1)}, bf16[512,1536]{1,0:T(8,128)(2,1)}, u32[]{:S(2)}) copy-start(bf16[512,1536]{1,0:T(8,128)(2,1)} %up_w.9) | copy-start | bytes 4718596
  20.6 25.1 %copy-start.5 = (bf16[512,1536]{1,0:T(8,128)(2,1)S(1)}, bf16[512,1536]{1,0:T(8,128)(2,1)}, u32[]{:S(2)}) copy-start(bf16[512,1536]{1,0:T(8,128)(2,1)} %down_w.5) | copy-start | bytes 4718596
  20.6 25.1 %copy-start.1 = (bf16[512,1536]{1,0:T(8,128)(2,1)S(1)}, bf16[512,1536]{1,0:T(8,128)(2,1)}, u32[]{:S(2)}) copy-start(bf16[512,1536]{1,0:T(8,128)(2,1)} %gate_w.9) | copy-start | bytes 4718596
  20.7 25.1 %copy-start.6 = (bf16[1760,256]{1,0:T(8,128)(2,1)S(1)}, bf16[1760,256]{1,0:T(8,128)(2,1)}, u32[]{:S(2)}) copy-start(bf16[1760,256]{1,0:T(8,128)(2,1)} %constant.7.clone.packer) | copy-start | bytes 2703364
  43.8 6.3 %collective-permute-start.2 = (bf16[256,2048]{1,0:T(8,128)(2,1)S(1)}, bf16[256,2048]{1,0:T(8,128)(2,1)S(1)}, u32[]{:S(2)}, u32[]{:S(2)}) collective-permute-start(bf16[256,2048]{1,0:T(8,128)(2,1)S(1)} %bitcast.7), channel_id=1, source_target_pairs={{0,4},{4,0},{1,5},{5,1},{2,6},{6,2},{3,7},{7,3},{8,12},{12,8},{9,1... | collective-permute-start | bytes 3145736 | tf_op jit(solution)/shard_map/ppermute | solution.py:371
  48.3 7.0 %collective-permute-start.3 = (bf16[168,384]{1,0:T(8,128)(2,1)S(1)}, bf16[168,384]{1,0:T(8,128)(2,1)S(1)}, u32[]{:S(2)}, u32[]{:S(2)}) collective-permute-start(bf16[168,384]{1,0:T(8,128)(2,1)S(1)} %get-tuple-element.49), channel_id=1, source_target_pairs={{0,3},{1,2},{2,1},{3,0},{4,7},{5,6},{6,5},{7,4},{8,11},{9,10},{10,... | collective-permute-start | bytes 387080 | tf_op jit(solution)/shard_map/ppermute | solution.py:371
  52.4 7.4 %collective-permute-start.6 = (bf16[168,384]{1,0:T(8,128)(2,1)S(1)}, bf16[168,384]{1,0:T(8,128)(2,1)S(1)}, u32[]{:S(2)}, u32[]{:S(2)}) collective-permute-start(bf16[168,384]{1,0:T(8,128)(2,1)S(1)} %get-tuple-element.57), channel_id=1, source_target_pairs={{0,1},{1,0},{2,3},{3,2},{4,5},{5,4},{6,7},{7,6},{8,9},{9,8},{10,11... | collective-permute-start | bytes 387080 | tf_op jit(solution)/shard_map/ppermute | solution.py:371
  52.5 9.7 %collective-permute-start.4 = (bf16[168,384]{1,0:T(8,128)(2,1)S(1)}, bf16[168,384]{1,0:T(8,128)(2,1)S(1)}, u32[]{:S(2)}, u32[]{:S(2)}) collective-permute-start(bf16[168,384]{1,0:T(8,128)(2,1)S(1)} %get-tuple-element.51), channel_id=1, source_target_pairs={{0,2},{1,3},{2,0},{3,1},{4,6},{5,7},{6,4},{7,5},{8,10},{9,11},{10,... | collective-permute-start | bytes 387080 | tf_op jit(solution)/shard_map/ppermute | solution.py:371
  54.4 10.0 %collective-permute-start.5 = (bf16[168,384]{1,0:T(8,128)(2,1)S(1)}, bf16[168,384]{1,0:T(8,128)(2,1)S(1)}, u32[]{:S(2)}, u32[]{:S(2)}) collective-permute-start(bf16[168,384]{1,0:T(8,128)(2,1)S(1)} %get-tuple-element.52), channel_id=1, source_target_pairs={{0,1},{1,0},{2,3},{3,2},{4,5},{5,4},{6,7},{7,6},{8,9},{9,8},{10,11... | collective-permute-start | bytes 387080 | tf_op jit(solution)/shard_map/ppermute | solution.py:371
  59.8 8.7 %collective-permute-start.7 = (bf16[168,384]{1,0:T(8,128)(2,1)S(1)}, bf16[168,384]{1,0:T(8,128)(2,1)S(1)}, u32[]{:S(2)}, u32[]{:S(2)}) collective-permute-start(bf16[168,384]{1,0:T(8,128)(2,1)S(1)} %shard_map.141), channel_id=1, source_target_pairs={{0,2},{1,3},{2,0},{3,1},{4,6},{5,7},{6,4},{7,5},{8,10},{9,11},{10,... | collective-permute-start | bytes 387080 | tf_op jit(solution)/shard_map/ppermute | solution.py:371
  59.9 9.9 %collective-permute-start.8 = (bf16[168,384]{1,0:T(8,128)(2,1)S(1)}, bf16[168,384]{1,0:T(8,128)(2,1)S(1)}, u32[]{:S(2)}, u32[]{:S(2)}) collective-permute-start(bf16[168,384]{1,0:T(8,128)(2,1)S(1)} %get-tuple-element.59), channel_id=1, source_target_pairs={{0,1},{1,0},{2,3},{3,2},{4,5},{5,4},{6,7},{7,6},{8,9},{9,8},{10,11... | collective-permute-start | bytes 387080 | tf_op jit(solution)/shard_map/ppermute | solution.py:371
  65.2 8.9 %collective-permute-start.10 = (bf16[168,384]{1,0:T(8,128)(2,1)S(1)}, bf16[168,384]{1,0:T(8,128)(2,1)S(1)}, u32[]{:S(2)}, u32[]{:S(2)}) collective-permute-start(bf16[168,384]{1,0:T(8,128)(2,1)S(1)} %get-tuple-element.53.p0.refs_0_), channel_id=1, source_target_pairs={{0,2},{1,3},{2,0},{3,1},{4,6},{5,7},{6,4},{7,5},{8,10},{9,11},{10,... | collective-permute-start | bytes 387080 | tf_op jit(solution)/shard_map/ppermute | solution.py:371
  65.2 10.1 %collective-permute-start.9 = (bf16[168,384]{1,0:T(8,128)(2,1)S(1)}, bf16[168,384]{1,0:T(8,128)(2,1)S(1)}, u32[]{:S(2)}, u32[]{:S(2)}) collective-permute-start(bf16[168,384]{1,0:T(8,128)(2,1)S(1)} %get-tuple-element.53.p0.refs_0_), channel_id=1, source_target_pairs={{0,1},{1,0},{2,3},{3,2},{4,5},{5,4},{6,7},{7,6},{8,9},{9,8},{10,11... | collective-permute-start | bytes 387080 | tf_op jit(solution)/shard_map/ppermute | solution.py:371
  70.6 9.1 %collective-permute-start.13 = (bf16[168,384]{1,0:T(8,128)(2,1)S(1)}, bf16[168,384]{1,0:T(8,128)(2,1)S(1)}, u32[]{:S(2)}, u32[]{:S(2)}) collective-permute-start(bf16[168,384]{1,0:T(8,128)(2,1)S(1)} %get-tuple-element.65.p0.refs_5_), channel_id=1, source_target_pairs={{0,2},{1,3},{2,0},{3,1},{4,6},{5,7},{6,4},{7,5},{8,10},{9,11},{10,... | collective-permute-start | bytes 387080 | tf_op jit(solution)/shard_map/ppermute | solution.py:371
  74.1 6.2 %collective-permute-start.11 = (bf16[168,384]{1,0:T(8,128)(2,1)S(1)}, bf16[168,384]{1,0:T(8,128)(2,1)S(1)}, u32[]{:S(2)}, u32[]{:S(2)}) collective-permute-start(bf16[168,384]{1,0:T(8,128)(2,1)S(1)} %collective-permute-done.10.p2.refs_2_), channel_id=1, source_target_pairs={{0,1},{1,0},{2,3},{3,2},{4,5},{5,4},{6,7},{7,6},{8,9},{9,8},{10,11... | collective-permute-start | bytes 387080 | tf_op jit(solution)/shard_map/ppermute | solution.py:371
  75.3 7.7 %collective-permute-start.12 = (bf16[168,384]{1,0:T(8,128)(2,1)S(1)}, bf16[168,384]{1,0:T(8,128)(2,1)S(1)}, u32[]{:S(2)}, u32[]{:S(2)}) collective-permute-start(bf16[168,384]{1,0:T(8,128)(2,1)S(1)} %get-tuple-element.65.p0.refs_5_), channel_id=1, source_target_pairs={{0,1},{1,0},{2,3},{3,2},{4,5},{5,4},{6,7},{7,6},{8,9},{9,8},{10,11... | collective-permute-start | bytes 387080 | tf_op jit(solution)/shard_map/ppermute | solution.py:371
  79.6 6.2 %collective-permute-start.14 = (bf16[168,384]{1,0:T(8,128)(2,1)S(1)}, bf16[168,384]{1,0:T(8,128)(2,1)S(1)}, u32[]{:S(2)}, u32[]{:S(2)}) collective-permute-start(bf16[168,384]{1,0:T(8,128)(2,1)S(1)} %collective-permute-done.13.p2.refs_7_), channel_id=1, source_target_pairs={{0,1},{1,0},{2,3},{3,2},{4,5},{5,4},{6,7},{7,6},{8,9},{9,8},{10,11... | collective-permute-start | bytes 387080 | tf_op jit(solution)/shard_map/ppermute | solution.py:371
  85.8 4.7 %copy-start.7 = (bf16[1664,176]{1,0:T(8,128)(2,1)S(1)}, bf16[1664,176]{1,0:T(8,128)(2,1)}, u32[]{:S(2)}) copy-start(bf16[1664,176]{1,0:T(8,128)(2,1)} %constant.8.clone.unpacker) | copy-start | bytes 1757188
  87.0 3.5 %collective-permute-start.15 = (bf16[176,1536]{1,0:T(8,128)(2,1)S(1)}, bf16[176,1536]{1,0:T(8,128)(2,1)S(1)}, u32[]{:S(2)}, u32[]{:S(2)}) collective-permute-start(bf16[176,1536]{1,0:T(8,128)(2,1)S(1)} %get-tuple-element.69), channel_id=1, source_target_pairs={{0,4},{4,0},{1,5},{5,1},{2,6},{6,2},{3,7},{7,3},{8,12},{12,8},{9,1... | collective-permute-start | bytes 1622024 | tf_op jit(solution)/shard_map/ppermute | solution.py:371
  106.7 7.8 %collective-permute-start.16 = (bf16[16,1536]{1,0:T(8,128)(2,1)S(1)}, bf16[16,1536]{1,0:T(8,128)(2,1)S(1)}, u32[]{:S(2)}, u32[]{:S(2)}) collective-permute-start(bf16[16,1536]{1,0:T(8,128)(2,1)S(1)} %get-tuple-element.73), channel_id=1, source_target_pairs={{0,128},{128,0},{1,129},{129,1},{2,130},{130,2},{3,131},{131,3},{4... | collective-permute-start | bytes 147464 | tf_op jit(solution)/shard_map/ppermute | solution.py:371

commit v7 on v6

--- a/solution.py
+++ b/solution.py
@@ -110,10 +110,10 @@
 
 
 def project_kernel(
-    width, share, has_own, block, gate_w, up_w, down_w, router_w, packer, own_block,
-    own, send1, send2, send3, chosen, notes,
+    width, share, has_own, steps, block, gate_w, up_w, down_w, router_w, packer, own_block,
+    *refs,
 ):
-    t = lax.axis_index("t")
+    sends, (own, chosen, notes) = refs[:-3], refs[-3:]
     slots, quarter = packer.shape[0] // 11, width // 4
     extra = block[:, width : width + quarter]
 
@@ -137,12 +137,31 @@
         notes[:, 2 * share : 2 * share + 16] = high + pltpu.roll(logits - high, 4, 0)
     own[:slots, 3 * share :] = toward
     own[slots:, 3 * share :] = jnp.zeros((8, 128), F32)
-    for step, out in enumerate((own, send1, send2, send3)):
-        rows_of = pl.ds(pl.multiple_of((t ^ step) * share, share), share)
-        both = jnp.concatenate([gate_w[rows_of, :], up_w[rows_of, :]], 0)
-        out[:slots, : 2 * share] = matmul(x_slot, both, NT).astype(out.dtype)
-        out[:slots, 2 * share : 3 * share] = matmul(g_slot, down_w[rows_of, :], NT).astype(out.dtype)
+    own[slots:, : 3 * share] = notes[...]
+    for step, out in zip(steps, sends):
+        partial_step(share, step, x_slot, g_slot, gate_w, up_w, down_w, out)
         out[slots:, : 3 * share] = notes[...].astype(out.dtype)
+    if len(steps) == 3:
+        partial_step(share, 0, x_slot, g_slot, gate_w, up_w, down_w, own)
+
+
+def partial_step(share, step, x_slot, g_slot, gate_w, up_w, down_w, out):
+    t, slots = lax.axis_index("t"), x_slot.shape[0]
+    rows_of = pl.ds(pl.multiple_of((t ^ step) * share, share), share)
+    both = jnp.concatenate([gate_w[rows_of, :], up_w[rows_of, :]], 0)
+    out[:slots, : 2 * share] = matmul(x_slot, both, NT).astype(out.dtype)
+    out[:slots, 2 * share : 3 * share] = matmul(g_slot, down_w[rows_of, :], NT).astype(out.dtype)
+
+
+def rest_kernel(share, begun, chosen, gate_w, up_w, down_w, send2, send1, own):
+    slots = chosen.shape[0] // 2
+    x_slot, g_slot = chosen[:slots], chosen[slots:]
+    own[:slots, 3 * share :] = begun[:slots, 3 * share :]
+    own[slots:, :] = begun[slots:, :]
+    for step, out in ((2, send2), (1, send1), (0, own)):
+        partial_step(share, step, x_slot, g_slot, gate_w, up_w, down_w, out)
+        if step:
+            out[slots:, :] = begun[slots:, : 3 * share].astype(out.dtype)
 
 
 def relay_kernel(slots, share, held, got, out):
@@ -425,16 +444,25 @@
     halves = []
     for index, block in enumerate((near, far)):
         if index == 1:
-            block, _ = lax.optimization_barrier((block, halves[0][2]))
-        mine, *sends, taken = call(
-            functools.partial(project_kernel, width, share, index == 0),
+            block, _ = lax.optimization_barrier((block, halves[0][0]))
+        steps = (1, 2, 3) if index else (3,)
+        types = (BF, F32, BF) if index else (BF,)
+        *sends, mine, taken = call(
+            functools.partial(project_kernel, width, share, index == 0, steps),
             [block, gate_weight, up_weight, down_weight, router_tall, packer, own_block],
-            [((height, 3 * share + 128), F32)]
-            + [((height, 3 * share), BF), ((height, 3 * share), F32 if index else BF)]
-            + [((height, 3 * share), BF), ((2 * slots, width), BF)],
-            2 * slots * width * (3 * hidden + 4 * slots),
+            [((height, 3 * share), dtype) for dtype in types]
+            + [((height, 3 * share + 128), F32), ((2 * slots, width), BF)],
+            2 * slots * width * (3 * share * len(steps) + 4 * slots),
             [pltpu.VMEM((8, 3 * share), F32)],
         )
+        if index == 0:
+            later = call(
+                functools.partial(rest_kernel, share),
+                [mine, taken, gate_weight, up_weight, down_weight],
+                [((height, 3 * share), BF)] * 2 + [((height, 3 * share + 128), F32)],
+                2 * slots * width * 9 * share,
+            )
+            sends, mine = [later[1], later[0], sends[0]], later[2]
         if index == 0:
             got = [exchange(sends[step - 1], "t", step) for step in (3, 2, 1)]
         else:

time: 116 us -> 114 us (0.983)
  waiting for transfers between devices: 26.9 us -> 23 us
  starting transfers between devices: 29.4 us -> 31.4 us
    ppermute x16, waiting for transfers between devices: 26 us -> 22.1 us  [exchange(): return lax.ppermute(value, axis, [(k, k ^ step) for k in range(count)])]
    ppermute x16, starting transfers between devices: 23 us -> 25 us  [exchange(): return lax.ppermute(value, axis, [(k, k ^ step) for k in range(count)])]
    pallas_call x13 -> x14, Pallas kernels: 14.5 us -> 14.7 us  [call(): pl.pallas_call(body, in_specs=[VMEM] * len(ins), out_specs=[out_spec] * l...]
  transfers between devices with their start and end apart: 17 -> 17, of which waited for: 14 -> 10; matrix products, arithmetic and copies ran while one was open for 1% -> 1% of each run, Pallas kernels for 10% -> 10%
where the time goes in v7:
time: 114 us
  blocking collectives  38 us (33%)
  starting transfers between devices  31.4 us (28%)
  waiting for transfers between devices  23 us (20%)
  Pallas kernels  14.7 us (13%)
  local copies, waits for them, and re-layouts  4.38 us (4%)
  other arithmetic  1.5 us (1%)
    ppermute x16, starting transfers between devices, exchange(): return lax.ppermute(value, axis, [(k, k ^ step) for k in range(count)])  25 us
    all_to_all x1, blocking collectives, shards(): near = lax.all_to_all(chosen, 'p', 0, 0).reshape(CHIPS * SENT_ROWS, -1)  22.6 us
    ppermute x16, waiting for transfers between devices, exchange(): return lax.ppermute(value, axis, [(k, k ^ step) for k in range(count)])  22.1 us
    all_to_all x1, blocking collectives, shards(): got = lax.all_to_all(pair.reshape(CHIPS, BACK_ROWS, -1), 'p', 0, 0)  15.4 us
    pallas_call x14, Pallas kernels, call(): pl.pallas_call(body, in_specs=[VMEM] * len(ins), out_specs=[out_spec] * l...  14.7 us
    ppermute x1, starting transfers between devices, shards(): lax.ppermute(stash[0], ('p', 'c'), [(k, places - 1 - k) for k in range(pl...  6.41 us
    unnamed x18, local copies, waits for them, and re-layouts  4.25 us
  transfers between devices with their start and end apart: 17, of which 10 were waited for; matrix products, arithmetic and copies ran while one was open for 1% of the time, Pallas kernels for 10%

profile of v7, /device:TPU:1, one launch (start us, length us, event | category | flops | bytes accessed | tf_op | source)
XLA Modules:
  0.0 113.8 jit_solution(13649138975366619944)
XLA Ops:
  0.6 6.4 %collective-permute-start = (bf16[8,1536]{1,0:T(8,128)(2,1)}, bf16[8,1536]{1,0:T(8,128)(2,1)S(1)}, u32[]{:S(2)}, u32[]{:S(2)}) collective-permute-start(bf16[8,1536]{1,0:T(8,128)(2,1)} %bitcast.11), channel_id=1, source_target_pairs={{0,124},{4,120},{8,116},{12,112},{16,108},{20,104},{24,100},{28,96... | collective-permute-start | bytes 73736 | tf_op jit(solution)/shard_map/ppermute | solution.py:429
  7.9 0.9 collective-permute-done.x
  9.5 6.9 %collective-permute-start.1 = (bf16[16,1664]{1,0:T(8,128)(2,1)S(1)}, bf16[16,1664]{1,0:T(8,128)(2,1)S(1)}, u32[]{:S(2)}, u32[]{:S(2)}) collective-permute-start(bf16[16,1664]{1,0:T(8,128)(2,1)S(1)} %fusion.1.mine), channel_id=1, source_target_pairs={{0,128},{128,0},{1,129},{129,1},{2,130},{130,2},{3,131},{131,3},{4... | collective-permute-start | bytes 159752 | tf_op jit(solution)/shard_map/ppermute | solution.py:390
  16.4 1.4 %copy-done = bf16[512,1536]{1,0:T(8,128)(2,1)S(1)} copy-done((bf16[512,1536]{1,0:T(8,128)(2,1)S(1)}, bf16[512,1536]{1,0:T(8,128)(2,1)}, u32[]{:S(2)}) %copy-start) | copy-done | bytes 1572888
  17.8 1.4 %copy-done.2 = bf16[512,1536]{1,0:T(8,128)(2,1)S(1)} copy-done((bf16[512,1536]{1,0:T(8,128)(2,1)S(1)}, bf16[512,1536]{1,0:T(8,128)(2,1)}, u32[]{:S(2)}) %copy-start.2) | copy-done | bytes 1572888
  19.2 1.4 %copy-done.4 = bf16[512,1536]{1,0:T(8,128)(2,1)S(1)} copy-done((bf16[512,1536]{1,0:T(8,128)(2,1)S(1)}, bf16[512,1536]{1,0:T(8,128)(2,1)}, u32[]{:S(2)}) %copy-start.4) | copy-done | bytes 1572888
  21.2 22.6 %all_to_all.10 = bf16[16,16,2048]{2,1,0:T(8,128)(2,1)S(1)} all-to-all(bf16[16,16,2048]{2,1,0:T(8,128)(2,1)S(1)} %get-tuple-element.45), channel_id=1, replica_groups=mesh['h'=2,'p'=16,'c'=2,'t'=4] {'p'}, dimensions={0} | all-to-all | bytes 2097152 | tf_op jit(solution)/shard_map/all_to_all | solution.py:441
  43.8 2.0 %collective-permute-start.2 = (bf16[256,2048]{1,0:T(8,128)(2,1)S(1)}, bf16[256,2048]{1,0:T(8,128)(2,1)S(1)}, u32[]{:S(2)}, u32[]{:S(2)}) collective-permute-start(bf16[256,2048]{1,0:T(8,128)(2,1)S(1)} %bitcast.7), channel_id=1, source_target_pairs={{0,4},{4,0},{1,5},{5,1},{2,6},{6,2},{3,7},{7,3},{8,12},{12,8},{9,1... | collective-permute-start | bytes 3145736 | tf_op jit(solution)/shard_map/ppermute | solution.py:390
  45.8 1.4 %shard_map.138 = (bf16[168,384]{1,0:T(8,128)(2,1)S(1)}, f32[168,512]{1,0:T(8,128)S(1)}, bf16[320,1536]{1,0:T(8,128)(2,1)S(1)}) custom-call(bf16[256,2048]{1,0:T(8,128)(2,1)S(1)} %bitcast.8, bf16[512,1536]{1,0:T(8,128)(2,1)S(1)} %copy-done.1, bf16[512,1536]{1,0:T(8,128)(2,1)S(1)} %copy-done.3, bf16[512,1536]{1,0:T(8,128)(2,1)S(1)} %copy-done.5, ...), custom_call_target="tpu_custom_call" | custom-call | flops 503316480 | bytes 7114752 | tf_op jit(solution)/shard_map/pallas_call | solution.py:375
  47.2 1.7 %collective-permute-start.3 = (bf16[168,384]{1,0:T(8,128)(2,1)S(1)}, bf16[168,384]{1,0:T(8,128)(2,1)S(1)}, u32[]{:S(2)}, u32[]{:S(2)}) collective-permute-start(bf16[168,384]{1,0:T(8,128)(2,1)S(1)} %get-tuple-element.51), channel_id=1, source_target_pairs={{0,3},{1,2},{2,1},{3,0},{4,7},{5,6},{6,5},{7,4},{8,11},{9,10},{10,... | collective-permute-start | bytes 387080 | tf_op jit(solution)/shard_map/ppermute | solution.py:390
  48.9 1.2 %shard_map.139 = (bf16[168,384]{1,0:T(8,128)(2,1)S(1)}, bf16[168,384]{1,0:T(8,128)(2,1)S(1)}, f32[168,512]{1,0:T(8,128)S(1)}) custom-call(f32[168,512]{1,0:T(8,128)S(1)} %get-tuple-element.46.begun, bf16[320,1536]{1,0:T(8,128)(2,1)S(1)} %get-tuple-element.47.chosen.refs_4_, bf16[512,1536]{1,0:T(8,128)(2,1)S(1)} %copy-done.1, ...), custom_call_target="tpu_custom_call" | custom-call | flops 566231040 | bytes 6045696 | tf_op jit(solution)/shard_map/pallas_call | solution.py:375
  50.1 2.4 %shard_map.140 = (bf16[168,384]{1,0:T(8,128)(2,1)S(1)}, f32[168,384]{1,0:T(8,128)S(1)}, bf16[168,384]{1,0:T(8,128)(2,1)S(1)}, f32[168,512]{1,0:T(8,128)S(1)}, bf16[320,1536]{1,0:T(8,128)(2,1)S(1)}) custom-call(bf16[256,2048]{1,0:T(8,128)(2,1)S(1)} %collective-permute-done.2.block, bf16[512,1536]{1,0:T(8,128)(2,1)S(1)} %copy-done.1, ...), custom_call_target="tpu_custom_call" | custom-call | flops 880803840 | bytes 7114752 | tf_op jit(solution)/shard_map/pallas_call | solution.py:375
  52.6 1.9 %collective-permute-start.4 = (bf16[168,384]{1,0:T(8,128)(2,1)S(1)}, bf16[168,384]{1,0:T(8,128)(2,1)S(1)}, u32[]{:S(2)}, u32[]{:S(2)}) collective-permute-start(bf16[168,384]{1,0:T(8,128)(2,1)S(1)} %get-tuple-element.53), channel_id=1, source_target_pairs={{0,2},{1,3},{2,0},{3,1},{4,6},{5,7},{6,4},{7,5},{8,10},{9,11},{10,... | collective-permute-start | bytes 387080 | tf_op jit(solution)/shard_map/ppermute | solution.py:390
  54.6 4.7 %collective-permute-done.6.got = bf16[168,384]{1,0:T(8,128)(2,1)S(1)} collective-permute-done((bf16[168,384]{1,0:T(8,128)(2,1)S(1)}, bf16[168,384]{1,0:T(8,128)(2,1)S(1)}, u32[]{:S(2)}, u32[]{:S(2)}) %collective-permute-start.6) | collective-permute-done | bytes 129056 | tf_op jit(solution)/shard_map/ppermute | solution.py:390
  59.5 1.9 %collective-permute-start.8 = (bf16[168,384]{1,0:T(8,128)(2,1)S(1)}, bf16[168,384]{1,0:T(8,128)(2,1)S(1)}, u32[]{:S(2)}, u32[]{:S(2)}) collective-permute-start(bf16[168,384]{1,0:T(8,128)(2,1)S(1)} %get-tuple-element.61), channel_id=1, source_target_pairs={{0,1},{1,0},{2,3},{3,2},{4,5},{5,4},{6,7},{7,6},{8,9},{9,8},{10,11... | collective-permute-start | bytes 387080 | tf_op jit(solution)/shard_map/ppermute | solution.py:390
  61.4 1.5 %collective-permute-done.5.refs_2_ = bf16[168,384]{1,0:T(8,128)(2,1)S(1)} collective-permute-done((bf16[168,384]{1,0:T(8,128)(2,1)S(1)}, bf16[168,384]{1,0:T(8,128)(2,1)S(1)}, u32[]{:S(2)}, u32[]{:S(2)}) %collective-permute-start.5) | collective-permute-done | bytes 129056 | tf_op jit(solution)/shard_map/ppermute | solution.py:390
  62.9 0.8 shard_map.141
  64.4 1.2 %collective-permute-start.9 = (bf16[168,384]{1,0:T(8,128)(2,1)S(1)}, bf16[168,384]{1,0:T(8,128)(2,1)S(1)}, u32[]{:S(2)}, u32[]{:S(2)}) collective-permute-start(bf16[168,384]{1,0:T(8,128)(2,1)S(1)} %get-tuple-element.55.p0.refs_0_), channel_id=1, source_target_pairs={{0,1},{1,0},{2,3},{3,2},{4,5},{5,4},{6,7},{7,6},{8,9},{9,8},{10,11... | collective-permute-start | bytes 387080 | tf_op jit(solution)/shard_map/ppermute | solution.py:390
  65.6 2.2 %collective-permute-done.7.refs_0_ = bf16[168,384]{1,0:T(8,128)(2,1)S(1)} collective-permute-done((bf16[168,384]{1,0:T(8,128)(2,1)S(1)}, bf16[168,384]{1,0:T(8,128)(2,1)S(1)}, u32[]{:S(2)}, u32[]{:S(2)}) %collective-permute-start.7) | collective-permute-done | bytes 129056 | tf_op jit(solution)/shard_map/ppermute | solution.py:390
  68.5 1.2 %collective-permute-start.13 = (bf16[168,384]{1,0:T(8,128)(2,1)S(1)}, bf16[168,384]{1,0:T(8,128)(2,1)S(1)}, u32[]{:S(2)}, u32[]{:S(2)}) collective-permute-start(bf16[168,384]{1,0:T(8,128)(2,1)S(1)} %get-tuple-element.67.p0.refs_5_), channel_id=1, source_target_pairs={{0,2},{1,3},{2,0},{3,1},{4,6},{5,7},{6,4},{7,5},{8,10},{9,11},{10,... | collective-permute-start | bytes 387080 | tf_op jit(solution)/shard_map/ppermute | solution.py:390
  69.7 3.6 %collective-permute-done.10.p2.refs_2_ = bf16[168,384]{1,0:T(8,128)(2,1)S(1)} collective-permute-done((bf16[168,384]{1,0:T(8,128)(2,1)S(1)}, bf16[168,384]{1,0:T(8,128)(2,1)S(1)}, u32[]{:S(2)}, u32[]{:S(2)}) %collective-permute-start.10) | collective-permute-done | bytes 129056 | tf_op jit(solution)/shard_map/ppermute | solution.py:390
  73.3 1.5 %collective-permute-start.12 = (bf16[168,384]{1,0:T(8,128)(2,1)S(1)}, bf16[168,384]{1,0:T(8,128)(2,1)S(1)}, u32[]{:S(2)}, u32[]{:S(2)}) collective-permute-start(bf16[168,384]{1,0:T(8,128)(2,1)S(1)} %get-tuple-element.67.p0.refs_5_), channel_id=1, source_target_pairs={{0,1},{1,0},{2,3},{3,2},{4,5},{5,4},{6,7},{7,6},{8,9},{9,8},{10,11... | collective-permute-start | bytes 387080 | tf_op jit(solution)/shard_map/ppermute | solution.py:390
  74.8 4.1 %collective-permute-done.13.p2.refs_7_ = bf16[168,384]{1,0:T(8,128)(2,1)S(1)} collective-permute-done((bf16[168,384]{1,0:T(8,128)(2,1)S(1)}, bf16[168,384]{1,0:T(8,128)(2,1)S(1)}, u32[]{:S(2)}, u32[]{:S(2)}) %collective-permute-start.13) | collective-permute-done | bytes 129056 | tf_op jit(solution)/shard_map/ppermute | solution.py:390
  78.9 1.2 %shard_map.144 = (f32[160,1536]{1,0:T(8,128)S(1)}, f32[8,1536]{1,0:T(8,128)S(1)}) custom-call(bf16[168,384]{1,0:T(8,128)(2,1)S(1)} %get-tuple-element.55.p0.refs_0_, bf16[168,384]{1,0:T(8,128)(2,1)S(1)} %collective-permute-done.9.p1.refs_1_, bf16[168,384]{1,0:T(8,128)(2,1)S(1)} %collective-permute-done.10.p2.refs_2_, ...), custom_call_target="tpu_custom_call" | custom-call | flops 503316480 | bytes 5181440 | tf_op jit(solution)/shard_map/pallas_call | solution.py:375
  80.9 3.5 %collective-permute-done.14.p3.refs_8_ = bf16[168,384]{1,0:T(8,128)(2,1)S(1)} collective-permute-done((bf16[168,384]{1,0:T(8,128)(2,1)S(1)}, bf16[168,384]{1,0:T(8,128)(2,1)S(1)}, u32[]{:S(2)}, u32[]{:S(2)}) %collective-permute-start.14) | collective-permute-done | bytes 129056 | tf_op jit(solution)/shard_map/ppermute | solution.py:390
  84.4 1.2 %shard_map.145 = (bf16[176,1536]{1,0:T(8,128)(2,1)S(1)}, f32[8,1536]{1,0:T(8,128)S(1)}) custom-call(bf16[168,384]{1,0:T(8,128)(2,1)S(1)} %get-tuple-element.67.p0.refs_5_, bf16[168,384]{1,0:T(8,128)(2,1)S(1)} %collective-permute-done.12.p1.refs_6_, bf16[168,384]{1,0:T(8,128)(2,1)S(1)} %collective-permute-done.13.p2.refs_7_, ...), custom_call_target="tpu_custom_call" | custom-call | flops 503316480 | bytes 5169152 | tf_op jit(solution)/shard_map/pallas_call | solution.py:375
  85.6 2.4 %collective-permute-start.15 = (bf16[176,1536]{1,0:T(8,128)(2,1)S(1)}, bf16[176,1536]{1,0:T(8,128)(2,1)S(1)}, u32[]{:S(2)}, u32[]{:S(2)}) collective-permute-start(bf16[176,1536]{1,0:T(8,128)(2,1)S(1)} %get-tuple-element.71), channel_id=1, source_target_pairs={{0,4},{4,0},{1,5},{5,1},{2,6},{6,2},{3,7},{7,3},{8,12},{12,8},{9,1... | collective-permute-start | bytes 1622024 | tf_op jit(solution)/shard_map/ppermute | solution.py:390
  87.9 1.6 %collective-permute-done.15.got = bf16[176,1536]{1,0:T(8,128)(2,1)S(1)} collective-permute-done((bf16[176,1536]{1,0:T(8,128)(2,1)S(1)}, bf16[176,1536]{1,0:T(8,128)(2,1)S(1)}, u32[]{:S(2)}, u32[]{:S(2)}) %collective-permute-start.15) | collective-permute-done | bytes 540704 | tf_op jit(solution)/shard_map/ppermute | solution.py:390
  90.2 15.4 %all_to_all.11.got = bf16[16,8,2688]{2,1,0:T(8,128)(2,1)S(1)} all-to-all(bf16[16,8,2688]{2,1,0:T(8,128)(2,1)S(1)} %bitcast.9), channel_id=1, replica_groups=mesh['h'=2,'p'=16,'c'=2,'t'=4] {'p'}, dimensions={0} | all-to-all | bytes 1376256 | tf_op jit(solution)/shard_map/all_to_all | solution.py:517
  105.7 3.3 %collective-permute-start.16 = (bf16[16,1536]{1,0:T(8,128)(2,1)S(1)}, bf16[16,1536]{1,0:T(8,128)(2,1)S(1)}, u32[]{:S(2)}, u32[]{:S(2)}) collective-permute-start(bf16[16,1536]{1,0:T(8,128)(2,1)S(1)} %get-tuple-element.75), channel_id=1, source_target_pairs={{0,128},{128,0},{1,129},{129,1},{2,130},{130,2},{3,131},{131,3},{4... | collective-permute-start | bytes 147464 | tf_op jit(solution)/shard_map/ppermute | solution.py:390
  109.1 3.5 %shard_map.149 = (bf16[512,1536]{1,0:T(8,128)(2,1)}, bf16[512,1536]{1,0:T(8,128)(2,1)}, bf16[512,1536]{1,0:T(8,128)(2,1)}) custom-call(bf16[168,384]{1,0:T(8,128)(2,1)S(1)} %get-tuple-element.55.p0.refs_0_, bf16[168,384]{1,0:T(8,128)(2,1)S(1)} %collective-permute-done.9.p1.refs_1_, bf16[168,384]{1,0:T(8,128)(2,1)S(1)} %collective-permute-done.10.p2.refs_2_, ...), custom_call_target="tpu_custom_call" | custom-call | flops 1509949440 | bytes 2998272 | tf_op jit(solution)/shard_map/pallas_call | solution.py:375
  112.8 1.0 shard_map.148
  (41 shorter events, 5.6 us)
Async XLA Ops:
  0.6 8.1 %collective-permute-start = (bf16[8,1536]{1,0:T(8,128)(2,1)}, bf16[8,1536]{1,0:T(8,128)(2,1)S(1)}, u32[]{:S(2)}, u32[]{:S(2)}) collective-permute-start(bf16[8,1536]{1,0:T(8,128)(2,1)} %bitcast.11), channel_id=1, source_target_pairs={{0,124},{4,120},{8,116},{12,112},{16,108},{20,104},{24,100},{28,96... | collective-permute-start | bytes 73736 | tf_op jit(solution)/shard_map/ppermute | solution.py:429
  9.5 11.2 %collective-permute-start.1 = (bf16[16,1664]{1,0:T(8,128)(2,1)S(1)}, bf16[16,1664]{1,0:T(8,128)(2,1)S(1)}, u32[]{:S(2)}, u32[]{:S(2)}) collective-permute-start(bf16[16,1664]{1,0:T(8,128)(2,1)S(1)} %fusion.1.mine), channel_id=1, source_target_pairs={{0,128},{128,0},{1,129},{129,1},{2,130},{130,2},{3,131},{131,3},{4... | collective-permute-start | bytes 159752 | tf_op jit(solution)/shard_map/ppermute | solution.py:390
  16.4 1.4 %copy-start = (bf16[512,1536]{1,0:T(8,128)(2,1)S(1)}, bf16[512,1536]{1,0:T(8,128)(2,1)}, u32[]{:S(2)}) copy-start(bf16[512,1536]{1,0:T(8,128)(2,1)} %gate_w.11) | copy-start | bytes 4718596
  17.8 1.4 %copy-start.2 = (bf16[512,1536]{1,0:T(8,128)(2,1)S(1)}, bf16[512,1536]{1,0:T(8,128)(2,1)}, u32[]{:S(2)}) copy-start(bf16[512,1536]{1,0:T(8,128)(2,1)} %up_w.11) | copy-start | bytes 4718596
  19.2 1.4 %copy-start.4 = (bf16[512,1536]{1,0:T(8,128)(2,1)S(1)}, bf16[512,1536]{1,0:T(8,128)(2,1)}, u32[]{:S(2)}) copy-start(bf16[512,1536]{1,0:T(8,128)(2,1)} %down_w.7) | copy-start | bytes 4718596
  20.6 25.1 %copy-start.8 = (bf16[4,1536]{1,0:T(4,128)(2,1)S(1)}, bf16[4,1536]{1,0:T(4,128)(2,1)}, u32[]{:S(2)}) copy-start(bf16[4,1536]{1,0:T(4,128)(2,1)} %param.11) | copy-start | bytes 36868
  20.6 25.1 %copy-start.3 = (bf16[512,1536]{1,0:T(8,128)(2,1)S(1)}, bf16[512,1536]{1,0:T(8,128)(2,1)}, u32[]{:S(2)}) copy-start(bf16[512,1536]{1,0:T(8,128)(2,1)} %up_w.11) | copy-start | bytes 4718596
  20.6 25.1 %copy-start.5 = (bf16[512,1536]{1,0:T(8,128)(2,1)S(1)}, bf16[512,1536]{1,0:T(8,128)(2,1)}, u32[]{:S(2)}) copy-start(bf16[512,1536]{1,0:T(8,128)(2,1)} %down_w.7) | copy-start | bytes 4718596
  20.6 25.1 %copy-start.1 = (bf16[512,1536]{1,0:T(8,128)(2,1)S(1)}, bf16[512,1536]{1,0:T(8,128)(2,1)}, u32[]{:S(2)}) copy-start(bf16[512,1536]{1,0:T(8,128)(2,1)} %gate_w.11) | copy-start | bytes 4718596
  20.7 25.1 %copy-start.6 = (bf16[1760,256]{1,0:T(8,128)(2,1)S(1)}, bf16[1760,256]{1,0:T(8,128)(2,1)}, u32[]{:S(2)}) copy-start(bf16[1760,256]{1,0:T(8,128)(2,1)} %constant.7.clone.packer) | copy-start | bytes 2703364
  43.8 6.4 %collective-permute-start.2 = (bf16[256,2048]{1,0:T(8,128)(2,1)S(1)}, bf16[256,2048]{1,0:T(8,128)(2,1)S(1)}, u32[]{:S(2)}, u32[]{:S(2)}) collective-permute-start(bf16[256,2048]{1,0:T(8,128)(2,1)S(1)} %bitcast.7), channel_id=1, source_target_pairs={{0,4},{4,0},{1,5},{5,1},{2,6},{6,2},{3,7},{7,3},{8,12},{12,8},{9,1... | collective-permute-start | bytes 3145736 | tf_op jit(solution)/shard_map/ppermute | solution.py:390
  47.2 7.4 %collective-permute-start.3 = (bf16[168,384]{1,0:T(8,128)(2,1)S(1)}, bf16[168,384]{1,0:T(8,128)(2,1)S(1)}, u32[]{:S(2)}, u32[]{:S(2)}) collective-permute-start(bf16[168,384]{1,0:T(8,128)(2,1)S(1)} %get-tuple-element.51), channel_id=1, source_target_pairs={{0,3},{1,2},{2,1},{3,0},{4,7},{5,6},{6,5},{7,4},{8,11},{9,10},{10,... | collective-permute-start | bytes 387080 | tf_op jit(solution)/shard_map/ppermute | solution.py:390
  52.5 6.8 %collective-permute-start.6 = (bf16[168,384]{1,0:T(8,128)(2,1)S(1)}, bf16[168,384]{1,0:T(8,128)(2,1)S(1)}, u32[]{:S(2)}, u32[]{:S(2)}) collective-permute-start(bf16[168,384]{1,0:T(8,128)(2,1)S(1)} %get-tuple-element.59), channel_id=1, source_target_pairs={{0,1},{1,0},{2,3},{3,2},{4,5},{5,4},{6,7},{7,6},{8,9},{9,8},{10,11... | collective-permute-start | bytes 387080 | tf_op jit(solution)/shard_map/ppermute | solution.py:390
  52.6 8.8 %collective-permute-start.4 = (bf16[168,384]{1,0:T(8,128)(2,1)S(1)}, bf16[168,384]{1,0:T(8,128)(2,1)S(1)}, u32[]{:S(2)}, u32[]{:S(2)}) collective-permute-start(bf16[168,384]{1,0:T(8,128)(2,1)S(1)} %get-tuple-element.53), channel_id=1, source_target_pairs={{0,2},{1,3},{2,0},{3,1},{4,6},{5,7},{6,4},{7,5},{8,10},{9,11},{10,... | collective-permute-start | bytes 387080 | tf_op jit(solution)/shard_map/ppermute | solution.py:390
  54.5 8.4 %collective-permute-start.5 = (bf16[168,384]{1,0:T(8,128)(2,1)S(1)}, bf16[168,384]{1,0:T(8,128)(2,1)S(1)}, u32[]{:S(2)}, u32[]{:S(2)}) collective-permute-start(bf16[168,384]{1,0:T(8,128)(2,1)S(1)} %get-tuple-element.54), channel_id=1, source_target_pairs={{0,1},{1,0},{2,3},{3,2},{4,5},{5,4},{6,7},{7,6},{8,9},{9,8},{10,11... | collective-permute-start | bytes 387080 | tf_op jit(solution)/shard_map/ppermute | solution.py:390
  59.4 8.3 %collective-permute-start.7 = (bf16[168,384]{1,0:T(8,128)(2,1)S(1)}, bf16[168,384]{1,0:T(8,128)(2,1)S(1)}, u32[]{:S(2)}, u32[]{:S(2)}) collective-permute-start(bf16[168,384]{1,0:T(8,128)(2,1)S(1)} %shard_map.142), channel_id=1, source_target_pairs={{0,2},{1,3},{2,0},{3,1},{4,6},{5,7},{6,4},{7,5},{8,10},{9,11},{10,... | collective-permute-start | bytes 387080 | tf_op jit(solution)/shard_map/ppermute | solution.py:390
  59.5 8.2 %collective-permute-start.8 = (bf16[168,384]{1,0:T(8,128)(2,1)S(1)}, bf16[168,384]{1,0:T(8,128)(2,1)S(1)}, u32[]{:S(2)}, u32[]{:S(2)}) collective-permute-start(bf16[168,384]{1,0:T(8,128)(2,1)S(1)} %get-tuple-element.61), channel_id=1, source_target_pairs={{0,1},{1,0},{2,3},{3,2},{4,5},{5,4},{6,7},{7,6},{8,9},{9,8},{10,11... | collective-permute-start | bytes 387080 | tf_op jit(solution)/shard_map/ppermute | solution.py:390
  63.7 9.6 %collective-permute-start.10 = (bf16[168,384]{1,0:T(8,128)(2,1)S(1)}, bf16[168,384]{1,0:T(8,128)(2,1)S(1)}, u32[]{:S(2)}, u32[]{:S(2)}) collective-permute-start(bf16[168,384]{1,0:T(8,128)(2,1)S(1)} %get-tuple-element.55.p0.refs_0_), channel_id=1, source_target_pairs={{0,2},{1,3},{2,0},{3,1},{4,6},{5,7},{6,4},{7,5},{8,10},{9,11},{10,... | collective-permute-start | bytes 387080 | tf_op jit(solution)/shard_map/ppermute | solution.py:390
  64.4 9.0 %collective-permute-start.9 = (bf16[168,384]{1,0:T(8,128)(2,1)S(1)}, bf16[168,384]{1,0:T(8,128)(2,1)S(1)}, u32[]{:S(2)}, u32[]{:S(2)}) collective-permute-start(bf16[168,384]{1,0:T(8,128)(2,1)S(1)} %get-tuple-element.55.p0.refs_0_), channel_id=1, source_target_pairs={{0,1},{1,0},{2,3},{3,2},{4,5},{5,4},{6,7},{7,6},{8,9},{9,8},{10,11... | collective-permute-start | bytes 387080 | tf_op jit(solution)/shard_map/ppermute | solution.py:390
  68.5 10.4 %collective-permute-start.13 = (bf16[168,384]{1,0:T(8,128)(2,1)S(1)}, bf16[168,384]{1,0:T(8,128)(2,1)S(1)}, u32[]{:S(2)}, u32[]{:S(2)}) collective-permute-start(bf16[168,384]{1,0:T(8,128)(2,1)S(1)} %get-tuple-element.67.p0.refs_5_), channel_id=1, source_target_pairs={{0,2},{1,3},{2,0},{3,1},{4,6},{5,7},{6,4},{7,5},{8,10},{9,11},{10,... | collective-permute-start | bytes 387080 | tf_op jit(solution)/shard_map/ppermute | solution.py:390
  73.3 5.6 %collective-permute-start.11 = (bf16[168,384]{1,0:T(8,128)(2,1)S(1)}, bf16[168,384]{1,0:T(8,128)(2,1)S(1)}, u32[]{:S(2)}, u32[]{:S(2)}) collective-permute-start(bf16[168,384]{1,0:T(8,128)(2,1)S(1)} %collective-permute-done.10.p2.refs_2_), channel_id=1, source_target_pairs={{0,1},{1,0},{2,3},{3,2},{4,5},{5,4},{6,7},{7,6},{8,9},{9,8},{10,11... | collective-permute-start | bytes 387080 | tf_op jit(solution)/shard_map/ppermute | solution.py:390
  73.3 7.5 %collective-permute-start.12 = (bf16[168,384]{1,0:T(8,128)(2,1)S(1)}, bf16[168,384]{1,0:T(8,128)(2,1)S(1)}, u32[]{:S(2)}, u32[]{:S(2)}) collective-permute-start(bf16[168,384]{1,0:T(8,128)(2,1)S(1)} %get-tuple-element.67.p0.refs_5_), channel_id=1, source_target_pairs={{0,1},{1,0},{2,3},{3,2},{4,5},{5,4},{6,7},{7,6},{8,9},{9,8},{10,11... | collective-permute-start | bytes 387080 | tf_op jit(solution)/shard_map/ppermute | solution.py:390
  78.9 5.5 %collective-permute-start.14 = (bf16[168,384]{1,0:T(8,128)(2,1)S(1)}, bf16[168,384]{1,0:T(8,128)(2,1)S(1)}, u32[]{:S(2)}, u32[]{:S(2)}) collective-permute-start(bf16[168,384]{1,0:T(8,128)(2,1)S(1)} %collective-permute-done.13.p2.refs_7_), channel_id=1, source_target_pairs={{0,1},{1,0},{2,3},{3,2},{4,5},{5,4},{6,7},{7,6},{8,9},{9,8},{10,11... | collective-permute-start | bytes 387080 | tf_op jit(solution)/shard_map/ppermute | solution.py:390
  84.4 5.1 %copy-start.7 = (bf16[1664,176]{1,0:T(8,128)(2,1)S(1)}, bf16[1664,176]{1,0:T(8,128)(2,1)}, u32[]{:S(2)}) copy-start(bf16[1664,176]{1,0:T(8,128)(2,1)} %constant.8.clone.unpacker) | copy-start | bytes 1757188
  85.6 3.9 %collective-permute-start.15 = (bf16[176,1536]{1,0:T(8,128)(2,1)S(1)}, bf16[176,1536]{1,0:T(8,128)(2,1)S(1)}, u32[]{:S(2)}, u32[]{:S(2)}) collective-permute-start(bf16[176,1536]{1,0:T(8,128)(2,1)S(1)} %get-tuple-element.71), channel_id=1, source_target_pairs={{0,4},{4,0},{1,5},{5,1},{2,6},{6,2},{3,7},{7,3},{8,12},{12,8},{9,1... | collective-permute-start | bytes 1622024 | tf_op jit(solution)/shard_map/ppermute | solution.py:390
  105.7 7.0 %collective-permute-start.16 = (bf16[16,1536]{1,0:T(8,128)(2,1)S(1)}, bf16[16,1536]{1,0:T(8,128)(2,1)S(1)}, u32[]{:S(2)}, u32[]{:S(2)}) collective-permute-start(bf16[16,1536]{1,0:T(8,128)(2,1)S(1)} %get-tuple-element.75), channel_id=1, source_target_pairs={{0,128},{128,0},{1,129},{129,1},{2,130},{130,2},{3,131},{131,3},{4... | collective-permute-start | bytes 147464 | tf_op jit(solution)/shard_map/ppermute | solution.py:390

commit v8 on v7

--- a/solution.py
+++ b/solution.py
@@ -324,28 +324,31 @@
     ).astype(BF)
 
 
-def final_kernel(
-    width, experts, own, router_part, got, own_block, local, router_w, in_grad, router_grad
-):
-    h = lax.axis_index("h")
+def chosen_rows(ids, half, rows, stride):
+    row = lax.broadcasted_iota(jnp.int32, (8, 128), 0)
+    total = 0.0
+    for side in range(2):
+        match, position, _ = spots(ids, (half * 2 + side).astype(F32), row)
+        for k in range(CAP):
+            chosen = (match & (position == k)).astype(F32)[:, 0:1]
+            total += chosen * rows[stride * side + k : stride * side + k + 1]
+    return total
+
+
+def base_kernel(width, own, own_block, local, router_w, base):
     ids = own_block[:, width:].astype(F32)[:8]
-    row = lax.broadcasted_iota(jnp.int32, (8, 128), 0)
     total = own_block[8:, :width].astype(F32)
+    total += chosen_rows(ids, lax.axis_index("h"), own[...], 8)
+    high, low = split_pair(local[...])
+    rw = router_w[:16]
+    base[...] = total + matmul(high, rw, TN)[:8] + matmul(low, rw, TN)[:8]
+
+
+def final_kernel(width, experts, base, router_part, got, own_block, in_grad, router_grad):
+    ids = own_block[:, width:].astype(F32)[:8]
     other = got[...].astype(F32)
     router = router_part[...] + pltpu.roll(other, 16 - 2 * CAP, 0)[:8]
-    for step in range(2):
-        for side in range(2):
-            match, position, _ = spots(ids, ((h ^ step) * 2 + side).astype(F32), row)
-            for k in range(CAP):
-                chosen = (match & (position == k)).astype(F32)[:, 0:1]
-                if step == 0:
-                    value = own[8 * side + k : 8 * side + k + 1, :]
-                else:
-                    value = other[CAP * side + k : CAP * side + k + 1]
-                total += chosen * value
-    high, low = split_pair(local[...])
-    rw = router_w[:16]
-    total += matmul(high, rw, TN)[:8] + matmul(low, rw, TN)[:8]
+    total = base[...] + chosen_rows(ids, lax.axis_index("h") ^ 1, other, CAP)
     in_grad[...] = total.astype(BF)
     router_grad[...] = router[:experts]
 
@@ -529,9 +532,15 @@
         [pltpu.VMEM((3, ways, share, width), BF), pltpu.SemaphoreType.DMA((3, ways))],
         pl.BlockSpec(memory_space=pl.ANY),
     )
+    (base,) = call(
+        functools.partial(base_kernel, width),
+        [own_rows, own_block, local, router_tall],
+        [((tokens, width), F32)],
+        tokens * width * 30,
+    )
     in_grad, router_grad = call(
         functools.partial(final_kernel, width, experts),
-        [own_rows, router_part, exchange(sent, "h", 1), own_block, local, router_tall],
+        [base, router_part, exchange(sent, "h", 1), own_block],
         [((tokens, width), BF), ((experts, width), F32)],
         tokens * width * 50,
     )

time: 114 us -> 114 us (level)
    pallas_call x14 -> x15, Pallas kernels: 14.7 us -> 14.9 us  [call(): pl.pallas_call(body, in_specs=[VMEM] * len(ins), out_specs=[out_spec] * l...]
  transfers between devices with their start and end apart: 17 -> 17, of which waited for: 10 -> 9; matrix products, arithmetic and copies ran while one was open for 1% -> 1% of each run, Pallas kernels for 10% -> 10%
where the time goes in v8:
time: 114 us
  blocking collectives  38 us (33%)
  starting transfers between devices  31.4 us (28%)
  waiting for transfers between devices  22.8 us (20%)
  Pallas kernels  14.9 us (13%)
  local copies, waits for them, and re-layouts  4.38 us (4%)
  other arithmetic  1.5 us (1%)
    ppermute x16, starting transfers between devices, exchange(): return lax.ppermute(value, axis, [(k, k ^ step) for k in range(count)])  25 us
    all_to_all x1, blocking collectives, shards(): near = lax.all_to_all(chosen, 'p', 0, 0).reshape(CHIPS * SENT_ROWS, -1)  22.6 us
    ppermute x16, waiting for transfers between devices, exchange(): return lax.ppermute(value, axis, [(k, k ^ step) for k in range(count)])  22 us
    all_to_all x1, blocking collectives, shards(): got = lax.all_to_all(pair.reshape(CHIPS, BACK_ROWS, -1), 'p', 0, 0)  15.4 us
    pallas_call x15, Pallas kernels, call(): pl.pallas_call(body, in_specs=[VMEM] * len(ins), out_specs=[out_spec] * l...  14.9 us
    ppermute x1, starting transfers between devices, shards(): lax.ppermute(stash[0], ('p', 'c'), [(k, places - 1 - k) for k in range(pl...  6.41 us
    unnamed x18, local copies, waits for them, and re-layouts  4.25 us
  transfers between devices with their start and end apart: 17, of which 9 were waited for; matrix products, arithmetic and copies ran while one was open for 1% of the time, Pallas kernels for 10%

profile of v8, /device:TPU:1, one launch (start us, length us, event | category | flops | bytes accessed | tf_op | source)
XLA Modules:
  0.0 113.8 jit_solution(1207692559845479515)
XLA Ops:
  0.6 6.4 %collective-permute-start = (bf16[8,1536]{1,0:T(8,128)(2,1)}, bf16[8,1536]{1,0:T(8,128)(2,1)S(1)}, u32[]{:S(2)}, u32[]{:S(2)}) collective-permute-start(bf16[8,1536]{1,0:T(8,128)(2,1)} %bitcast.11), channel_id=1, source_target_pairs={{0,124},{4,120},{8,116},{12,112},{16,108},{20,104},{24,100},{28,96... | collective-permute-start | bytes 73736 | tf_op jit(solution)/shard_map/ppermute | solution.py:432
  7.9 0.9 collective-permute-done.x
  9.5 6.9 %collective-permute-start.1 = (bf16[16,1664]{1,0:T(8,128)(2,1)S(1)}, bf16[16,1664]{1,0:T(8,128)(2,1)S(1)}, u32[]{:S(2)}, u32[]{:S(2)}) collective-permute-start(bf16[16,1664]{1,0:T(8,128)(2,1)S(1)} %fusion.1.mine), channel_id=1, source_target_pairs={{0,128},{128,0},{1,129},{129,1},{2,130},{130,2},{3,131},{131,3},{4... | collective-permute-start | bytes 159752 | tf_op jit(solution)/shard_map/ppermute | solution.py:393
  16.4 1.4 %copy-done = bf16[512,1536]{1,0:T(8,128)(2,1)S(1)} copy-done((bf16[512,1536]{1,0:T(8,128)(2,1)S(1)}, bf16[512,1536]{1,0:T(8,128)(2,1)}, u32[]{:S(2)}) %copy-start) | copy-done | bytes 1572888
  17.8 1.4 %copy-done.2 = bf16[512,1536]{1,0:T(8,128)(2,1)S(1)} copy-done((bf16[512,1536]{1,0:T(8,128)(2,1)S(1)}, bf16[512,1536]{1,0:T(8,128)(2,1)}, u32[]{:S(2)}) %copy-start.2) | copy-done | bytes 1572888
  19.2 1.4 %copy-done.4 = bf16[512,1536]{1,0:T(8,128)(2,1)S(1)} copy-done((bf16[512,1536]{1,0:T(8,128)(2,1)S(1)}, bf16[512,1536]{1,0:T(8,128)(2,1)}, u32[]{:S(2)}) %copy-start.4) | copy-done | bytes 1572888
  21.2 22.6 %all_to_all.10 = bf16[16,16,2048]{2,1,0:T(8,128)(2,1)S(1)} all-to-all(bf16[16,16,2048]{2,1,0:T(8,128)(2,1)S(1)} %get-tuple-element.45), channel_id=1, replica_groups=mesh['h'=2,'p'=16,'c'=2,'t'=4] {'p'}, dimensions={0} | all-to-all | bytes 2097152 | tf_op jit(solution)/shard_map/all_to_all | solution.py:444
  43.8 2.0 %collective-permute-start.2 = (bf16[256,2048]{1,0:T(8,128)(2,1)S(1)}, bf16[256,2048]{1,0:T(8,128)(2,1)S(1)}, u32[]{:S(2)}, u32[]{:S(2)}) collective-permute-start(bf16[256,2048]{1,0:T(8,128)(2,1)S(1)} %bitcast.7), channel_id=1, source_target_pairs={{0,4},{4,0},{1,5},{5,1},{2,6},{6,2},{3,7},{7,3},{8,12},{12,8},{9,1... | collective-permute-start | bytes 3145736 | tf_op jit(solution)/shard_map/ppermute | solution.py:393
  45.8 1.4 %shard_map.138 = (bf16[168,384]{1,0:T(8,128)(2,1)S(1)}, f32[168,512]{1,0:T(8,128)S(1)}, bf16[320,1536]{1,0:T(8,128)(2,1)S(1)}) custom-call(bf16[256,2048]{1,0:T(8,128)(2,1)S(1)} %bitcast.8, bf16[512,1536]{1,0:T(8,128)(2,1)S(1)} %copy-done.1, bf16[512,1536]{1,0:T(8,128)(2,1)S(1)} %copy-done.3, bf16[512,1536]{1,0:T(8,128)(2,1)S(1)} %copy-done.5, ...), custom_call_target="tpu_custom_call" | custom-call | flops 503316480 | bytes 7114752 | tf_op jit(solution)/shard_map/pallas_call | solution.py:378
  47.2 1.7 %collective-permute-start.3 = (bf16[168,384]{1,0:T(8,128)(2,1)S(1)}, bf16[168,384]{1,0:T(8,128)(2,1)S(1)}, u32[]{:S(2)}, u32[]{:S(2)}) collective-permute-start(bf16[168,384]{1,0:T(8,128)(2,1)S(1)} %get-tuple-element.51), channel_id=1, source_target_pairs={{0,3},{1,2},{2,1},{3,0},{4,7},{5,6},{6,5},{7,4},{8,11},{9,10},{10,... | collective-permute-start | bytes 387080 | tf_op jit(solution)/shard_map/ppermute | solution.py:393
  48.9 1.2 %shard_map.139 = (bf16[168,384]{1,0:T(8,128)(2,1)S(1)}, bf16[168,384]{1,0:T(8,128)(2,1)S(1)}, f32[168,512]{1,0:T(8,128)S(1)}) custom-call(f32[168,512]{1,0:T(8,128)S(1)} %get-tuple-element.46.begun, bf16[320,1536]{1,0:T(8,128)(2,1)S(1)} %get-tuple-element.47.chosen.refs_4_, bf16[512,1536]{1,0:T(8,128)(2,1)S(1)} %copy-done.1, ...), custom_call_target="tpu_custom_call" | custom-call | flops 566231040 | bytes 6045696 | tf_op jit(solution)/shard_map/pallas_call | solution.py:378
  50.1 2.4 %shard_map.140 = (bf16[168,384]{1,0:T(8,128)(2,1)S(1)}, f32[168,384]{1,0:T(8,128)S(1)}, bf16[168,384]{1,0:T(8,128)(2,1)S(1)}, f32[168,512]{1,0:T(8,128)S(1)}, bf16[320,1536]{1,0:T(8,128)(2,1)S(1)}) custom-call(bf16[256,2048]{1,0:T(8,128)(2,1)S(1)} %collective-permute-done.2.block, bf16[512,1536]{1,0:T(8,128)(2,1)S(1)} %copy-done.1, ...), custom_call_target="tpu_custom_call" | custom-call | flops 880803840 | bytes 7114752 | tf_op jit(solution)/shard_map/pallas_call | solution.py:378
  52.6 1.9 %collective-permute-start.4 = (bf16[168,384]{1,0:T(8,128)(2,1)S(1)}, bf16[168,384]{1,0:T(8,128)(2,1)S(1)}, u32[]{:S(2)}, u32[]{:S(2)}) collective-permute-start(bf16[168,384]{1,0:T(8,128)(2,1)S(1)} %get-tuple-element.53), channel_id=1, source_target_pairs={{0,2},{1,3},{2,0},{3,1},{4,6},{5,7},{6,4},{7,5},{8,10},{9,11},{10,... | collective-permute-start | bytes 387080 | tf_op jit(solution)/shard_map/ppermute | solution.py:393
  54.6 4.7 %collective-permute-done.6.got = bf16[168,384]{1,0:T(8,128)(2,1)S(1)} collective-permute-done((bf16[168,384]{1,0:T(8,128)(2,1)S(1)}, bf16[168,384]{1,0:T(8,128)(2,1)S(1)}, u32[]{:S(2)}, u32[]{:S(2)}) %collective-permute-start.6) | collective-permute-done | bytes 129056 | tf_op jit(solution)/shard_map/ppermute | solution.py:393
  59.5 1.9 %collective-permute-start.8 = (bf16[168,384]{1,0:T(8,128)(2,1)S(1)}, bf16[168,384]{1,0:T(8,128)(2,1)S(1)}, u32[]{:S(2)}, u32[]{:S(2)}) collective-permute-start(bf16[168,384]{1,0:T(8,128)(2,1)S(1)} %get-tuple-element.61), channel_id=1, source_target_pairs={{0,1},{1,0},{2,3},{3,2},{4,5},{5,4},{6,7},{7,6},{8,9},{9,8},{10,11... | collective-permute-start | bytes 387080 | tf_op jit(solution)/shard_map/ppermute | solution.py:393
  61.4 1.5 %collective-permute-done.5.refs_2_ = bf16[168,384]{1,0:T(8,128)(2,1)S(1)} collective-permute-done((bf16[168,384]{1,0:T(8,128)(2,1)S(1)}, bf16[168,384]{1,0:T(8,128)(2,1)S(1)}, u32[]{:S(2)}, u32[]{:S(2)}) %collective-permute-start.5) | collective-permute-done | bytes 129056 | tf_op jit(solution)/shard_map/ppermute | solution.py:393
  62.9 0.8 shard_map.141
  64.4 1.2 %collective-permute-start.9 = (bf16[168,384]{1,0:T(8,128)(2,1)S(1)}, bf16[168,384]{1,0:T(8,128)(2,1)S(1)}, u32[]{:S(2)}, u32[]{:S(2)}) collective-permute-start(bf16[168,384]{1,0:T(8,128)(2,1)S(1)} %get-tuple-element.55.p0.refs_0_), channel_id=1, source_target_pairs={{0,1},{1,0},{2,3},{3,2},{4,5},{5,4},{6,7},{7,6},{8,9},{9,8},{10,11... | collective-permute-start | bytes 387080 | tf_op jit(solution)/shard_map/ppermute | solution.py:393
  65.6 2.2 %collective-permute-done.7.refs_0_ = bf16[168,384]{1,0:T(8,128)(2,1)S(1)} collective-permute-done((bf16[168,384]{1,0:T(8,128)(2,1)S(1)}, bf16[168,384]{1,0:T(8,128)(2,1)S(1)}, u32[]{:S(2)}, u32[]{:S(2)}) %collective-permute-start.7) | collective-permute-done | bytes 129056 | tf_op jit(solution)/shard_map/ppermute | solution.py:393
  68.5 1.2 %collective-permute-start.13 = (bf16[168,384]{1,0:T(8,128)(2,1)S(1)}, bf16[168,384]{1,0:T(8,128)(2,1)S(1)}, u32[]{:S(2)}, u32[]{:S(2)}) collective-permute-start(bf16[168,384]{1,0:T(8,128)(2,1)S(1)} %get-tuple-element.67.p0.refs_5_), channel_id=1, source_target_pairs={{0,2},{1,3},{2,0},{3,1},{4,6},{5,7},{6,4},{7,5},{8,10},{9,11},{10,... | collective-permute-start | bytes 387080 | tf_op jit(solution)/shard_map/ppermute | solution.py:393
  69.7 3.6 %collective-permute-done.10.p2.refs_2_ = bf16[168,384]{1,0:T(8,128)(2,1)S(1)} collective-permute-done((bf16[168,384]{1,0:T(8,128)(2,1)S(1)}, bf16[168,384]{1,0:T(8,128)(2,1)S(1)}, u32[]{:S(2)}, u32[]{:S(2)}) %collective-permute-start.10) | collective-permute-done | bytes 129056 | tf_op jit(solution)/shard_map/ppermute | solution.py:393
  73.3 1.5 %collective-permute-start.12 = (bf16[168,384]{1,0:T(8,128)(2,1)S(1)}, bf16[168,384]{1,0:T(8,128)(2,1)S(1)}, u32[]{:S(2)}, u32[]{:S(2)}) collective-permute-start(bf16[168,384]{1,0:T(8,128)(2,1)S(1)} %get-tuple-element.67.p0.refs_5_), channel_id=1, source_target_pairs={{0,1},{1,0},{2,3},{3,2},{4,5},{5,4},{6,7},{7,6},{8,9},{9,8},{10,11... | collective-permute-start | bytes 387080 | tf_op jit(solution)/shard_map/ppermute | solution.py:393
  74.8 4.1 %collective-permute-done.13.p2.refs_7_ = bf16[168,384]{1,0:T(8,128)(2,1)S(1)} collective-permute-done((bf16[168,384]{1,0:T(8,128)(2,1)S(1)}, bf16[168,384]{1,0:T(8,128)(2,1)S(1)}, u32[]{:S(2)}, u32[]{:S(2)}) %collective-permute-start.13) | collective-permute-done | bytes 129056 | tf_op jit(solution)/shard_map/ppermute | solution.py:393
  78.9 1.2 %shard_map.144 = (f32[160,1536]{1,0:T(8,128)S(1)}, f32[8,1536]{1,0:T(8,128)S(1)}) custom-call(bf16[168,384]{1,0:T(8,128)(2,1)S(1)} %get-tuple-element.55.p0.refs_0_, bf16[168,384]{1,0:T(8,128)(2,1)S(1)} %collective-permute-done.9.p1.refs_1_, bf16[168,384]{1,0:T(8,128)(2,1)S(1)} %collective-permute-done.10.p2.refs_2_, ...), custom_call_target="tpu_custom_call" | custom-call | flops 503316480 | bytes 5181440 | tf_op jit(solution)/shard_map/pallas_call | solution.py:378
  80.9 3.5 %collective-permute-done.14.p3.refs_8_ = bf16[168,384]{1,0:T(8,128)(2,1)S(1)} collective-permute-done((bf16[168,384]{1,0:T(8,128)(2,1)S(1)}, bf16[168,384]{1,0:T(8,128)(2,1)S(1)}, u32[]{:S(2)}, u32[]{:S(2)}) %collective-permute-start.14) | collective-permute-done | bytes 129056 | tf_op jit(solution)/shard_map/ppermute | solution.py:393
  84.4 1.2 %shard_map.145 = (bf16[176,1536]{1,0:T(8,128)(2,1)S(1)}, f32[8,1536]{1,0:T(8,128)S(1)}) custom-call(bf16[168,384]{1,0:T(8,128)(2,1)S(1)} %get-tuple-element.67.p0.refs_5_, bf16[168,384]{1,0:T(8,128)(2,1)S(1)} %collective-permute-done.12.p1.refs_6_, bf16[168,384]{1,0:T(8,128)(2,1)S(1)} %collective-permute-done.13.p2.refs_7_, ...), custom_call_target="tpu_custom_call" | custom-call | flops 503316480 | bytes 5169152 | tf_op jit(solution)/shard_map/pallas_call | solution.py:378
  85.6 2.4 %collective-permute-start.15 = (bf16[176,1536]{1,0:T(8,128)(2,1)S(1)}, bf16[176,1536]{1,0:T(8,128)(2,1)S(1)}, u32[]{:S(2)}, u32[]{:S(2)}) collective-permute-start(bf16[176,1536]{1,0:T(8,128)(2,1)S(1)} %get-tuple-element.71), channel_id=1, source_target_pairs={{0,4},{4,0},{1,5},{5,1},{2,6},{6,2},{3,7},{7,3},{8,12},{12,8},{9,1... | collective-permute-start | bytes 1622024 | tf_op jit(solution)/shard_map/ppermute | solution.py:393
  87.9 1.6 %collective-permute-done.15.got = bf16[176,1536]{1,0:T(8,128)(2,1)S(1)} collective-permute-done((bf16[176,1536]{1,0:T(8,128)(2,1)S(1)}, bf16[176,1536]{1,0:T(8,128)(2,1)S(1)}, u32[]{:S(2)}, u32[]{:S(2)}) %collective-permute-start.15) | collective-permute-done | bytes 540704 | tf_op jit(solution)/shard_map/ppermute | solution.py:393
  90.2 15.4 %all_to_all.11.got = bf16[16,8,2688]{2,1,0:T(8,128)(2,1)S(1)} all-to-all(bf16[16,8,2688]{2,1,0:T(8,128)(2,1)S(1)} %bitcast.9), channel_id=1, replica_groups=mesh['h'=2,'p'=16,'c'=2,'t'=4] {'p'}, dimensions={0} | all-to-all | bytes 1376256 | tf_op jit(solution)/shard_map/all_to_all | solution.py:520
  105.7 3.3 %collective-permute-start.16 = (bf16[16,1536]{1,0:T(8,128)(2,1)S(1)}, bf16[16,1536]{1,0:T(8,128)(2,1)S(1)}, u32[]{:S(2)}, u32[]{:S(2)}) collective-permute-start(bf16[16,1536]{1,0:T(8,128)(2,1)S(1)} %get-tuple-element.75), channel_id=1, source_target_pairs={{0,128},{128,0},{1,129},{129,1},{2,130},{130,2},{3,131},{131,3},{4... | collective-permute-start | bytes 147464 | tf_op jit(solution)/shard_map/ppermute | solution.py:393
  109.1 3.5 %shard_map.150 = (bf16[512,1536]{1,0:T(8,128)(2,1)}, bf16[512,1536]{1,0:T(8,128)(2,1)}, bf16[512,1536]{1,0:T(8,128)(2,1)}) custom-call(bf16[168,384]{1,0:T(8,128)(2,1)S(1)} %get-tuple-element.55.p0.refs_0_, bf16[168,384]{1,0:T(8,128)(2,1)S(1)} %collective-permute-done.9.p1.refs_1_, bf16[168,384]{1,0:T(8,128)(2,1)S(1)} %collective-permute-done.10.p2.refs_2_, ...), custom_call_target="tpu_custom_call" | custom-call | flops 1509949440 | bytes 2998272 | tf_op jit(solution)/shard_map/pallas_call | solution.py:378
  113.0 0.8 shard_map.149
  (42 shorter events, 5.9 us)
Async XLA Ops:
  0.6 8.1 %collective-permute-start = (bf16[8,1536]{1,0:T(8,128)(2,1)}, bf16[8,1536]{1,0:T(8,128)(2,1)S(1)}, u32[]{:S(2)}, u32[]{:S(2)}) collective-permute-start(bf16[8,1536]{1,0:T(8,128)(2,1)} %bitcast.11), channel_id=1, source_target_pairs={{0,124},{4,120},{8,116},{12,112},{16,108},{20,104},{24,100},{28,96... | collective-permute-start | bytes 73736 | tf_op jit(solution)/shard_map/ppermute | solution.py:432
  9.5 11.2 %collective-permute-start.1 = (bf16[16,1664]{1,0:T(8,128)(2,1)S(1)}, bf16[16,1664]{1,0:T(8,128)(2,1)S(1)}, u32[]{:S(2)}, u32[]{:S(2)}) collective-permute-start(bf16[16,1664]{1,0:T(8,128)(2,1)S(1)} %fusion.1.mine), channel_id=1, source_target_pairs={{0,128},{128,0},{1,129},{129,1},{2,130},{130,2},{3,131},{131,3},{4... | collective-permute-start | bytes 159752 | tf_op jit(solution)/shard_map/ppermute | solution.py:393
  16.4 1.4 %copy-start = (bf16[512,1536]{1,0:T(8,128)(2,1)S(1)}, bf16[512,1536]{1,0:T(8,128)(2,1)}, u32[]{:S(2)}) copy-start(bf16[512,1536]{1,0:T(8,128)(2,1)} %gate_w.11) | copy-start | bytes 4718596
  17.8 1.4 %copy-start.2 = (bf16[512,1536]{1,0:T(8,128)(2,1)S(1)}, bf16[512,1536]{1,0:T(8,128)(2,1)}, u32[]{:S(2)}) copy-start(bf16[512,1536]{1,0:T(8,128)(2,1)} %up_w.11) | copy-start | bytes 4718596
  19.2 1.4 %copy-start.4 = (bf16[512,1536]{1,0:T(8,128)(2,1)S(1)}, bf16[512,1536]{1,0:T(8,128)(2,1)}, u32[]{:S(2)}) copy-start(bf16[512,1536]{1,0:T(8,128)(2,1)} %down_w.7) | copy-start | bytes 4718596
  20.6 25.1 %copy-start.8 = (bf16[4,1536]{1,0:T(4,128)(2,1)S(1)}, bf16[4,1536]{1,0:T(4,128)(2,1)}, u32[]{:S(2)}) copy-start(bf16[4,1536]{1,0:T(4,128)(2,1)} %param.11) | copy-start | bytes 36868
  20.6 25.1 %copy-start.3 = (bf16[512,1536]{1,0:T(8,128)(2,1)S(1)}, bf16[512,1536]{1,0:T(8,128)(2,1)}, u32[]{:S(2)}) copy-start(bf16[512,1536]{1,0:T(8,128)(2,1)} %up_w.11) | copy-start | bytes 4718596
  20.6 25.1 %copy-start.5 = (bf16[512,1536]{1,0:T(8,128)(2,1)S(1)}, bf16[512,1536]{1,0:T(8,128)(2,1)}, u32[]{:S(2)}) copy-start(bf16[512,1536]{1,0:T(8,128)(2,1)} %down_w.7) | copy-start | bytes 4718596
  20.6 25.1 %copy-start.1 = (bf16[512,1536]{1,0:T(8,128)(2,1)S(1)}, bf16[512,1536]{1,0:T(8,128)(2,1)}, u32[]{:S(2)}) copy-start(bf16[512,1536]{1,0:T(8,128)(2,1)} %gate_w.11) | copy-start | bytes 4718596
  20.7 25.1 %copy-start.6 = (bf16[1760,256]{1,0:T(8,128)(2,1)S(1)}, bf16[1760,256]{1,0:T(8,128)(2,1)}, u32[]{:S(2)}) copy-start(bf16[1760,256]{1,0:T(8,128)(2,1)} %constant.7.clone.packer) | copy-start | bytes 2703364
  43.8 6.4 %collective-permute-start.2 = (bf16[256,2048]{1,0:T(8,128)(2,1)S(1)}, bf16[256,2048]{1,0:T(8,128)(2,1)S(1)}, u32[]{:S(2)}, u32[]{:S(2)}) collective-permute-start(bf16[256,2048]{1,0:T(8,128)(2,1)S(1)} %bitcast.7), channel_id=1, source_target_pairs={{0,4},{4,0},{1,5},{5,1},{2,6},{6,2},{3,7},{7,3},{8,12},{12,8},{9,1... | collective-permute-start | bytes 3145736 | tf_op jit(solution)/shard_map/ppermute | solution.py:393
  47.2 7.4 %collective-permute-start.3 = (bf16[168,384]{1,0:T(8,128)(2,1)S(1)}, bf16[168,384]{1,0:T(8,128)(2,1)S(1)}, u32[]{:S(2)}, u32[]{:S(2)}) collective-permute-start(bf16[168,384]{1,0:T(8,128)(2,1)S(1)} %get-tuple-element.51), channel_id=1, source_target_pairs={{0,3},{1,2},{2,1},{3,0},{4,7},{5,6},{6,5},{7,4},{8,11},{9,10},{10,... | collective-permute-start | bytes 387080 | tf_op jit(solution)/shard_map/ppermute | solution.py:393
  52.5 6.8 %collective-permute-start.6 = (bf16[168,384]{1,0:T(8,128)(2,1)S(1)}, bf16[168,384]{1,0:T(8,128)(2,1)S(1)}, u32[]{:S(2)}, u32[]{:S(2)}) collective-permute-start(bf16[168,384]{1,0:T(8,128)(2,1)S(1)} %get-tuple-element.59), channel_id=1, source_target_pairs={{0,1},{1,0},{2,3},{3,2},{4,5},{5,4},{6,7},{7,6},{8,9},{9,8},{10,11... | collective-permute-start | bytes 387080 | tf_op jit(solution)/shard_map/ppermute | solution.py:393
  52.6 8.8 %collective-permute-start.4 = (bf16[168,384]{1,0:T(8,128)(2,1)S(1)}, bf16[168,384]{1,0:T(8,128)(2,1)S(1)}, u32[]{:S(2)}, u32[]{:S(2)}) collective-permute-start(bf16[168,384]{1,0:T(8,128)(2,1)S(1)} %get-tuple-element.53), channel_id=1, source_target_pairs={{0,2},{1,3},{2,0},{3,1},{4,6},{5,7},{6,4},{7,5},{8,10},{9,11},{10,... | collective-permute-start | bytes 387080 | tf_op jit(solution)/shard_map/ppermute | solution.py:393
  54.5 8.4 %collective-permute-start.5 = (bf16[168,384]{1,0:T(8,128)(2,1)S(1)}, bf16[168,384]{1,0:T(8,128)(2,1)S(1)}, u32[]{:S(2)}, u32[]{:S(2)}) collective-permute-start(bf16[168,384]{1,0:T(8,128)(2,1)S(1)} %get-tuple-element.54), channel_id=1, source_target_pairs={{0,1},{1,0},{2,3},{3,2},{4,5},{5,4},{6,7},{7,6},{8,9},{9,8},{10,11... | collective-permute-start | bytes 387080 | tf_op jit(solution)/shard_map/ppermute | solution.py:393
  59.4 8.3 %collective-permute-start.7 = (bf16[168,384]{1,0:T(8,128)(2,1)S(1)}, bf16[168,384]{1,0:T(8,128)(2,1)S(1)}, u32[]{:S(2)}, u32[]{:S(2)}) collective-permute-start(bf16[168,384]{1,0:T(8,128)(2,1)S(1)} %shard_map.142), channel_id=1, source_target_pairs={{0,2},{1,3},{2,0},{3,1},{4,6},{5,7},{6,4},{7,5},{8,10},{9,11},{10,... | collective-permute-start | bytes 387080 | tf_op jit(solution)/shard_map/ppermute | solution.py:393
  59.5 8.2 %collective-permute-start.8 = (bf16[168,384]{1,0:T(8,128)(2,1)S(1)}, bf16[168,384]{1,0:T(8,128)(2,1)S(1)}, u32[]{:S(2)}, u32[]{:S(2)}) collective-permute-start(bf16[168,384]{1,0:T(8,128)(2,1)S(1)} %get-tuple-element.61), channel_id=1, source_target_pairs={{0,1},{1,0},{2,3},{3,2},{4,5},{5,4},{6,7},{7,6},{8,9},{9,8},{10,11... | collective-permute-start | bytes 387080 | tf_op jit(solution)/shard_map/ppermute | solution.py:393
  63.7 9.6 %collective-permute-start.10 = (bf16[168,384]{1,0:T(8,128)(2,1)S(1)}, bf16[168,384]{1,0:T(8,128)(2,1)S(1)}, u32[]{:S(2)}, u32[]{:S(2)}) collective-permute-start(bf16[168,384]{1,0:T(8,128)(2,1)S(1)} %get-tuple-element.55.p0.refs_0_), channel_id=1, source_target_pairs={{0,2},{1,3},{2,0},{3,1},{4,6},{5,7},{6,4},{7,5},{8,10},{9,11},{10,... | collective-permute-start | bytes 387080 | tf_op jit(solution)/shard_map/ppermute | solution.py:393
  64.4 9.0 %collective-permute-start.9 = (bf16[168,384]{1,0:T(8,128)(2,1)S(1)}, bf16[168,384]{1,0:T(8,128)(2,1)S(1)}, u32[]{:S(2)}, u32[]{:S(2)}) collective-permute-start(bf16[168,384]{1,0:T(8,128)(2,1)S(1)} %get-tuple-element.55.p0.refs_0_), channel_id=1, source_target_pairs={{0,1},{1,0},{2,3},{3,2},{4,5},{5,4},{6,7},{7,6},{8,9},{9,8},{10,11... | collective-permute-start | bytes 387080 | tf_op jit(solution)/shard_map/ppermute | solution.py:393
  68.5 10.4 %collective-permute-start.13 = (bf16[168,384]{1,0:T(8,128)(2,1)S(1)}, bf16[168,384]{1,0:T(8,128)(2,1)S(1)}, u32[]{:S(2)}, u32[]{:S(2)}) collective-permute-start(bf16[168,384]{1,0:T(8,128)(2,1)S(1)} %get-tuple-element.67.p0.refs_5_), channel_id=1, source_target_pairs={{0,2},{1,3},{2,0},{3,1},{4,6},{5,7},{6,4},{7,5},{8,10},{9,11},{10,... | collective-permute-start | bytes 387080 | tf_op jit(solution)/shard_map/ppermute | solution.py:393
  73.3 5.6 %collective-permute-start.11 = (bf16[168,384]{1,0:T(8,128)(2,1)S(1)}, bf16[168,384]{1,0:T(8,128)(2,1)S(1)}, u32[]{:S(2)}, u32[]{:S(2)}) collective-permute-start(bf16[168,384]{1,0:T(8,128)(2,1)S(1)} %collective-permute-done.10.p2.refs_2_), channel_id=1, source_target_pairs={{0,1},{1,0},{2,3},{3,2},{4,5},{5,4},{6,7},{7,6},{8,9},{9,8},{10,11... | collective-permute-start | bytes 387080 | tf_op jit(solution)/shard_map/ppermute | solution.py:393
  73.3 7.5 %collective-permute-start.12 = (bf16[168,384]{1,0:T(8,128)(2,1)S(1)}, bf16[168,384]{1,0:T(8,128)(2,1)S(1)}, u32[]{:S(2)}, u32[]{:S(2)}) collective-permute-start(bf16[168,384]{1,0:T(8,128)(2,1)S(1)} %get-tuple-element.67.p0.refs_5_), channel_id=1, source_target_pairs={{0,1},{1,0},{2,3},{3,2},{4,5},{5,4},{6,7},{7,6},{8,9},{9,8},{10,11... | collective-permute-start | bytes 387080 | tf_op jit(solution)/shard_map/ppermute | solution.py:393
  78.9 5.5 %collective-permute-start.14 = (bf16[168,384]{1,0:T(8,128)(2,1)S(1)}, bf16[168,384]{1,0:T(8,128)(2,1)S(1)}, u32[]{:S(2)}, u32[]{:S(2)}) collective-permute-start(bf16[168,384]{1,0:T(8,128)(2,1)S(1)} %collective-permute-done.13.p2.refs_7_), channel_id=1, source_target_pairs={{0,1},{1,0},{2,3},{3,2},{4,5},{5,4},{6,7},{7,6},{8,9},{9,8},{10,11... | collective-permute-start | bytes 387080 | tf_op jit(solution)/shard_map/ppermute | solution.py:393
  84.4 5.1 %copy-start.7 = (bf16[1664,176]{1,0:T(8,128)(2,1)S(1)}, bf16[1664,176]{1,0:T(8,128)(2,1)}, u32[]{:S(2)}) copy-start(bf16[1664,176]{1,0:T(8,128)(2,1)} %constant.8.clone.unpacker) | copy-start | bytes 1757188
  85.6 3.9 %collective-permute-start.15 = (bf16[176,1536]{1,0:T(8,128)(2,1)S(1)}, bf16[176,1536]{1,0:T(8,128)(2,1)S(1)}, u32[]{:S(2)}, u32[]{:S(2)}) collective-permute-start(bf16[176,1536]{1,0:T(8,128)(2,1)S(1)} %get-tuple-element.71), channel_id=1, source_target_pairs={{0,4},{4,0},{1,5},{5,1},{2,6},{6,2},{3,7},{7,3},{8,12},{12,8},{9,1... | collective-permute-start | bytes 1622024 | tf_op jit(solution)/shard_map/ppermute | solution.py:393
  105.7 7.3 %collective-permute-start.16 = (bf16[16,1536]{1,0:T(8,128)(2,1)S(1)}, bf16[16,1536]{1,0:T(8,128)(2,1)S(1)}, u32[]{:S(2)}, u32[]{:S(2)}) collective-permute-start(bf16[16,1536]{1,0:T(8,128)(2,1)S(1)} %get-tuple-element.75), channel_id=1, source_target_pairs={{0,128},{128,0},{1,129},{129,1},{2,130},{130,2},{3,131},{131,3},{4... | collective-permute-start | bytes 147464 | tf_op jit(solution)/shard_map/ppermute | solution.py:393
